TPU v7x, 256 devices: a whole 4x4x8 slice. The times are simulated.
256 devices in a mesh: expert: 32 (over x, z), row: 8 (over y, core).
Axes of the slice: x: 4, y: 4, z: 8, core: 2. Of those that a mesh axis runs over, the one named last changes fastest.
Arguments:
- tokens: bfloat16 [8192, 7168], P('expert', 'row'), may hold values from -6 to 6
- routing: int32 [8192, 8], P('expert'), may hold values from 0 to 255, all different within a row; in each aligned block of 256 rows (0 to 255, 256 to 511, ...) at most 12 rows name the same one
- weights: bfloat16 [256, 2048, 256], P('expert', 'row'), may hold values from -6 to 6
- indices: int32 [256, 2048, 128], P('expert', 'row'), may hold values from 0 to 63
- codebook: bfloat16 [256, 2, 64], P('expert'), may hold values from -5 to 5
- hinv_panel: float32 [256, 256, 256], P(('expert', 'row')), may hold values from -1.6 to 2, as said below
Outputs:
- hessian: float32 [256, 7168, 256], P('expert', 'row')
- errors: float32 [256, 2048, 256], P('expert', 'row')
Inputs may be any that keep to these rules, and one draw needn't show every extreme that they name: `routing`: each token names 8 different experts; within each aligned block of 256 tokens (the tokens of one index of the expert axis) no expert is named by more than 12 tokens, a bound that some block reaches; every expert is named by some token. `hinv_panel`: upper triangular with positive diagonal entries.
All inputs are finite; a program needn't handle non-finite values.
Results may differ from a plain program's by a relative error of at most 0.0003.
Values may be sent and summed in bfloat16 or wider, within the bound.
No kernel may reach another device: no remote copies, remote signals or barrier semaphores. Data moves between devices by JAX's collectives and lax.ppermute only.
A program may use at most 192 MiB of HBM per device.

v0:
```python
import jax
import jax.numpy as jnp
from jax import lax
from jax.sharding import PartitionSpec as P

EXP_DEV = 8


def broadcast(value, axis, source):
    kept = jnp.where(lax.axis_index(axis) == source, value, 0).astype(value.dtype)
    return lax.psum(kept, axis)


def invert_upper(factors):
    width = factors.shape[-1]
    diag_values = jnp.diagonal(factors, axis1=1, axis2=2)
    recip = 1.0 / diag_values
    position = jnp.arange(width, dtype=jnp.int32)
    strict = (position[:, None] < position[None, :]).astype(jnp.float32)
    scaled = factors * recip[:, :, None] * strict[None, :, :]
    identity = jnp.eye(width, dtype=jnp.float32)[None, :, :]
    power = -scaled
    result = identity + power
    steps_needed = (width - 1).bit_length()
    for level in range(1, steps_needed):
        power = jnp.einsum("eij,ejk->eik", power, power, precision=lax.Precision.HIGHEST)
        result = jnp.einsum(
            "eij,ejk->eik", result, identity + power, precision=lax.Precision.HIGHEST
        )
    return result * recip[:, None, :]


def local(tokens, routing, weights, indices, codebook, hinv_panel):
    experts_axis = lax.axis_size("expert")
    group_index = lax.axis_index("expert")
    token_rows, slice_width = tokens.shape
    top_count = routing.shape[1]
    experts_all = EXP_DEV * experts_axis
    capacity = max(2, 3 * token_rows * top_count // (2 * experts_all))
    window = weights.shape[2]
    first_expert = group_index * EXP_DEV
    labels = jnp.arange(experts_all, dtype=jnp.int32)
    member = jnp.any(routing[:, :, None] == labels[None, None, :], axis=1).astype(jnp.int32)
    local_counts = jnp.sum(member, axis=0).astype(jnp.float32)
    total_counts = lax.psum(local_counts, "expert")
    counts = lax.dynamic_slice_in_dim(total_counts, first_expert, EXP_DEV, 0)
    row_ids = jnp.arange(token_rows, dtype=jnp.int32)
    lower_ones = (row_ids[:, None] >= row_ids[None, :]).astype(jnp.float32)
    running = jnp.dot(lower_ones, member.astype(jnp.float32), preferred_element_type=jnp.float32)
    ranked = running.astype(jnp.int32) - 1
    slot_ids = jnp.arange(capacity, dtype=jnp.int32)
    placed = (member[:, :, None] * (ranked[:, :, None] == slot_ids[None, None, :])).astype(
        jnp.bfloat16
    )
    placed = placed.reshape(token_rows, experts_all * capacity)
    outgoing = jnp.einsum("tk,td->kd", placed, tokens, preferred_element_type=jnp.float32).astype(
        jnp.bfloat16
    )
    outgoing = outgoing.reshape(experts_axis, EXP_DEV, capacity, slice_width)
    arrived = lax.all_to_all(outgoing, "expert", split_axis=0, concat_axis=0, tiled=True)
    window_cols = broadcast(arrived[:, :, :, :window], "row", 0)
    partial_sum = jnp.einsum(
        "slcd,slcw->ldw", arrived, window_cols, preferred_element_type=jnp.float32
    )
    hessian = partial_sum * (2.0 / counts)[:, None, None]

    def decode_block(pair_item):
        book_rows, picked = pair_item
        onehot = (
            picked[:, :, None] == jnp.arange(book_rows.shape[1], dtype=jnp.int32)[None, None, :]
        ).astype(jnp.bfloat16)
        pair_values = jnp.einsum(
            "rpk,ck->rpc", onehot, book_rows, preferred_element_type=jnp.float32
        )
        return pair_values.reshape(picked.shape[0], 2 * picked.shape[1])

    decoded = lax.map(decode_block, (codebook, indices))
    residual = weights.astype(jnp.float32) - decoded
    inverse = invert_upper(lax.all_gather(hinv_panel, "row", axis=0, tiled=True))
    errors = jnp.einsum("eoj,ejk->eok", residual, inverse, precision=lax.Precision.HIGHEST)
    return (hessian, errors)


def solution(mesh):
    in_specs = (
        P("expert", "row"),
        P("expert", None),
        P("expert", "row", None),
        P("expert", "row", None),
        P("expert", None, None),
        P(("expert", "row"), None, None),
    )
    out_specs = (P("expert", "row", None), P("expert", "row", None))
    return jax.shard_map(local, mesh=mesh, in_specs=in_specs, out_specs=out_specs, check_vma=False)
```

profile of v0, /device:TPU:2, one launch (start us, length us, event | category | flops | bytes accessed | tf_op | source)
XLA Modules:
  0.0 416.4 jit_solution(5579716021736798169)
XLA Ops:
  7.2 0.9 copy.44
  8.1 0.7 fusion.23
  8.8 0.2 fusion.27
  9.2 2.4 eq.75
  11.5 4.6 %eq.76 = s32[256,3072]{0,1:T(8,128)} reshape(s32[256,256,12]{0,2,1:T(8,128)} %eq.75) | data formatting | bytes 6291456 | tf_op jit(solution)/shard_map/eq | solution.py:52
  16.2 2.4 mul.45
  18.6 4.6 %mul.46 = s32[256,3072]{0,1:T(8,128)} reshape(s32[256,256,12]{0,2,1:T(8,128)} %mul.45) | data formatting | bytes 6291456 | tf_op jit(solution)/shard_map/mul | solution.py:52
  23.4 7.1 %convolution_convert_fusion = bf16[3072,896]{1,0:T(8,128)(2,1)} fusion(bf16[256,896]{1,0:T(8,128)(2,1)S(1)} %copy-done, s32[256,3072]{0,1:T(8,128)} %mul.46, s32[256,3072]{0,1:T(8,128)} %eq.76, s32[3072]{0:T(1024)S(1)} %eq.78), kind=kOutput, calls=%fused_computation.9 | convolution fusion | flops 1414397952 | bytes 12267520 | tf_op jit(solution)/shard_map/tk,td->kd/dot_general | solution.py:56
  30.5 9.5 %reshape.48 = bf16[32,8,12,896]{3,2,1,0:T(8,128)(2,1)} reshape(bf16[3072,896]{1,0:T(8,128)(2,1)} %convolution_convert_fusion) | data formatting | bytes 11010048 | tf_op jit(solution)/shard_map/reshape | solution.py:59
  40.0 6.9 %copy.47 = bf16[32,8,12,896]{3,1,2,0:T(8,128)(2,1)} copy(bf16[32,8,12,896]{3,2,1,0:T(8,128)(2,1)} %reshape.48) | data formatting | bytes 11010048 | tf_op jit(solution)/shard_map/reshape | solution.py:59
  46.9 11.8 %all-to-all-start = ((bf16[32,8,12,896]{3,1,2,0:T(8,128)(2,1)}), bf16[32,8,12,896]{3,1,2,0:T(8,128)(2,1)}, u32[]{:S(2)}, u32[]{:S(2)}) async-start(bf16[32,8,12,896]{3,1,2,0:T(8,128)(2,1)} %copy.47), calls=%async_computation | async-start | bytes 11010048 | tf_op jit(solution)/shard_map/all_to_all | solution.py:60
  58.8 0.7 all-gather.2.cloned.1.call-update
  59.5 1.3 copy.50
  60.9 174.3 %psum.15 = f32[256]{0:T(256)S(1)} all-reduce(f32[256]{0:T(256)S(1)} %convert_element_type.64), channel_id=1, replica_groups=mesh['expert'=32,'row'=8] {'expert'}, use_global_device_ids=true, to_apply=%region_3.4 | all-reduce | flops 256 | bytes 2048 | tf_op jit(solution)/shard_map/psum | solution.py:45
  235.3 31.9 %while.10 = (s32[]{:T(128)}, f32[8,256,256]{1,2,0:T(8,128)}, s32[8,256,128]{2,1,0:T(8,128)}, bf16[8,2,64]{2,1,0:T(2,128)(2,1)}, s32[]{:T(128)}) while((s32[]{:T(128)}, f32[8,256,256]{1,2,0:T(8,128)}, s32[8,256,128]{2,1,0:T(8,128)}, bf16[8,2,64]{2,1,0:T(2,128)(2,1)}, s32[]{:T(128)}) %tuple.23), condition=%wide.region_5.6_spmd, body=%wide.region_4.5_spmd.sunk | while | flops 10485762 | bytes 2229825 | solution.py:77
  235.3 0.9 dynamic-slice_bitcast_fusion.2
  236.2 2.0 fusion.75
  238.4 0.2 broadcast_in_dim.18
  238.6 0.7 constant_dynamic-update-slice_fusion.2
  239.3 0.9 dynamic-slice_bitcast_fusion.2
  240.2 2.0 fusion.75
  242.6 0.7 constant_dynamic-update-slice_fusion.2
  243.3 0.9 dynamic-slice_bitcast_fusion.2
  244.2 2.0 fusion.75
  246.6 0.7 constant_dynamic-update-slice_fusion.2
  247.3 0.9 dynamic-slice_bitcast_fusion.2
  248.2 2.0 fusion.75
  250.4 0.2 broadcast_in_dim.18
  250.5 0.7 constant_dynamic-update-slice_fusion.2
  251.3 0.9 dynamic-slice_bitcast_fusion.2
  252.2 2.0 fusion.75
  254.5 0.7 constant_dynamic-update-slice_fusion.2
  255.3 0.9 dynamic-slice_bitcast_fusion.2
  256.2 2.0 fusion.75
  258.5 0.7 constant_dynamic-update-slice_fusion.2
  259.2 0.9 dynamic-slice_bitcast_fusion.2
  260.1 2.0 fusion.75
  262.3 0.2 broadcast_in_dim.18
  262.5 0.7 constant_dynamic-update-slice_fusion.2
  263.2 0.9 dynamic-slice_bitcast_fusion.2
  264.1 2.0 fusion.75
  266.5 0.7 constant_dynamic-update-slice_fusion.2
  267.2 17.8 %copy.51 = f32[8,256,256]{0,2,1:T(8,128)} copy(f32[8,256,256]{2,1,0:T(8,128)} %all-gather.2.cloned.1.call-done) | data formatting | bytes 4194304 | tf_op jit(solution)/shard_map/all_gather | solution.py:79
  285.1 2.3 gather_fusion
  287.5 2.7 fusion.24
  290.2 2.2 fusion.46
  292.3 2.2 fusion.47
  294.5 2.2 fusion.48
  296.7 2.3 fusion.49
  299.0 2.2 fusion.50
  301.2 3.4 fusion.51
  304.7 2.5 fusion.18
  307.2 2.3 fusion.16
  309.5 2.3 fusion.14
  311.7 2.5 fusion.12
  314.2 2.3 fusion.10
  316.5 3.5 fusion.8
  320.0 4.4 %copy.49 = bf16[32,8,12,896]{3,0,2,1:T(8,128)(2,1)S(1)} copy(bf16[32,8,12,896]{3,1,2,0:T(8,128)(2,1)} %all-to-all-done) | data formatting | bytes 11010048 | tf_op jit(solution)/shard_map/all_to_all | solution.py:60
  324.5 1.3 slice_select_fusion
  325.8 0.8 copy-done.3
  326.6 3.9 fusion.6
  330.6 5.2 %fusion.4 = f32[8,256,256]{2,1,0:T(8,128)} fusion(f32[8,256,256]{2,1,0:T(8,128)S(1)} %fusion.6, f32[8,256,256]{1,2,0:T(8,128)S(1)} %copy-done.5, bf16[8,256,256]{1,2,0:T(8,128)(2,1)S(1)} %copy-done.4, f32[8,256]{1,0:T(8,128)S(1)} %copy.52), kind=kOutput, calls=%fused_computation.11 | convolution fusion | flops 1612185600 | bytes 7348224 | tf_op jit(solution)/shard_map/eoj,ejk->eok/dot_general | solution.py:80
  335.8 62.9 %all-reduce.2.cloned.1.call-done = bf16[32,8,12,256]{3,0,2,1:T(8,128)(2,1)} async-done(((bf16[32,8,12,256]{3,0,2,1:T(8,128)(2,1)}), bf16[32,8,12,256]{3,0,2,1:T(8,128)(2,1)}) %all-reduce.2.cloned.1.call-update) | async-done | bytes 1572880 | tf_op jit(solution)/shard_map/psum | solution.py:11
  398.7 10.4 %bitcast_multiply_fusion = f32[8,896,256]{2,1,0:T(8,128)} fusion(f32[8]{0:T(128)S(1)} %dynamic-slice_divide_fusion, bf16[32,8,12,256]{3,0,2,1:T(8,128)(2,1)} %all-reduce.2.cloned.1.call-done, bf16[32,8,12,896]{3,1,2,0:T(8,128)(2,1)} %all-to-all-done), kind=kOutput, calls=%fused_computation.8 | convolution fusion | flops 1411121152 | bytes 14417952 | tf_op jit(solution)/shard_map/slcd,slcw->ldw/dot_general | solution.py:62
  (44 shorter events, 3.0 us)
Async XLA Ops:
  7.2 16.2 %copy-start = (bf16[256,896]{1,0:T(8,128)(2,1)S(1)}, bf16[256,896]{1,0:T(8,128)(2,1)}, u32[]{:S(2)}) copy-start(bf16[256,896]{1,0:T(8,128)(2,1)} %param.8) | copy-start | bytes 1376260
  46.9 12.6 %copy-start.6 = (bf16[8,256,256]{2,1,0:T(8,128)(2,1)S(1)}, bf16[8,256,256]{2,1,0:T(8,128)(2,1)}, u32[]{:S(2)}) copy-start(bf16[8,256,256]{2,1,0:T(8,128)(2,1)} %param.10) | copy-start | bytes 3145732
  46.9 273.1 %all-to-all-start = ((bf16[32,8,12,896]{3,1,2,0:T(8,128)(2,1)}), bf16[32,8,12,896]{3,1,2,0:T(8,128)(2,1)}, u32[]{:S(2)}, u32[]{:S(2)}) async-start(bf16[32,8,12,896]{3,1,2,0:T(8,128)(2,1)} %copy.47), calls=%async_computation | async-start | bytes 11010048 | tf_op jit(solution)/shard_map/all_to_all | solution.py:60
  58.7 208.5 %all-gather.2.cloned.1.call-start = ((), (), s32[]{:S(2)}) async-start(), calls=%async_computation.2 | async-start | bytes 2359296 | tf_op jit(solution)/shard_map/all_gather | solution.py:79
  59.4 339.3 %all-reduce.2.cloned.1.call-start = ((), (), s32[]{:S(2)}) async-start(), calls=%async_computation.1 | async-start | bytes 3145728 | tf_op jit(solution)/shard_map/psum | solution.py:11
  267.2 20.3 %copy-start.2 = (f32[8,256,256]{2,1,0:T(8,128)S(1)}, f32[8,256,256]{2,1,0:T(8,128)}, u32[]{:S(2)}) copy-start(f32[8,256,256]{2,1,0:T(8,128)} %all-gather.2.cloned.1.call-done) | copy-start | bytes 6291460
  324.5 2.2 copy-start.3
  326.6 4.0 copy-start.4
  326.6 4.0 copy-start.5
  398.7 10.4 %copy-start.1 = (bf16[256,896]{1,0:T(8,128)(2,1)S(1)}, bf16[256,896]{1,0:T(8,128)(2,1)}, u32[]{:S(2)}) copy-start(bf16[256,896]{1,0:T(8,128)(2,1)} %param.8) | copy-start | bytes 1376260
Sparse Core Ops, SparseCore 0:
  61.4 28.8 all-gather.1
  325.9 72.7 all-reduce.1
where the time goes:
time: 424 us; the launch traced here: 416 us
  blocking collectives  174 us (41%)
  matrix products  75.2 us (18%)
  local copies, waits for them, and re-layouts  74.3 us (18%)
  waiting for transfers between devices  63.6 us (15%)
  between operations  14.7 us (3%)
  starting transfers between devices  11.9 us (3%)
    psum x1, blocking collectives, local(): total_counts = lax.psum(local_counts, 'expert')  174 us
    psum x1, waiting for transfers between devices, broadcast(): return lax.psum(kept, axis)  62.9 us
    dot_general x7, matrix products, invert_upper(): jnp.einsum('eij,ejk->eik', result, identity + power, precision=lax.Precis...  19.3 us
    all_gather x1, local copies, waits for them, and re-layouts, local(): lax.all_gather(hinv_panel, 'row', axis=0, tiled=True)  17.8 us
    dot_general x7, matrix products, invert_upper(): jnp.einsum('eij,ejk->eik', power, power, precision=lax.Precision.HIGHEST)  17.1 us
    reshape x2, local copies, waits for them, and re-layouts, local(): outgoing = outgoing.reshape(experts_axis, EXP_DEV, capacity, slice_width)  16.4 us
    dot_general x8, matrix products, decode_block(): jnp.einsum('rpk,ck->rpc', onehot, book_rows, preferred_element_type=jnp.f...  16 us
    all_to_all x1, starting transfers between devices, local(): lax.all_to_all(outgoing, 'expert', split_axis=0, concat_axis=0, tiled=True)  11.8 us
  transfers between devices with their start and end apart: 3, of which 1 were waited for; matrix products, arithmetic and copies ran while one was open for 23% of the time, Pallas kernels for 0%

commit v1 on v0

v1 whole, which is shorter than its diff:
```python
import functools

import jax
import jax.numpy as jnp
from jax import lax
from jax.experimental import pallas as pl
from jax.experimental.pallas import tpu as pltpu
from jax.sharding import Mesh, PartitionSpec as P

NX, NZ, NY, NC = 4, 8, 4, 2
EXP_DEV = 8
CAP = 12
TOK = 256
LANES = 128
FEAT = 896
ROWS = TOK + 16
WROWS = TOK + 32
CHUNKS = ((0,), (-1, 1), (-2, 2), (-3, 3), (4,))
SLOTS = NZ * EXP_DEV * CAP
WMSG = SLOTS + 16
F32 = jnp.float32
BF16 = jnp.bfloat16
VMEM_LIMIT = 48 * 1024 * 1024


def params():
    return pltpu.CompilerParams(vmem_limit_bytes=VMEM_LIMIT)


def vmem():
    return pl.BlockSpec(memory_space=pltpu.VMEM)


def smem():
    return pl.BlockSpec(memory_space=pltpu.SMEM)


def cost(flops, moved):
    return pl.CostEstimate(flops=flops, bytes_accessed=moved, transcendentals=0)


def routing_rows(routing_t):
    listed = routing_t.astype(F32)
    return jnp.concatenate([listed, jnp.full(listed.shape, -1.0, F32)], axis=0).astype(BF16)


def payload_kernel(tokens_ref, routing_ref, out_ref):
    out_ref[0:TOK, :] = tokens_ref[...]
    out_ref[TOK:ROWS, :] = jnp.zeros((16, FEAT), BF16)
    out_ref[TOK:ROWS, 0:TOK] = routing_rows(routing_ref[...])


def window_payload_kernel(place_ref, tokens_ref, routing_ref, got_ref, out_ref):
    first = place_ref[2] == 0

    @pl.when(first)
    def _():
        out_ref[0:TOK, :] = tokens_ref[:, 0:LANES]

    @pl.when(jnp.logical_not(first))
    def _():
        out_ref[0:TOK, :] = got_ref[...]

    listed = routing_rows(routing_ref[...])
    out_ref[TOK:TOK + 16, :] = listed[:, 0:LANES]
    out_ref[TOK + 16:WROWS, :] = listed[:, LANES:TOK]


def ranks(listed, x_index, z_index):
    line = lax.broadcasted_iota(jnp.int32, (NX * EXP_DEV, TOK), 0)
    label = EXP_DEV * (((x_index + line // EXP_DEV) % NX) * NZ + z_index) + line % EXP_DEV
    label = label.astype(F32)
    member = jnp.zeros((NX * EXP_DEV, TOK), F32)
    for slot in range(8):
        member = member + jnp.where(listed[slot:slot + 1, :] == label, 1.0, 0.0)
    row = lax.broadcasted_iota(jnp.int32, (TOK, TOK), 0)
    column = lax.broadcasted_iota(jnp.int32, (TOK, TOK), 1)
    upto = jnp.where(row <= column, 1.0, 0.0).astype(BF16)
    running = jnp.dot(member.astype(BF16), upto, preferred_element_type=F32)
    return member, member * running


def selectors(rank, count, spot):
    size = count * EXP_DEV * CAP
    shape = (NX * size, NX * EXP_DEV)
    row = lax.broadcasted_iota(jnp.int32, shape, 0)
    column = lax.broadcasted_iota(jnp.int32, shape, 1)
    inside = row % size
    if count == 1:
        expert = inside // CAP
        mine = row >= 0
    else:
        expert = 2 * (inside // (2 * count * CAP)) + (inside % (2 * CAP)) // CAP
        mine = (inside // (2 * CAP)) % count == spot
    match = jnp.logical_and(column == (row // size) * EXP_DEV + expert, mine)
    spread = jnp.where(match, 1.0, 0.0).astype(BF16)
    wide = jnp.dot(spread, rank.astype(BF16), preferred_element_type=F32)
    want = (lax.broadcasted_iota(jnp.int32, (NX * size, TOK), 0) % CAP + 1).astype(F32)
    return jnp.where(wide == want, 1.0, 0.0).astype(BF16)


def pack_kernel(count, place_ref, *refs):
    blocks, outs = refs[:count], refs[count:]
    size = count * EXP_DEV * CAP
    total = None
    for spot, block in enumerate(blocks):
        listed = block[TOK:ROWS, 0:TOK].astype(F32)
        _, rank = ranks(listed, place_ref[0], place_ref[1])
        picked = jnp.dot(
            selectors(rank, count, spot), block[0:TOK, :], preferred_element_type=F32
        )
        total = picked if total is None else total + picked
    for k, out in enumerate(outs):
        out[...] = total[k * size:(k + 1) * size, :].astype(BF16)


def pack(place, blocks):
    count = len(blocks)
    size = count * EXP_DEV * CAP
    return pl.pallas_call(
        functools.partial(pack_kernel, count),
        out_shape=[jax.ShapeDtypeStruct((size, FEAT), BF16)] * NX,
        in_specs=[smem()] + [vmem()] * count,
        out_specs=[vmem()] * NX,
        compiler_params=params(),
        cost_estimate=cost(2 * NX * size * TOK * FEAT * count, 2 * FEAT * (ROWS * count + NX * size)),
        name="pack_%d" % count,
    )(place, *blocks)


def window_kernel(place_ref, gathered_ref, *outs):
    x_index, z_index = place_ref[0], place_ref[1]
    start = 0
    counts = jnp.zeros((NX * EXP_DEV, LANES), F32)
    for chunk in CHUNKS:
        count = len(chunk)
        size = count * EXP_DEV * CAP
        total = None
        for spot, offset in enumerate(chunk):
            block = gathered_ref[(z_index + offset + NZ) % NZ]
            listed = jnp.concatenate(
                [block[TOK:TOK + 16, :], block[TOK + 16:WROWS, :]], axis=1
            ).astype(F32)
            member, rank = ranks(listed, x_index, z_index)
            counts = counts + jnp.sum(member, axis=1, keepdims=True)
            picked = jnp.dot(
                selectors(rank, count, spot), block[0:TOK, :], preferred_element_type=F32
            )
            total = picked if total is None else total + picked
        for k, out in enumerate(outs):
            out[start:start + size, :] = total[k * size:(k + 1) * size, :].astype(BF16)
        start += size
    for k, out in enumerate(outs):
        mine = counts[k * EXP_DEV:(k + 1) * EXP_DEV, :]
        out[SLOTS:WMSG, :] = jnp.concatenate([mine, mine], axis=0).astype(BF16)


def inverse_kernel(factor_ref, out_ref):
    width = factor_ref.shape[-1]
    factor = factor_ref[0]
    row = lax.broadcasted_iota(jnp.int32, (width, width), 0)
    column = lax.broadcasted_iota(jnp.int32, (width, width), 1)
    diagonal = jnp.where(row == column, factor, 0.0)
    across = 1.0 / jnp.sum(diagonal, axis=0, keepdims=True)
    down = 1.0 / jnp.sum(diagonal, axis=1, keepdims=True)

    def level(span):
        return jnp.where(
            jnp.logical_and(
                row // (2 * span) == column // (2 * span),
                jnp.logical_and(row // span % 2 == 0, column // span % 2 == 1),
            ),
            factor,
            0.0,
        )

    result = jnp.where(row == column, across, 0.0) - down * level(1) * across
    span = 2
    while span < width:
        first = jnp.dot(result, level(span), precision=lax.Precision.HIGHEST, preferred_element_type=F32)
        result = result - jnp.dot(first, result, precision=lax.Precision.HIGHEST, preferred_element_type=F32)
        span *= 2
    out_ref[0] = result


def split(value):
    high = value.astype(BF16)
    return high, (value - high.astype(F32)).astype(BF16)


def errors_kernel(weights_ref, indices_ref, codebook_ref, inverse_ref, out_ref):
    picked = indices_ref[0]
    rows, pairs = picked.shape
    book = codebook_ref[0].astype(F32)
    book = jnp.concatenate([book, jnp.zeros(book.shape, F32)], axis=1)
    coords = [
        jnp.take_along_axis(jnp.broadcast_to(book[c:c + 1, :], (rows, pairs)), picked, axis=1)
        for c in range(2)
    ]
    both = jnp.concatenate(coords, axis=1).astype(BF16)
    row = lax.broadcasted_iota(jnp.int32, (2 * pairs, 2 * pairs), 0)
    column = lax.broadcasted_iota(jnp.int32, (2 * pairs, 2 * pairs), 1)
    weave = jnp.where(column == 2 * (row % pairs) + row // pairs, 1.0, 0.0).astype(BF16)
    decoded = jnp.dot(both, weave, preferred_element_type=F32)
    residual_high, residual_low = split(weights_ref[0].astype(F32) - decoded)
    inverse_high, inverse_low = split(inverse_ref[0])
    total = jnp.dot(residual_low, inverse_high, preferred_element_type=F32)
    total = total + jnp.dot(residual_high, inverse_low, preferred_element_type=F32)
    out_ref[0] = total + jnp.dot(residual_high, inverse_high, preferred_element_type=F32)


def hessian_kernel(place_ref, *refs):
    messages, (mine_ref, other_ref, out_ref) = refs[:-3], refs[-3:]
    pair = pl.program_id(0)
    first = place_ref[2] == 0
    features, windows = [], []
    row = lax.broadcasted_iota(jnp.int32, (4 * CAP, TOK), 0)
    single = (row // CAP - 2 * (pair % 2), row // CAP - 2 * (pair % 2))
    double = (row % (2 * CAP)) // CAP
    for k in range(NX):
        start = k * WMSG
        for c, chunk in enumerate(CHUNKS):
            features.append(messages[k * len(CHUNKS) + c][...])
            if len(chunk) == 1:
                begin, owner = start + 4 * CAP * (pair // 2), single[0]
            else:
                begin, owner = start + 4 * CAP * pair, double
            where = pl.ds(pl.multiple_of(begin, 16), 4 * CAP)
            near, far = mine_ref[where, :].astype(F32), other_ref[where, :].astype(F32)
            both = jnp.concatenate(
                [jnp.where(first, near, far), jnp.where(first, far, near)], axis=1
            )
            windows.append(
                jnp.concatenate(
                    [jnp.where(owner == e, both, 0.0) for e in range(2)], axis=1
                ).astype(BF16)
            )
            start += len(chunk) * EXP_DEV * CAP
    product = lax.dot_general(
        jnp.concatenate(features, axis=0),
        jnp.concatenate(windows, axis=0),
        (((0,), (0,)), ((), ())),
        preferred_element_type=F32,
    )
    counts = jnp.zeros((16, LANES), F32)
    for k in range(NX):
        counts = counts + mine_ref[k * WMSG + SLOTS:(k + 1) * WMSG, :].astype(F32)
    line = lax.broadcasted_iota(jnp.int32, (16, LANES), 0)
    for e in range(2):
        count = jnp.sum(jnp.where(line == 2 * pair + e, counts, 0.0), axis=0, keepdims=True)
        scale = 2.0 / count
        scale = jnp.concatenate([scale, scale], axis=1)
        out_ref[e] = product[:, e * TOK:(e + 1) * TOK] * scale


def shifted(size, step):
    return [(i, (i + step) % size) for i in range(size)]


def x_pairs(step):
    return [
        ((a * NY) * NC + c, (((a + step) % NX) * NY) * NC + c) for a in range(NX) for c in range(NC)
    ]


def local(tokens, routing, weights, indices, codebook, hinv_panel):
    x_index, z_index = lax.axis_index("x"), lax.axis_index("z")
    y_index, core = lax.axis_index("y"), lax.axis_index("core")
    place = jnp.stack([x_index, z_index, core]).astype(jnp.int32)
    routing_t = routing.T
    half = lax.ppermute(tokens[:, LANES:2 * LANES], "core", [(0, 1)])
    payload = pl.pallas_call(
        payload_kernel,
        out_shape=jax.ShapeDtypeStruct((ROWS, FEAT), BF16),
        in_specs=[vmem()] * 2,
        out_specs=vmem(),
        compiler_params=params(),
        cost_estimate=cost(0, 4 * ROWS * FEAT),
        name="payload",
    )(tokens, routing_t)
    window_payload = pl.pallas_call(
        window_payload_kernel,
        out_shape=jax.ShapeDtypeStruct((WROWS, LANES), BF16),
        in_specs=[smem()] + [vmem()] * 3,
        out_specs=vmem(),
        compiler_params=params(),
        name="window_payload",
    )(place, tokens, routing_t, half)
    gathered = lax.all_gather(window_payload, "z", axis=0, tiled=False)
    forward, backward = [payload], [payload]
    for step in range(1, 5):
        forward.append(lax.ppermute(forward[-1], "z", shifted(NZ, 1)))
        if step < 4:
            backward.append(lax.ppermute(backward[-1], "z", shifted(NZ, -1)))
    chunks = [[payload]] + [[forward[s], backward[s]] for s in (1, 2, 3)] + [[forward[4]]]
    messages = [[None] * len(CHUNKS) for _ in range(NX)]
    for c, blocks in enumerate(chunks):
        packed = pack(place, blocks)
        messages[0][c] = packed[0]
        for k in (2, 1, 3):
            messages[k][c] = lax.ppermute(packed[k], "x", shifted(NX, k))

    inverse = pl.pallas_call(
        inverse_kernel,
        out_shape=jax.ShapeDtypeStruct(hinv_panel.shape, F32),
        in_specs=[vmem()],
        out_specs=vmem(),
        compiler_params=params(),
        cost_estimate=cost(14 * 6 * 2 * TOK ** 3, 8 * TOK * TOK),
        name="inverse",
    )(hinv_panel)
    inverses = lax.all_gather(inverse, ("y", "core"), axis=0, tiled=True)
    experts, rows, width = weights.shape
    pairs = indices.shape[2]
    errors = pl.pallas_call(
        errors_kernel,
        grid=(experts,),
        out_shape=jax.ShapeDtypeStruct(weights.shape, F32),
        in_specs=[
            pl.BlockSpec((1, rows, width), lambda e: (e, 0, 0)),
            pl.BlockSpec((1, rows, pairs), lambda e: (e, 0, 0)),
            pl.BlockSpec((1,) + codebook.shape[1:], lambda e: (e, 0, 0)),
            pl.BlockSpec((1, width, width), lambda e: (e, 0, 0)),
        ],
        out_specs=pl.BlockSpec((1, rows, width), lambda e: (e, 0, 0)),
        compiler_params=params(),
        cost_estimate=cost(8 * experts * rows * width * width, experts * rows * width * 12),
        name="errors",
    )(weights, indices, codebook, inverses)

    window_parts = pl.pallas_call(
        window_kernel,
        out_shape=[jax.ShapeDtypeStruct((WMSG, LANES), BF16)] * NX,
        in_specs=[smem(), vmem()],
        out_specs=[vmem()] * NX,
        compiler_params=params(),
        cost_estimate=cost(2 * NX * 2 * SLOTS * TOK * LANES, 4 * NX * WMSG * LANES),
        name="window_pack",
    )(place, gathered)
    arrived = [window_parts[0]] + [
        lax.ppermute(window_parts[k], ("x", "y", "core"), x_pairs(k)) for k in (1, 2, 3)
    ]
    low = jnp.concatenate(arrived[:2], axis=0)
    high = jnp.concatenate(arrived[2:], axis=0)
    up_low = lax.ppermute(low, "y", [(0, 1)])
    down_high = lax.ppermute(high, "y", [(0, 3)])
    up = lax.ppermute(jnp.where(y_index == 0, high, up_low), "y", [(0, 1), (1, 2)])
    down = lax.ppermute(jnp.where(y_index == 0, low, down_high), "y", [(0, 3), (3, 2)])
    low = jnp.where(y_index == 0, low, jnp.where(y_index == 1, up_low, jnp.where(y_index == 2, up, down)))
    high = jnp.where(y_index == 0, high, jnp.where(y_index == 1, up, jnp.where(y_index == 2, down, down_high)))
    mine = jnp.concatenate([low, high], axis=0)
    other = lax.ppermute(mine, "core", shifted(NC, 1))

    operands, specs = [], []
    for k in range(NX):
        for c, chunk in enumerate(CHUNKS):
            operands.append(messages[k][c])
            if len(chunk) == 1:
                specs.append(pl.BlockSpec((4 * CAP, FEAT), lambda p: (p // 2, 0)))
            else:
                specs.append(pl.BlockSpec((4 * CAP, FEAT), lambda p: (p, 0)))
    full = pl.BlockSpec((NX * WMSG, LANES), lambda p: (0, 0))
    hessian = pl.pallas_call(
        hessian_kernel,
        grid=(EXP_DEV // 2,),
        out_shape=jax.ShapeDtypeStruct((EXP_DEV, FEAT, TOK), F32),
        in_specs=[smem()] + specs + [full, full],
        out_specs=pl.BlockSpec((2, FEAT, TOK), lambda p: (p, 0, 0)),
        compiler_params=params(),
        cost_estimate=cost(8 * 960 * FEAT * 2 * TOK, 4 * EXP_DEV * FEAT * TOK + 2 * NX * SLOTS * FEAT),
        name="hessian",
    )(place, *operands, mine, other)
    return hessian, errors


def solution(mesh):
    grid = Mesh(mesh.devices.reshape(NX, NZ, NY, NC), ("x", "z", "y", "core"))
    expert, row = ("x", "z"), ("y", "core")
    in_specs = (
        P(expert, row),
        P(expert, None),
        P(expert, row, None),
        P(expert, row, None),
        P(expert, None, None),
        P(expert + row, None, None),
    )
    out_specs = (P(expert, row, None), P(expert, row, None))
    return jax.shard_map(local, mesh=grid, in_specs=in_specs, out_specs=out_specs, check_vma=False)
```

time: 424 us -> 178 us (0.42); the launches traced: 416 us -> 177 us
  blocking collectives: 174 us -> 29.3 us
  matrix products: 75.2 us -> 0 us
  local copies, waits for them, and re-layouts: 74.3 us -> 4.32 us
  starting transfers between devices: 11.9 us -> 55.1 us
  Pallas kernels: 0 us -> 36.9 us
  waiting for transfers between devices: 63.6 us -> 34.1 us
    psum x1 -> x0, blocking collectives: 174 us -> none  [local(): total_counts = lax.psum(local_counts, 'expert')]
    dot_general x26 -> x0, matrix products: 75.2 us -> none  [the longest x7 19.3 us: invert_upper(): jnp.einsum('eij,ejk->eik', result, identity + power, precision=lax.Precis...]
    psum x1 -> x0, waiting for transfers between devices: 62.9 us -> none  [broadcast(): return lax.psum(kept, axis)]
    ppermute x0 -> x31, starting transfers between devices: none -> 55.1 us  [the longest x15 21.6 us: local(): messages[k][c] = lax.ppermute(packed[k], 'x', shifted(NX, k))]
    pallas_call x0 -> x11, Pallas kernels: none -> 36.9 us  [the longest x5 11.9 us: pack(): pl.pallas_call(functools.partial(pack_kernel, count), out_shape=[jax.Shap...]
    ppermute x0 -> x31, waiting for transfers between devices: none -> 34.1 us  [the longest x15 32.1 us: local(): messages[k][c] = lax.ppermute(packed[k], 'x', shifted(NX, k))]
    all_gather x0 -> x1, blocking collectives: none -> 29.3 us  [local(): gathered = lax.all_gather(window_payload, 'z', axis=0, tiled=False)]
    all_gather x1 -> x0, local copies, waits for them, and re-layouts: 17.8 us -> none  [local(): lax.all_gather(hinv_panel, 'row', axis=0, tiled=True)]
  transfers between devices with their start and end apart: 3 -> 32, of which waited for: 1 -> 11; matrix products, arithmetic and copies ran while one was open for 23% -> 2% of each run, Pallas kernels for 0% -> 15%
where the time goes in v1:
time: 178 us; the launch traced here: 177 us
  starting transfers between devices  55.1 us (31%)
  Pallas kernels  36.9 us (21%)
  waiting for transfers between devices  34.1 us (19%)
  blocking collectives  29.3 us (16%)
  between operations  14.4 us (8%)
  local copies, waits for them, and re-layouts  4.32 us (2%)
  other arithmetic  3.1 us (2%)
    ppermute x15, waiting for transfers between devices, local(): messages[k][c] = lax.ppermute(packed[k], 'x', shifted(NX, k))  32.1 us
    all_gather x1, blocking collectives, local(): gathered = lax.all_gather(window_payload, 'z', axis=0, tiled=False)  29.3 us
    ppermute x15, starting transfers between devices, local(): messages[k][c] = lax.ppermute(packed[k], 'x', shifted(NX, k))  21.6 us
    pallas_call x5, Pallas kernels, pack(): pl.pallas_call(functools.partial(pack_kernel, count), out_shape=[jax.Shap...  11.9 us
    ppermute x3, starting transfers between devices, local(): lax.ppermute(window_parts[k], ('x', 'y', 'core'), x_pairs(k))  10.5 us
    ppermute x3, starting transfers between devices, local(): backward.append(lax.ppermute(backward[-1], 'z', shifted(NZ, -1)))  8.08 us
    pallas_call x1, Pallas kernels, local(): pl.pallas_call(hessian_kernel, grid=(EXP_DEV // 2,), out_shape=jax.ShapeD...  7.57 us
    pallas_call x1, Pallas kernels, local(): pl.pallas_call(inverse_kernel, out_shape=jax.ShapeDtypeStruct(hinv_panel....  7.51 us
  transfers between devices with their start and end apart: 32, of which 11 were waited for; matrix products, arithmetic and copies ran while one was open for 2% of the time, Pallas kernels for 15%

profile of v1, /device:TPU:2, one launch (start us, length us, event | category | flops | bytes accessed | tf_op | source)
XLA Modules:
  0.0 177.3 jit_solution(1991633086027345235)
XLA Ops:
  7.2 0.0 copy-start.6
  7.2 0.0 all-gather.3.cloned.1.call-start
  7.2 0.8 slice.3
  8.1 1.7 collective-permute-start.22
  9.8 0.1 pad_add_fusion.place_ref
  9.9 0.8 collective-permute-done.22.got_ref
  10.7 1.0 copy-done
  11.7 0.7 copy-done.5
  12.4 0.6 window_payload.1
  13.0 29.3 %all-gather = bf16[2304,128]{1,0:T(8,128)(2,1)S(1)} all-gather(bf16[288,128]{1,0:T(8,128)(2,1)S(1)} %window_payload.1), channel_id=2, replica_groups=mesh['x'=4,'z'=8,'y'=4,'core'=2] {'z'}, dimensions={0}, use_global_device_ids=true | all-gather | bytes 663552 | tf_op jit(solution)/shard_map/all_gather | solution.py:289
  42.2 4.1 %window_pack.1 = (bf16[784,128]{1,0:T(8,128)(2,1)S(1)}, bf16[784,128]{1,0:T(8,128)(2,1)S(1)}, bf16[784,128]{1,0:T(8,128)(2,1)S(1)}, bf16[784,128]{1,0:T(8,128)(2,1)S(1)}) custom-call(s32[3]{0:T(128)S(1)} %pad_add_fusion.place_ref, bf16[8,288,128]{2,1,0:T(8,128)(2,1)S(1)} %bitcast.5), custom_call_target="tpu_custom_call" | custom-call | flops 402653184 | bytes 1605632 | tf_op jit(solution)/shard_map/window_pack/pallas_call | solution.py:331
  46.4 3.4 %collective-permute-start.23 = (bf16[784,128]{1,0:T(8,128)(2,1)S(1)}, bf16[784,128]{1,0:T(8,128)(2,1)S(1)}, u32[]{:S(2)}, u32[]{:S(2)}) collective-permute-start(bf16[784,128]{1,0:T(8,128)(2,1)S(1)} %get-tuple-element.47), channel_id=1, source_target_pairs={{0,64},{1,65},{64,128},{65,129},{128,192},{129,193},{192,0},{193,1... | collective-permute-start | bytes 602120 | tf_op jit(solution)/shard_map/ppermute | solution.py:341
  49.8 1.1 collective-permute-start
  51.0 2.2 %collective-permute-start.1 = (bf16[272,896]{1,0:T(8,128)(2,1)S(1)}, bf16[272,896]{1,0:T(8,128)(2,1)S(1)}, u32[]{:S(2)}, u32[]{:S(2)}) collective-permute-start(bf16[272,896]{1,0:T(8,128)(2,1)S(1)} %payload.1.refs_0_), channel_id=1, source_target_pairs={{0,56},{8,0},{16,8},{24,16},{32,24},{40,32},{48,40},{56,48},{1,57}... | collective-permute-start | bytes 1462280 | tf_op jit(solution)/shard_map/ppermute | solution.py:294
  53.2 3.0 %collective-permute-start.25 = (bf16[784,128]{1,0:T(8,128)(2,1)S(1)}, bf16[784,128]{1,0:T(8,128)(2,1)S(1)}, u32[]{:S(2)}, u32[]{:S(2)}) collective-permute-start(bf16[784,128]{1,0:T(8,128)(2,1)S(1)} %get-tuple-element.48), channel_id=1, source_target_pairs={{0,128},{1,129},{64,192},{65,193},{128,0},{129,1},{192,64},{193,65... | collective-permute-start | bytes 602120 | tf_op jit(solution)/shard_map/ppermute | solution.py:341
  56.2 4.1 %collective-permute-start.26 = (bf16[784,128]{1,0:T(8,128)(2,1)S(1)}, bf16[784,128]{1,0:T(8,128)(2,1)S(1)}, u32[]{:S(2)}, u32[]{:S(2)}) collective-permute-start(bf16[784,128]{1,0:T(8,128)(2,1)S(1)} %get-tuple-element.49), channel_id=1, source_target_pairs={{0,192},{1,193},{64,0},{65,1},{128,64},{129,65},{192,128},{193,129... | collective-permute-start | bytes 602120 | tf_op jit(solution)/shard_map/ppermute | solution.py:341
  60.3 2.1 %collective-permute-start.24 = (bf16[1568,128]{1,0:T(8,128)(2,1)S(1)}, bf16[1568,128]{1,0:T(8,128)(2,1)}, u32[]{:S(2)}, u32[]{:S(2)}) collective-permute-start(bf16[1568,128]{1,0:T(8,128)(2,1)S(1)} %constant_dynamic-update-slice_fusion), channel_id=1, source_target_pairs={{0,2},{1,3},{8,10},{9,11},{16,18},{17,19},{24,26},{25,27},{32,34},... | collective-permute-start | bytes 1204232 | tf_op jit(solution)/shard_map/ppermute | solution.py:345
  62.4 7.5 %inverse.1 = f32[1,256,256]{2,1,0:T(8,128)} custom-call(f32[1,256,256]{2,1,0:T(8,128)S(1)} %copy-done.8), custom_call_target="tpu_custom_call" | custom-call | flops 2818572288 | bytes 524288 | tf_op jit(solution)/shard_map/inverse/pallas_call | solution.py:303
  69.9 0.0 all-gather.3.cloned.1.call-update
  70.0 1.3 collective-permute-start.28
  71.4 0.1 collective-permute-start.2
  71.5 3.2 %collective-permute-start.3 = (bf16[272,896]{1,0:T(8,128)(2,1)S(1)}, bf16[272,896]{1,0:T(8,128)(2,1)S(1)}, u32[]{:S(2)}, u32[]{:S(2)}) collective-permute-start(bf16[272,896]{1,0:T(8,128)(2,1)S(1)} %collective-permute-done.1.refs_1_), channel_id=1, source_target_pairs={{0,56},{8,0},{16,8},{24,16},{32,24},{40,32},{48,40},{56,48},{1,57}... | collective-permute-start | bytes 1462280 | tf_op jit(solution)/shard_map/ppermute | solution.py:294
  74.7 0.8 broadcast_select_fusion.1
  75.5 2.1 %collective-permute-start.27 = (bf16[1568,128]{1,0:T(8,128)(2,1)}, bf16[1568,128]{1,0:T(8,128)(2,1)}, u32[]{:S(2)}, u32[]{:S(2)}) collective-permute-start(bf16[1568,128]{1,0:T(8,128)(2,1)} %broadcast_select_fusion.1), channel_id=1, source_target_pairs={{0,2},{2,4},{1,3},{3,5},{8,10},{10,12},{9,11},{11,13},{16,18},{18,... | collective-permute-start | bytes 1204232 | tf_op jit(solution)/shard_map/ppermute | solution.py:347
  77.5 0.9 broadcast_select_fusion
  78.4 0.0 copy-done.14
  78.4 5.9 %collective-permute-start.29 = (bf16[1568,128]{1,0:T(8,128)(2,1)}, bf16[1568,128]{1,0:T(8,128)(2,1)}, u32[]{:S(2)}, u32[]{:S(2)}) collective-permute-start(bf16[1568,128]{1,0:T(8,128)(2,1)} %broadcast_select_fusion), channel_id=1, source_target_pairs={{0,6},{6,4},{1,7},{7,5},{8,14},{14,12},{9,15},{15,13},{16,22},{22,... | collective-permute-start | bytes 1204232 | tf_op jit(solution)/shard_map/ppermute | solution.py:348
  84.3 1.9 %pack_1.2 = (bf16[96,896]{1,0:T(8,128)(2,1)S(1)}, bf16[96,896]{1,0:T(8,128)(2,1)S(1)}, bf16[96,896]{1,0:T(8,128)(2,1)}, bf16[96,896]{1,0:T(8,128)(2,1)S(1)}) custom-call(s32[3]{0:T(128)S(1)} %pad_add_fusion.place_ref, bf16[272,896]{1,0:T(8,128)(2,1)S(1)} %payload.1.refs_0_), custom_call_target="tpu_custom_call" | custom-call | flops 176160768 | bytes 1175552 | tf_op jit(solution)/shard_map/pack_1/pallas_call | solution.py:120
  86.2 0.0 collective-permute-start.12
  86.2 1.9 %collective-permute-start.17 = (bf16[96,896]{1,0:T(8,128)(2,1)S(1)}, bf16[96,896]{1,0:T(8,128)(2,1)S(1)}, u32[]{:S(2)}, u32[]{:S(2)}) collective-permute-start(bf16[96,896]{1,0:T(8,128)(2,1)S(1)} %get-tuple-element.41), channel_id=1, source_target_pairs={{0,192},{64,0},{128,64},{192,128},{1,193},{65,1},{129,65},{193,129... | collective-permute-start | bytes 516104 | tf_op jit(solution)/shard_map/ppermute | solution.py:301
  88.2 2.9 %pack_2.3 = (bf16[192,896]{1,0:T(8,128)(2,1)S(1)}, bf16[192,896]{1,0:T(8,128)(2,1)S(1)}, bf16[192,896]{1,0:T(8,128)(2,1)S(1)}, bf16[192,896]{1,0:T(8,128)(2,1)S(1)}) custom-call(s32[3]{0:T(128)S(1)} %pad_add_fusion.place_ref, bf16[272,896]{1,0:T(8,128)(2,1)S(1)} %collective-permute-done.refs_0_, bf16[272,896]{1,0:T(8,128)(2,1)S(1)} %collective-permute-done.1.refs_1_), custom_call_target="tpu_custom_call" | custom-call | flops 704643072 | bytes 2351104 | tf_op jit(solution)/shard_map/pack_2/pallas_call | solution.py:120
  91.1 1.1 collective-permute-start.7
  92.2 2.9 %pack_2.4 = (bf16[192,896]{1,0:T(8,128)(2,1)S(1)}, bf16[192,896]{1,0:T(8,128)(2,1)S(1)}, bf16[192,896]{1,0:T(8,128)(2,1)S(1)}, bf16[192,896]{1,0:T(8,128)(2,1)S(1)}) custom-call(s32[3]{0:T(128)S(1)} %pad_add_fusion.place_ref, bf16[272,896]{1,0:T(8,128)(2,1)S(1)} %collective-permute-done.2.refs_0_, bf16[272,896]{1,0:T(8,128)(2,1)S(1)} %collective-permute-done.3.refs_1_), custom_call_target="tpu_custom_call" | custom-call | flops 704643072 | bytes 2351104 | tf_op jit(solution)/shard_map/pack_2/pallas_call | solution.py:120
  95.1 0.1 collective-permute-done.12.refs_10_
  95.2 3.8 %collective-permute-start.13 = (bf16[192,896]{1,0:T(8,128)(2,1)S(1)}, bf16[192,896]{1,0:T(8,128)(2,1)S(1)}, u32[]{:S(2)}, u32[]{:S(2)}) collective-permute-start(bf16[192,896]{1,0:T(8,128)(2,1)S(1)} %get-tuple-element.37), channel_id=1, source_target_pairs={{0,128},{64,192},{128,0},{192,64},{1,129},{65,193},{129,1},{193,65... | collective-permute-start | bytes 1032200 | tf_op jit(solution)/shard_map/ppermute | solution.py:301
  99.0 0.3 collective-permute-done.17.refs_15_
  99.3 0.0 collective-permute-start.18
  99.3 0.6 collective-permute-start.4
  99.9 2.7 %collective-permute-start.5 = (bf16[272,896]{1,0:T(8,128)(2,1)S(1)}, bf16[272,896]{1,0:T(8,128)(2,1)S(1)}, u32[]{:S(2)}, u32[]{:S(2)}) collective-permute-start(bf16[272,896]{1,0:T(8,128)(2,1)S(1)} %collective-permute-done.3.refs_1_), channel_id=1, source_target_pairs={{0,56},{8,0},{16,8},{24,16},{32,24},{40,32},{48,40},{56,48},{1,57}... | collective-permute-start | bytes 1462280 | tf_op jit(solution)/shard_map/ppermute | solution.py:294
  102.6 1.3 select_select_fusion.1
  103.9 2.1 %collective-permute-start.8 = (bf16[192,896]{1,0:T(8,128)(2,1)S(1)}, bf16[192,896]{1,0:T(8,128)(2,1)S(1)}, u32[]{:S(2)}, u32[]{:S(2)}) collective-permute-start(bf16[192,896]{1,0:T(8,128)(2,1)S(1)} %get-tuple-element.32), channel_id=1, source_target_pairs={{0,64},{64,128},{128,192},{192,0},{1,65},{65,129},{129,193},{193,1... | collective-permute-start | bytes 1032200 | tf_op jit(solution)/shard_map/ppermute | solution.py:301
  106.0 2.2 %collective-permute-done.13.refs_11_ = bf16[192,896]{1,0:T(8,128)(2,1)S(1)} collective-permute-done((bf16[192,896]{1,0:T(8,128)(2,1)S(1)}, bf16[192,896]{1,0:T(8,128)(2,1)S(1)}, u32[]{:S(2)}, u32[]{:S(2)}) %collective-permute-start.13) | collective-permute-done | bytes 344096 | tf_op jit(solution)/shard_map/ppermute | solution.py:301
  108.1 2.3 %collective-permute-start.14 = (bf16[192,896]{1,0:T(8,128)(2,1)S(1)}, bf16[192,896]{1,0:T(8,128)(2,1)S(1)}, u32[]{:S(2)}, u32[]{:S(2)}) collective-permute-start(bf16[192,896]{1,0:T(8,128)(2,1)S(1)} %get-tuple-element.38), channel_id=1, source_target_pairs={{0,128},{64,192},{128,0},{192,64},{1,129},{65,193},{129,1},{193,65... | collective-permute-start | bytes 1032200 | tf_op jit(solution)/shard_map/ppermute | solution.py:301
  110.4 6.8 %collective-permute-done.18.refs_16_ = bf16[192,896]{1,0:T(8,128)(2,1)S(1)} collective-permute-done((bf16[192,896]{1,0:T(8,128)(2,1)S(1)}, bf16[192,896]{1,0:T(8,128)(2,1)S(1)}, u32[]{:S(2)}, u32[]{:S(2)}) %collective-permute-start.18) | collective-permute-done | bytes 344096 | tf_op jit(solution)/shard_map/ppermute | solution.py:301
  117.2 0.1 pad_maximum_fusion.refs_20_
  117.3 0.1 collective-permute-start.30
  117.4 2.9 %pack_2.5 = (bf16[192,896]{1,0:T(8,128)(2,1)S(1)}, bf16[192,896]{1,0:T(8,128)(2,1)S(1)}, bf16[192,896]{1,0:T(8,128)(2,1)S(1)}, bf16[192,896]{1,0:T(8,128)(2,1)S(1)}) custom-call(s32[3]{0:T(128)S(1)} %pad_add_fusion.place_ref, bf16[272,896]{1,0:T(8,128)(2,1)S(1)} %collective-permute-done.4.refs_0_, bf16[272,896]{1,0:T(8,128)(2,1)S(1)} %collective-permute-done.5.refs_1_), custom_call_target="tpu_custom_call" | custom-call | flops 704643072 | bytes 2351104 | tf_op jit(solution)/shard_map/pack_2/pallas_call | solution.py:120
  120.4 2.1 %collective-permute-start.9 = (bf16[192,896]{1,0:T(8,128)(2,1)S(1)}, bf16[192,896]{1,0:T(8,128)(2,1)S(1)}, u32[]{:S(2)}, u32[]{:S(2)}) collective-permute-start(bf16[192,896]{1,0:T(8,128)(2,1)S(1)} %get-tuple-element.33), channel_id=1, source_target_pairs={{0,64},{64,128},{128,192},{192,0},{1,65},{65,129},{129,193},{193,1... | collective-permute-start | bytes 1032200 | tf_op jit(solution)/shard_map/ppermute | solution.py:301
  122.5 0.1 collective-permute-start.10
  122.6 1.9 %collective-permute-done.19.refs_17_ = bf16[192,896]{1,0:T(8,128)(2,1)S(1)} collective-permute-done((bf16[192,896]{1,0:T(8,128)(2,1)S(1)}, bf16[192,896]{1,0:T(8,128)(2,1)S(1)}, u32[]{:S(2)}, u32[]{:S(2)}) %collective-permute-start.19) | collective-permute-done | bytes 344096 | tf_op jit(solution)/shard_map/ppermute | solution.py:301
  124.5 1.5 collective-permute-start.15
  126.0 1.2 collective-permute-done.6.refs_0_
  127.2 0.1 collective-permute-start.20
  127.4 1.3 pack_1.3
  128.6 2.9 %collective-permute-done.9.refs_7_ = bf16[192,896]{1,0:T(8,128)(2,1)S(1)} collective-permute-done((bf16[192,896]{1,0:T(8,128)(2,1)S(1)}, bf16[192,896]{1,0:T(8,128)(2,1)S(1)}, u32[]{:S(2)}, u32[]{:S(2)}) %collective-permute-start.9) | collective-permute-done | bytes 344096 | tf_op jit(solution)/shard_map/ppermute | solution.py:301
  131.5 1.8 %collective-permute-start.11 = (bf16[96,896]{1,0:T(8,128)(2,1)S(1)}, bf16[96,896]{1,0:T(8,128)(2,1)S(1)}, u32[]{:S(2)}, u32[]{:S(2)}) collective-permute-start(bf16[96,896]{1,0:T(8,128)(2,1)S(1)} %get-tuple-element.35), channel_id=1, source_target_pairs={{0,64},{64,128},{128,192},{192,0},{1,65},{65,129},{129,193},{193,1... | collective-permute-start | bytes 516104 | tf_op jit(solution)/shard_map/ppermute | solution.py:301
  133.3 12.1 %collective-permute-done.10.refs_8_ = bf16[192,896]{1,0:T(8,128)(2,1)S(1)} collective-permute-done((bf16[192,896]{1,0:T(8,128)(2,1)S(1)}, bf16[192,896]{1,0:T(8,128)(2,1)S(1)}, u32[]{:S(2)}, u32[]{:S(2)}) %collective-permute-start.10) | collective-permute-done | bytes 344096 | tf_op jit(solution)/shard_map/ppermute | solution.py:301
  145.4 2.2 %collective-permute-start.16 = (bf16[96,896]{1,0:T(8,128)(2,1)S(1)}, bf16[96,896]{1,0:T(8,128)(2,1)S(1)}, u32[]{:S(2)}, u32[]{:S(2)}) collective-permute-start(bf16[96,896]{1,0:T(8,128)(2,1)S(1)} %get-tuple-element.40), channel_id=1, source_target_pairs={{0,128},{64,192},{128,0},{192,64},{1,129},{65,193},{129,1},{193,65... | collective-permute-start | bytes 516104 | tf_op jit(solution)/shard_map/ppermute | solution.py:301
  147.6 2.5 %collective-permute-start.21 = (bf16[96,896]{1,0:T(8,128)(2,1)S(1)}, bf16[96,896]{1,0:T(8,128)(2,1)S(1)}, u32[]{:S(2)}, u32[]{:S(2)}) collective-permute-start(bf16[96,896]{1,0:T(8,128)(2,1)S(1)} %get-tuple-element.45), channel_id=1, source_target_pairs={{0,192},{64,0},{128,64},{192,128},{1,193},{65,1},{129,65},{193,129... | collective-permute-start | bytes 516104 | tf_op jit(solution)/shard_map/ppermute | solution.py:301
  150.1 2.4 %collective-permute-done.16.refs_14_ = bf16[96,896]{1,0:T(8,128)(2,1)S(1)} collective-permute-done((bf16[96,896]{1,0:T(8,128)(2,1)S(1)}, bf16[96,896]{1,0:T(8,128)(2,1)S(1)}, u32[]{:S(2)}, u32[]{:S(2)}) %collective-permute-start.16) | collective-permute-done | bytes 172064 | tf_op jit(solution)/shard_map/ppermute | solution.py:301
  152.6 3.4 %collective-permute-done.21.refs_19_ = bf16[96,896]{1,0:T(8,128)(2,1)S(1)} collective-permute-done((bf16[96,896]{1,0:T(8,128)(2,1)S(1)}, bf16[96,896]{1,0:T(8,128)(2,1)S(1)}, u32[]{:S(2)}, u32[]{:S(2)}) %collective-permute-start.21) | collective-permute-done | bytes 172064 | tf_op jit(solution)/shard_map/ppermute | solution.py:301
  156.0 7.6 %hessian.1 = f32[8,896,256]{2,1,0:T(8,128)} custom-call(s32[3]{0:T(128)S(1)} %pad_add_fusion.place_ref, bf16[96,896]{1,0:T(8,128)(2,1)S(1)} %get-tuple-element.26.refs_0_, bf16[192,896]{1,0:T(8,128)(2,1)S(1)} %get-tuple-element.27.refs_1_, bf16[192,896]{1,0:T(8,128)(2,1)S(1)} %get-tuple-element.28.refs_2_, bf16[192,896]{1,0:T(8,128)(2,1)S(1)} %get-tuple-element.29.refs_3_, ...), custom_call_target="tpu_custom_call" | custom-call | flops 3523215360 | bytes 12845056 | tf_op jit(solution)/shard_map/hessian/pallas_call | solution.py:363
  163.6 1.6 copy-done.2
  165.2 5.2 %errors.1 = f32[8,256,256]{2,1,0:T(8,128)} custom-call(bf16[8,256,256]{2,1,0:T(8,128)(2,1)S(1)} %copy-done.3, s32[8,256,128]{2,1,0:T(8,128)S(1)} %copy-done.4, bf16[8,2,64]{2,1,0:T(2,128)(2,1)S(1)} %copy-done.7, f32[8,256,256]{2,1,0:T(8,128)S(1)} %copy-done.2), custom_call_target="tpu_custom_call" | custom-call | flops 1073741824 | bytes 6291456 | tf_op jit(solution)/shard_map/errors/pallas_call | solution.py:315
  (57 shorter events, 0.3 us)
Async XLA Ops:
  7.2 42.6 %copy-start.6 = (s32[256,8]{0,1:T(8,128)S(1)}, s32[256,8]{0,1:T(8,128)}, u32[]{:S(2)}) copy-start(s32[256,8]{0,1:T(8,128)} %param.7) | copy-start | bytes 24580
  7.2 156.4 %all-gather.3.cloned.1.call-start = ((), (), s32[]{:S(2)}) async-start(), calls=%async_computation | async-start | bytes 2359296 | tf_op jit(solution)/shard_map/all_gather | solution.py:312
  8.1 2.6 %collective-permute-start.22 = (bf16[256,128]{1,0:T(8,128)(2,1)S(1)}, bf16[256,128]{1,0:T(8,128)(2,1)S(1)}, u32[]{:S(2)}, u32[]{:S(2)}) collective-permute-start(bf16[256,128]{1,0:T(8,128)(2,1)S(1)} %slice.3), channel_id=1, source_target_pairs={{0,1},{2,3},{4,5},{6,7},{8,9},{10,11},{12,13},{14,15},{16,17},{18,... | collective-permute-start | bytes 196616 | tf_op jit(solution)/shard_map/ppermute | solution.py:271
  10.7 1.0 copy-start
  11.7 0.7 copy-start.5
  12.4 37.4 %copy-start.1 = (bf16[256,896]{1,0:T(8,128)(2,1)S(1)}, bf16[256,896]{1,0:T(8,128)(2,1)}, u32[]{:S(2)}) copy-start(bf16[256,896]{1,0:T(8,128)(2,1)} %tokens_ref.3) | copy-start | bytes 1376260
  13.0 49.4 %copy-start.8 = (f32[1,256,256]{2,1,0:T(8,128)S(1)}, f32[1,256,256]{2,1,0:T(8,128)}, u32[]{:S(2)}) copy-start(f32[1,256,256]{2,1,0:T(8,128)} %factor_ref.1) | copy-start | bytes 786436
  46.4 13.9 %collective-permute-start.23 = (bf16[784,128]{1,0:T(8,128)(2,1)S(1)}, bf16[784,128]{1,0:T(8,128)(2,1)S(1)}, u32[]{:S(2)}, u32[]{:S(2)}) collective-permute-start(bf16[784,128]{1,0:T(8,128)(2,1)S(1)} %get-tuple-element.47), channel_id=1, source_target_pairs={{0,64},{1,65},{64,128},{65,129},{128,192},{129,193},{192,0},{193,1... | collective-permute-start | bytes 602120 | tf_op jit(solution)/shard_map/ppermute | solution.py:341
  49.8 21.5 %collective-permute-start = (bf16[272,896]{1,0:T(8,128)(2,1)S(1)}, bf16[272,896]{1,0:T(8,128)(2,1)S(1)}, u32[]{:S(2)}, u32[]{:S(2)}) collective-permute-start(bf16[272,896]{1,0:T(8,128)(2,1)S(1)} %payload.1.refs_0_), channel_id=1, source_target_pairs={{0,8},{8,16},{16,24},{24,32},{32,40},{40,48},{48,56},{56,0},{1,9},... | collective-permute-start | bytes 1462280 | tf_op jit(solution)/shard_map/ppermute | solution.py:292
  51.0 20.5 %collective-permute-start.1 = (bf16[272,896]{1,0:T(8,128)(2,1)S(1)}, bf16[272,896]{1,0:T(8,128)(2,1)S(1)}, u32[]{:S(2)}, u32[]{:S(2)}) collective-permute-start(bf16[272,896]{1,0:T(8,128)(2,1)S(1)} %payload.1.refs_0_), channel_id=1, source_target_pairs={{0,56},{8,0},{16,8},{24,16},{32,24},{40,32},{48,40},{56,48},{1,57}... | collective-permute-start | bytes 1462280 | tf_op jit(solution)/shard_map/ppermute | solution.py:294
  53.2 16.8 %collective-permute-start.25 = (bf16[784,128]{1,0:T(8,128)(2,1)S(1)}, bf16[784,128]{1,0:T(8,128)(2,1)S(1)}, u32[]{:S(2)}, u32[]{:S(2)}) collective-permute-start(bf16[784,128]{1,0:T(8,128)(2,1)S(1)} %get-tuple-element.48), channel_id=1, source_target_pairs={{0,128},{1,129},{64,192},{65,193},{128,0},{129,1},{192,64},{193,65... | collective-permute-start | bytes 602120 | tf_op jit(solution)/shard_map/ppermute | solution.py:341
  56.2 13.8 %collective-permute-start.26 = (bf16[784,128]{1,0:T(8,128)(2,1)S(1)}, bf16[784,128]{1,0:T(8,128)(2,1)S(1)}, u32[]{:S(2)}, u32[]{:S(2)}) collective-permute-start(bf16[784,128]{1,0:T(8,128)(2,1)S(1)} %get-tuple-element.49), channel_id=1, source_target_pairs={{0,192},{1,193},{64,0},{65,1},{128,64},{129,65},{192,128},{193,129... | collective-permute-start | bytes 602120 | tf_op jit(solution)/shard_map/ppermute | solution.py:341
  60.3 17.2 %copy-start.10 = (bf16[1568,128]{1,0:T(8,128)(2,1)}, bf16[1568,128]{1,0:T(8,128)(2,1)S(1)}, u32[]{:S(2)}) copy-start(bf16[1568,128]{1,0:T(8,128)(2,1)S(1)} %constant_dynamic-update-slice_fusion) | copy-start | bytes 1204228
  60.3 14.4 %collective-permute-start.24 = (bf16[1568,128]{1,0:T(8,128)(2,1)S(1)}, bf16[1568,128]{1,0:T(8,128)(2,1)}, u32[]{:S(2)}, u32[]{:S(2)}) collective-permute-start(bf16[1568,128]{1,0:T(8,128)(2,1)S(1)} %constant_dynamic-update-slice_fusion), channel_id=1, source_target_pairs={{0,2},{1,3},{8,10},{9,11},{16,18},{17,19},{24,26},{25,27},{32,34},... | collective-permute-start | bytes 1204232 | tf_op jit(solution)/shard_map/ppermute | solution.py:345
  70.0 8.4 %copy-start.12 = (bf16[1568,128]{1,0:T(8,128)(2,1)}, bf16[1568,128]{1,0:T(8,128)(2,1)S(1)}, u32[]{:S(2)}) copy-start(bf16[1568,128]{1,0:T(8,128)(2,1)S(1)} %constant_dynamic-update-slice_fusion.2) | copy-start | bytes 1204228
  70.0 7.5 %collective-permute-start.28 = (bf16[1568,128]{1,0:T(8,128)(2,1)S(1)}, bf16[1568,128]{1,0:T(8,128)(2,1)S(1)}, u32[]{:S(2)}, u32[]{:S(2)}) collective-permute-start(bf16[1568,128]{1,0:T(8,128)(2,1)S(1)} %constant_dynamic-update-slice_fusion.2), channel_id=1, source_target_pairs={{0,6},{1,7},{8,14},{9,15},{16,22},{17,23},{24,30},{25,31},{32,38},... | collective-permute-start | bytes 1204232 | tf_op jit(solution)/shard_map/ppermute | solution.py:346
  71.4 14.9 %collective-permute-start.2 = (bf16[272,896]{1,0:T(8,128)(2,1)S(1)}, bf16[272,896]{1,0:T(8,128)(2,1)S(1)}, u32[]{:S(2)}, u32[]{:S(2)}) collective-permute-start(bf16[272,896]{1,0:T(8,128)(2,1)S(1)} %collective-permute-done.refs_0_), channel_id=1, source_target_pairs={{0,8},{8,16},{16,24},{24,32},{32,40},{40,48},{48,56},{56,0},{1,9},... | collective-permute-start | bytes 1462280 | tf_op jit(solution)/shard_map/ppermute | solution.py:292
  71.5 19.7 %collective-permute-start.3 = (bf16[272,896]{1,0:T(8,128)(2,1)S(1)}, bf16[272,896]{1,0:T(8,128)(2,1)S(1)}, u32[]{:S(2)}, u32[]{:S(2)}) collective-permute-start(bf16[272,896]{1,0:T(8,128)(2,1)S(1)} %collective-permute-done.1.refs_1_), channel_id=1, source_target_pairs={{0,56},{8,0},{16,8},{24,16},{32,24},{40,32},{48,40},{56,48},{1,57}... | collective-permute-start | bytes 1462280 | tf_op jit(solution)/shard_map/ppermute | solution.py:294
  75.5 23.9 %collective-permute-start.27 = (bf16[1568,128]{1,0:T(8,128)(2,1)}, bf16[1568,128]{1,0:T(8,128)(2,1)}, u32[]{:S(2)}, u32[]{:S(2)}) collective-permute-start(bf16[1568,128]{1,0:T(8,128)(2,1)} %broadcast_select_fusion.1), channel_id=1, source_target_pairs={{0,2},{2,4},{1,3},{3,5},{8,10},{10,12},{9,11},{11,13},{16,18},{18,... | collective-permute-start | bytes 1204232 | tf_op jit(solution)/shard_map/ppermute | solution.py:347
  77.5 0.9 copy-start.14
  78.4 21.4 %collective-permute-start.29 = (bf16[1568,128]{1,0:T(8,128)(2,1)}, bf16[1568,128]{1,0:T(8,128)(2,1)}, u32[]{:S(2)}, u32[]{:S(2)}) collective-permute-start(bf16[1568,128]{1,0:T(8,128)(2,1)} %broadcast_select_fusion), channel_id=1, source_target_pairs={{0,6},{6,4},{1,7},{7,5},{8,14},{14,12},{9,15},{15,13},{16,22},{22,... | collective-permute-start | bytes 1204232 | tf_op jit(solution)/shard_map/ppermute | solution.py:348
  86.2 9.0 %collective-permute-start.12 = (bf16[96,896]{1,0:T(8,128)(2,1)}, bf16[96,896]{1,0:T(8,128)(2,1)S(1)}, u32[]{:S(2)}, u32[]{:S(2)}) collective-permute-start(bf16[96,896]{1,0:T(8,128)(2,1)} %get-tuple-element.36), channel_id=1, source_target_pairs={{0,128},{64,192},{128,0},{192,64},{1,129},{65,193},{129,1},{193,65... | collective-permute-start | bytes 516104 | tf_op jit(solution)/shard_map/ppermute | solution.py:301
  86.2 13.1 %collective-permute-start.17 = (bf16[96,896]{1,0:T(8,128)(2,1)S(1)}, bf16[96,896]{1,0:T(8,128)(2,1)S(1)}, u32[]{:S(2)}, u32[]{:S(2)}) collective-permute-start(bf16[96,896]{1,0:T(8,128)(2,1)S(1)} %get-tuple-element.41), channel_id=1, source_target_pairs={{0,192},{64,0},{128,64},{192,128},{1,193},{65,1},{129,65},{193,129... | collective-permute-start | bytes 516104 | tf_op jit(solution)/shard_map/ppermute | solution.py:301
  88.2 14.4 %copy-start.11 = (bf16[1568,128]{1,0:T(8,128)(2,1)S(1)}, bf16[1568,128]{1,0:T(8,128)(2,1)}, u32[]{:S(2)}) copy-start(bf16[1568,128]{1,0:T(8,128)(2,1)} %copy-done.10) | copy-start | bytes 1204228
  88.2 14.4 %copy-start.13 = (bf16[1568,128]{1,0:T(8,128)(2,1)S(1)}, bf16[1568,128]{1,0:T(8,128)(2,1)}, u32[]{:S(2)}) copy-start(bf16[1568,128]{1,0:T(8,128)(2,1)} %copy-done.12) | copy-start | bytes 1204228
  88.2 14.4 %copy-start.15 = (bf16[1568,128]{1,0:T(8,128)(2,1)S(1)}, bf16[1568,128]{1,0:T(8,128)(2,1)}, u32[]{:S(2)}) copy-start(bf16[1568,128]{1,0:T(8,128)(2,1)} %copy-done.14) | copy-start | bytes 1204228
  91.1 12.8 %collective-permute-start.7 = (bf16[96,896]{1,0:T(8,128)(2,1)S(1)}, bf16[96,896]{1,0:T(8,128)(2,1)S(1)}, u32[]{:S(2)}, u32[]{:S(2)}) collective-permute-start(bf16[96,896]{1,0:T(8,128)(2,1)S(1)} %get-tuple-element.31), channel_id=1, source_target_pairs={{0,64},{64,128},{128,192},{192,0},{1,65},{65,129},{129,193},{193,1... | collective-permute-start | bytes 516104 | tf_op jit(solution)/shard_map/ppermute | solution.py:301
  95.2 12.9 %collective-permute-start.13 = (bf16[192,896]{1,0:T(8,128)(2,1)S(1)}, bf16[192,896]{1,0:T(8,128)(2,1)S(1)}, u32[]{:S(2)}, u32[]{:S(2)}) collective-permute-start(bf16[192,896]{1,0:T(8,128)(2,1)S(1)} %get-tuple-element.37), channel_id=1, source_target_pairs={{0,128},{64,192},{128,0},{192,64},{1,129},{65,193},{129,1},{193,65... | collective-permute-start | bytes 1032200 | tf_op jit(solution)/shard_map/ppermute | solution.py:301
  99.3 17.9 %collective-permute-start.18 = (bf16[192,896]{1,0:T(8,128)(2,1)S(1)}, bf16[192,896]{1,0:T(8,128)(2,1)S(1)}, u32[]{:S(2)}, u32[]{:S(2)}) collective-permute-start(bf16[192,896]{1,0:T(8,128)(2,1)S(1)} %get-tuple-element.42), channel_id=1, source_target_pairs={{0,192},{64,0},{128,64},{192,128},{1,193},{65,1},{129,65},{193,129... | collective-permute-start | bytes 1032200 | tf_op jit(solution)/shard_map/ppermute | solution.py:301
  99.3 17.9 %collective-permute-start.4 = (bf16[272,896]{1,0:T(8,128)(2,1)S(1)}, bf16[272,896]{1,0:T(8,128)(2,1)S(1)}, u32[]{:S(2)}, u32[]{:S(2)}) collective-permute-start(bf16[272,896]{1,0:T(8,128)(2,1)S(1)} %collective-permute-done.2.refs_0_), channel_id=1, source_target_pairs={{0,8},{8,16},{16,24},{24,32},{32,40},{40,48},{48,56},{56,0},{1,9},... | collective-permute-start | bytes 1462280 | tf_op jit(solution)/shard_map/ppermute | solution.py:292
  99.9 17.4 %collective-permute-start.5 = (bf16[272,896]{1,0:T(8,128)(2,1)S(1)}, bf16[272,896]{1,0:T(8,128)(2,1)S(1)}, u32[]{:S(2)}, u32[]{:S(2)}) collective-permute-start(bf16[272,896]{1,0:T(8,128)(2,1)S(1)} %collective-permute-done.3.refs_1_), channel_id=1, source_target_pairs={{0,56},{8,0},{16,8},{24,16},{32,24},{40,32},{48,40},{56,48},{1,57}... | collective-permute-start | bytes 1462280 | tf_op jit(solution)/shard_map/ppermute | solution.py:294
  103.9 16.5 %collective-permute-start.8 = (bf16[192,896]{1,0:T(8,128)(2,1)S(1)}, bf16[192,896]{1,0:T(8,128)(2,1)S(1)}, u32[]{:S(2)}, u32[]{:S(2)}) collective-permute-start(bf16[192,896]{1,0:T(8,128)(2,1)S(1)} %get-tuple-element.32), channel_id=1, source_target_pairs={{0,64},{64,128},{128,192},{192,0},{1,65},{65,129},{129,193},{193,1... | collective-permute-start | bytes 1032200 | tf_op jit(solution)/shard_map/ppermute | solution.py:301
  108.1 14.3 %collective-permute-start.14 = (bf16[192,896]{1,0:T(8,128)(2,1)S(1)}, bf16[192,896]{1,0:T(8,128)(2,1)S(1)}, u32[]{:S(2)}, u32[]{:S(2)}) collective-permute-start(bf16[192,896]{1,0:T(8,128)(2,1)S(1)} %get-tuple-element.38), channel_id=1, source_target_pairs={{0,128},{64,192},{128,0},{192,64},{1,129},{65,193},{129,1},{193,65... | collective-permute-start | bytes 1032200 | tf_op jit(solution)/shard_map/ppermute | solution.py:301
  117.2 7.2 %collective-permute-start.19 = (bf16[192,896]{1,0:T(8,128)(2,1)S(1)}, bf16[192,896]{1,0:T(8,128)(2,1)S(1)}, u32[]{:S(2)}, u32[]{:S(2)}) collective-permute-start(bf16[192,896]{1,0:T(8,128)(2,1)S(1)} %get-tuple-element.43), channel_id=1, source_target_pairs={{0,192},{64,0},{128,64},{192,128},{1,193},{65,1},{129,65},{193,129... | collective-permute-start | bytes 1032200 | tf_op jit(solution)/shard_map/ppermute | solution.py:301
  117.2 10.0 %collective-permute-start.6 = (bf16[272,896]{1,0:T(8,128)(2,1)S(1)}, bf16[272,896]{1,0:T(8,128)(2,1)S(1)}, u32[]{:S(2)}, u32[]{:S(2)}) collective-permute-start(bf16[272,896]{1,0:T(8,128)(2,1)S(1)} %collective-permute-done.4.refs_0_), channel_id=1, source_target_pairs={{0,8},{8,16},{16,24},{24,32},{32,40},{40,48},{48,56},{56,0},{1,9},... | collective-permute-start | bytes 1462280 | tf_op jit(solution)/shard_map/ppermute | solution.py:292
  117.3 38.7 %copy-start.9 = (bf16[3136,128]{1,0:T(8,128)(2,1)}, bf16[3136,128]{1,0:T(8,128)(2,1)S(1)}, u32[]{:S(2)}) copy-start(bf16[3136,128]{1,0:T(8,128)(2,1)S(1)} %pad_maximum_fusion.refs_20_) | copy-start | bytes 2408452
  117.3 32.8 %collective-permute-start.30 = (bf16[3136,128]{1,0:T(8,128)(2,1)S(1)}, bf16[3136,128]{1,0:T(8,128)(2,1)S(1)}, u32[]{:S(2)}, u32[]{:S(2)}) collective-permute-start(bf16[3136,128]{1,0:T(8,128)(2,1)S(1)} %pad_maximum_fusion.refs_20_), channel_id=1, source_target_pairs={{0,1},{1,0},{2,3},{3,2},{4,5},{5,4},{6,7},{7,6},{8,9},{9,8},{10,11... | collective-permute-start | bytes 2408456 | tf_op jit(solution)/shard_map/ppermute | solution.py:352
  120.4 11.1 %collective-permute-start.9 = (bf16[192,896]{1,0:T(8,128)(2,1)S(1)}, bf16[192,896]{1,0:T(8,128)(2,1)S(1)}, u32[]{:S(2)}, u32[]{:S(2)}) collective-permute-start(bf16[192,896]{1,0:T(8,128)(2,1)S(1)} %get-tuple-element.33), channel_id=1, source_target_pairs={{0,64},{64,128},{128,192},{192,0},{1,65},{65,129},{129,193},{193,1... | collective-permute-start | bytes 1032200 | tf_op jit(solution)/shard_map/ppermute | solution.py:301
  122.5 22.9 %collective-permute-start.10 = (bf16[192,896]{1,0:T(8,128)(2,1)S(1)}, bf16[192,896]{1,0:T(8,128)(2,1)S(1)}, u32[]{:S(2)}, u32[]{:S(2)}) collective-permute-start(bf16[192,896]{1,0:T(8,128)(2,1)S(1)} %get-tuple-element.34), channel_id=1, source_target_pairs={{0,64},{64,128},{128,192},{192,0},{1,65},{65,129},{129,193},{193,1... | collective-permute-start | bytes 1032200 | tf_op jit(solution)/shard_map/ppermute | solution.py:301
  124.5 23.1 %collective-permute-start.15 = (bf16[192,896]{1,0:T(8,128)(2,1)S(1)}, bf16[192,896]{1,0:T(8,128)(2,1)S(1)}, u32[]{:S(2)}, u32[]{:S(2)}) collective-permute-start(bf16[192,896]{1,0:T(8,128)(2,1)S(1)} %get-tuple-element.39), channel_id=1, source_target_pairs={{0,128},{64,192},{128,0},{192,64},{1,129},{65,193},{129,1},{193,65... | collective-permute-start | bytes 1032200 | tf_op jit(solution)/shard_map/ppermute | solution.py:301
  127.2 22.9 %collective-permute-start.20 = (bf16[192,896]{1,0:T(8,128)(2,1)S(1)}, bf16[192,896]{1,0:T(8,128)(2,1)S(1)}, u32[]{:S(2)}, u32[]{:S(2)}) collective-permute-start(bf16[192,896]{1,0:T(8,128)(2,1)S(1)} %get-tuple-element.44), channel_id=1, source_target_pairs={{0,192},{64,0},{128,64},{192,128},{1,193},{65,1},{129,65},{193,129... | collective-permute-start | bytes 1032200 | tf_op jit(solution)/shard_map/ppermute | solution.py:301
  131.5 18.6 %collective-permute-start.11 = (bf16[96,896]{1,0:T(8,128)(2,1)S(1)}, bf16[96,896]{1,0:T(8,128)(2,1)S(1)}, u32[]{:S(2)}, u32[]{:S(2)}) collective-permute-start(bf16[96,896]{1,0:T(8,128)(2,1)S(1)} %get-tuple-element.35), channel_id=1, source_target_pairs={{0,64},{64,128},{128,192},{192,0},{1,65},{65,129},{129,193},{193,1... | collective-permute-start | bytes 516104 | tf_op jit(solution)/shard_map/ppermute | solution.py:301
  145.4 7.2 %collective-permute-start.16 = (bf16[96,896]{1,0:T(8,128)(2,1)S(1)}, bf16[96,896]{1,0:T(8,128)(2,1)S(1)}, u32[]{:S(2)}, u32[]{:S(2)}) collective-permute-start(bf16[96,896]{1,0:T(8,128)(2,1)S(1)} %get-tuple-element.40), channel_id=1, source_target_pairs={{0,128},{64,192},{128,0},{192,64},{1,129},{65,193},{129,1},{193,65... | collective-permute-start | bytes 516104 | tf_op jit(solution)/shard_map/ppermute | solution.py:301
  147.6 8.3 %collective-permute-start.21 = (bf16[96,896]{1,0:T(8,128)(2,1)S(1)}, bf16[96,896]{1,0:T(8,128)(2,1)S(1)}, u32[]{:S(2)}, u32[]{:S(2)}) collective-permute-start(bf16[96,896]{1,0:T(8,128)(2,1)S(1)} %get-tuple-element.45), channel_id=1, source_target_pairs={{0,192},{64,0},{128,64},{192,128},{1,193},{65,1},{129,65},{193,129... | collective-permute-start | bytes 516104 | tf_op jit(solution)/shard_map/ppermute | solution.py:301
  150.1 5.9 %copy-start.16 = (bf16[3136,128]{1,0:T(8,128)(2,1)}, bf16[3136,128]{1,0:T(8,128)(2,1)S(1)}, u32[]{:S(2)}) copy-start(bf16[3136,128]{1,0:T(8,128)(2,1)S(1)} %collective-permute-done.30.refs_21_) | copy-start | bytes 2408452
  156.0 7.6 %copy-start.3 = (bf16[8,256,256]{2,1,0:T(8,128)(2,1)S(1)}, bf16[8,256,256]{2,1,0:T(8,128)(2,1)}, u32[]{:S(2)}) copy-start(bf16[8,256,256]{2,1,0:T(8,128)(2,1)} %weights_ref.1) | copy-start | bytes 3145732
  156.0 7.6 %copy-start.4 = (s32[8,256,128]{2,1,0:T(8,128)S(1)}, s32[8,256,128]{2,1,0:T(8,128)}, u32[]{:S(2)}) copy-start(s32[8,256,128]{2,1,0:T(8,128)} %indices_ref.1) | copy-start | bytes 3145732
  156.0 7.6 %copy-start.7 = (bf16[8,2,64]{2,1,0:T(2,128)(2,1)S(1)}, bf16[8,2,64]{2,1,0:T(2,128)(2,1)}, u32[]{:S(2)}) copy-start(bf16[8,2,64]{2,1,0:T(2,128)(2,1)} %codebook_ref.1) | copy-start | bytes 6148
  163.6 1.6 copy-start.2
Sparse Core Ops, SparseCore 0:
  70.0 24.2 all-gather.2

commit v2 on v1

v2 whole, which is shorter than its diff:
```python
import functools

import jax
import jax.numpy as jnp
from jax import lax
from jax.experimental import pallas as pl
from jax.experimental.pallas import tpu as pltpu
from jax.sharding import Mesh, PartitionSpec as P

NX, NZ, NY, NC = 4, 8, 4, 2
EXP_DEV = 8
CAP = 12
TOK = 256
LANES = 128
FEAT = 896
WIDE = FEAT + LANES
ROWS = TOK + 16
CHUNKS = (1, 2, 2, 2, 1)
PAIR = 4 * CAP
LAST = EXP_DEV * CAP
FOLD = 6
F32 = jnp.float32
BF16 = jnp.bfloat16


def params(mebibytes):
    return pltpu.CompilerParams(vmem_limit_bytes=mebibytes * 1024 * 1024)


def vmem():
    return pl.BlockSpec(memory_space=pltpu.VMEM)


def smem():
    return pl.BlockSpec(memory_space=pltpu.SMEM)


def cost(micros):
    return pl.CostEstimate(flops=0, bytes_accessed=int(3.69e6 * micros), transcendentals=0)


def routing_rows(routing_t):
    listed = routing_t.astype(F32)
    return jnp.concatenate([listed, jnp.full(listed.shape, -1.0, F32)], axis=0).astype(BF16)


def halves_kernel(tokens_ref, out_ref):
    for copy in range(NY * NC):
        out_ref[copy] = tokens_ref[:, copy % NC * LANES:(copy % NC + 1) * LANES]


def payload_kernel(tokens_ref, routing_ref, out_ref):
    out_ref[0:TOK, :] = tokens_ref[...]
    out_ref[TOK:ROWS, :] = jnp.zeros((16, FEAT), BF16)
    out_ref[TOK:ROWS, 0:TOK] = routing_rows(routing_ref[...])


def join_kernel(forward_ref, backward_ref, edge_ref, *outs):
    for block, out in zip((forward_ref, backward_ref), outs):
        out[:, 0:FEAT] = block[...]
        out[0:TOK, FEAT:WIDE] = edge_ref[...]
        out[TOK:ROWS, FEAT:WIDE] = jnp.zeros((16, LANES), BF16)


def ranks(listed, x_index, z_index):
    line = lax.broadcasted_iota(jnp.int32, (NX * EXP_DEV, TOK), 0)
    label = EXP_DEV * (((x_index + line // EXP_DEV) % NX) * NZ + z_index) + line % EXP_DEV
    label = label.astype(F32)
    member = jnp.zeros((NX * EXP_DEV, TOK), F32)
    for slot in range(8):
        member = member + jnp.where(listed[slot:slot + 1, :] == label, 1.0, 0.0)
    row = lax.broadcasted_iota(jnp.int32, (TOK, TOK), 0)
    column = lax.broadcasted_iota(jnp.int32, (TOK, TOK), 1)
    upto = jnp.where(row <= column, 1.0, 0.0).astype(BF16)
    running = jnp.dot(member.astype(BF16), upto, preferred_element_type=F32)
    return member, member * running


def selectors(rank, count, spot):
    size = count * EXP_DEV * CAP
    shape = (NX * size, NX * EXP_DEV)
    row = lax.broadcasted_iota(jnp.int32, shape, 0)
    column = lax.broadcasted_iota(jnp.int32, shape, 1)
    inside = row % size
    if count == 1:
        expert = inside // CAP
        mine = row >= 0
    else:
        expert = 2 * (inside // (2 * count * CAP)) + (inside % (2 * CAP)) // CAP
        mine = (inside // (2 * CAP)) % count == spot
    match = jnp.logical_and(column == (row // size) * EXP_DEV + expert, mine)
    spread = jnp.where(match, 1.0, 0.0).astype(BF16)
    wide = jnp.dot(spread, rank.astype(BF16), preferred_element_type=F32)
    want = (lax.broadcasted_iota(jnp.int32, (NX * size, TOK), 0) % CAP + 1).astype(F32)
    return jnp.where(wide == want, 1.0, 0.0).astype(BF16)


def fold(rows, out, k, begin):
    for part in range(rows.shape[0] // 16):
        line, lane = begin + part // FOLD * 16, part % FOLD * LANES
        out[line:line + 16, lane:lane + LANES] = rows[part * 16:part * 16 + 16, :]


def choose(select_ref, values, size):
    total = None
    for spot, value in enumerate(values):
        picked = jnp.dot(select_ref[spot], value, preferred_element_type=F32)
        total = picked if total is None else total + picked
    total = total.astype(BF16)
    return [total[k * size:(k + 1) * size, :] for k in range(NX)]


def pack_kernel(chunk, place_ref, before_ref, *refs):
    count = CHUNKS[chunk]
    size = count * LAST
    blocks, refs = refs[:count], refs[count:]
    counts_ref, select_ref, outs = refs[-NX - 2], refs[-NX - 1], refs[-NX:]
    extra = refs[:-NX - 2]
    counts = before_ref[...]
    for spot, block in enumerate(blocks):
        listed = block[TOK:ROWS, 0:TOK].astype(F32)
        member, rank = ranks(listed, place_ref[0], place_ref[1])
        counts = counts + jnp.sum(member, axis=1, keepdims=True)
        select_ref[spot] = selectors(rank, count, spot)
    counts_ref[...] = counts
    features = choose(select_ref, [block[0:TOK, 0:FEAT] for block in blocks], size)
    for k, out in enumerate(outs):
        out[0:size, 0:FEAT] = features[k]
    if chunk == 2:
        older_ref, old_ref, edge_ref = extra
        near = choose(old_ref, [block[0:TOK, FEAT:WIDE] for block in blocks], 2 * LAST)
        own = choose(older_ref, [edge_ref[...]], LAST)
        for k, out in enumerate(outs):
            out[0:size, FEAT:WIDE] = near[k]
            fold(own[k], out, k, size)
    elif chunk == 3:
        old_ref, = extra
        near = choose(old_ref, [block[0:TOK, FEAT:WIDE] for block in blocks], 2 * LAST)
        for k, out in enumerate(outs):
            out[0:size, FEAT:WIDE] = near[k]
    elif chunk == 4:
        old_ref, back_ref, end_ref = extra
        near = choose(old_ref, [blocks[0][0:TOK, FEAT:WIDE], back_ref[...]], 2 * LAST)
        end = choose(select_ref, [end_ref[...]], LAST)
        for k, out in enumerate(outs):
            out[0:size, FEAT:WIDE] = end[k]
            fold(near[k], out, k, size)
            mine = counts[k * EXP_DEV:(k + 1) * EXP_DEV, :]
            out[size:size + 16, FOLD * LANES:FEAT] = jnp.concatenate([mine, mine], axis=0).astype(BF16)


SHAPES = ((LAST, FEAT), (2 * LAST, FEAT), (2 * LAST + 16, WIDE), (2 * LAST, WIDE), (LAST + 32, WIDE))


def pack(chunk, place, before, blocks, *extra):
    count = len(blocks)
    size = count * LAST
    counts, select, *packed = pl.pallas_call(
        functools.partial(pack_kernel, chunk),
        out_shape=[
            jax.ShapeDtypeStruct((NX * EXP_DEV, LANES), F32),
            jax.ShapeDtypeStruct((count, NX * size, TOK), BF16),
        ]
        + [jax.ShapeDtypeStruct(SHAPES[chunk], BF16)] * NX,
        in_specs=[smem()] + [vmem()] * (1 + count + len(extra)),
        out_specs=[vmem()] * (2 + NX),
        compiler_params=params(16),
        cost_estimate=cost(1 + count),
        name="pack_%d" % chunk,
    )(place, before, *blocks, *extra)
    return counts, select, packed


def dot(left, right):
    return jnp.dot(left, right, precision=lax.Precision.HIGHEST, preferred_element_type=F32)


def invert(factor):
    width = factor.shape[0]
    row = lax.broadcasted_iota(jnp.int32, (width, width), 0)
    column = lax.broadcasted_iota(jnp.int32, (width, width), 1)
    diagonal = jnp.where(row == column, factor, 0.0)
    across = 1.0 / jnp.sum(diagonal, axis=0, keepdims=True)
    down = 1.0 / jnp.sum(diagonal, axis=1, keepdims=True)

    def level(span):
        same = row // (2 * span) == column // (2 * span)
        return jnp.where(jnp.logical_and(same, row // span < column // span), factor, 0.0)

    result = jnp.where(row == column, across, 0.0) - down * level(1) * across
    span = 2
    while span < width:
        result = result - dot(dot(result, level(span)), result)
        span *= 2
    return result


def inverse_kernel(factor_ref, out_ref):
    near = invert(factor_ref[0, 0:LANES, 0:LANES])
    far = invert(factor_ref[0, LANES:TOK, LANES:TOK])
    corner = -dot(dot(near, factor_ref[0, 0:LANES, LANES:TOK]), far)
    for copy in range(NY * NC):
        out_ref[copy, 0:LANES, 0:LANES] = near
        out_ref[copy, LANES:TOK, LANES:TOK] = far
        out_ref[copy, LANES:TOK, 0:LANES] = jnp.zeros((LANES, LANES), F32)
        out_ref[copy, 0:LANES, LANES:TOK] = corner


def split(value):
    high = value.astype(BF16)
    return high, (value - high.astype(F32)).astype(BF16)


def errors_kernel(weights_ref, indices_ref, codebook_ref, inverse_ref, out_ref):
    picked = indices_ref[0]
    rows, pairs = picked.shape
    book = codebook_ref[0].astype(F32)
    book = jnp.concatenate([book, jnp.zeros(book.shape, F32)], axis=1)
    coords = [
        jnp.take_along_axis(jnp.broadcast_to(book[c:c + 1, :], (rows, pairs)), picked, axis=1)
        for c in range(2)
    ]
    both = jnp.concatenate(coords, axis=1).astype(BF16)
    row = lax.broadcasted_iota(jnp.int32, (2 * pairs, 2 * pairs), 0)
    column = lax.broadcasted_iota(jnp.int32, (2 * pairs, 2 * pairs), 1)
    weave = jnp.where(column == 2 * (row % pairs) + row // pairs, 1.0, 0.0).astype(BF16)
    decoded = jnp.dot(both, weave, preferred_element_type=F32)
    residual_high, residual_low = split(weights_ref[0].astype(F32) - decoded)
    inverse_high, inverse_low = split(inverse_ref[0])
    total = jnp.dot(residual_low, inverse_high, preferred_element_type=F32)
    total = total + jnp.dot(residual_high, inverse_low, preferred_element_type=F32)
    out_ref[0] = total + jnp.dot(residual_high, inverse_high, preferred_element_type=F32)


def hessian_kernel(place_ref, *refs):
    pieces = NX * len(CHUNKS)
    messages, windows_of, out_ref = refs[:pieces], refs[pieces:-1], refs[-1]
    pair = pl.program_id(0)
    first = place_ref[2] == 0
    row = lax.broadcasted_iota(jnp.int32, (PAIR, TOK), 0)
    single = row // CAP - 2 * (pair % 2)
    double = (row % (2 * CAP)) // CAP
    features, windows = [], []
    for k in range(NX):
        for c, count in enumerate(CHUNKS):
            step = pair // (3 - count)
            where = pl.ds(pl.multiple_of(step * PAIR, 16), PAIR)
            features.append(messages[k * len(CHUNKS) + c][where, 0:FEAT])
            mine_ref, other_ref = windows_of[0:2] if c < 3 else windows_of[2:4]
            begin = WINDOW_ROWS[c] + k * count * LAST
            where = pl.ds(pl.multiple_of(begin + step * PAIR, 16), PAIR)
            near, far = mine_ref[where, :].astype(F32), other_ref[where, :].astype(F32)
            both = jnp.concatenate(
                [jnp.where(first, near, far), jnp.where(first, far, near)], axis=1
            )
            owner = single if count == 1 else double
            windows.append(
                jnp.concatenate(
                    [jnp.where(owner == e, both, 0.0) for e in range(2)], axis=1
                ).astype(BF16)
            )
    product = lax.dot_general(
        jnp.concatenate(features, axis=0),
        jnp.concatenate(windows, axis=0),
        (((0,), (0,)), ((), ())),
        preferred_element_type=F32,
    )
    counts = jnp.zeros((16, LANES), F32)
    for k in range(NX):
        ref = messages[k * len(CHUNKS) + 4]
        counts = counts + ref[LAST:LAST + 16, FOLD * LANES:FEAT].astype(F32)
    line = lax.broadcasted_iota(jnp.int32, counts.shape, 0)
    for e in range(2):
        count = jnp.sum(jnp.where(line == 2 * pair + e, counts, 0.0), axis=0, keepdims=True)
        scale = 2.0 / count
        scale = jnp.concatenate([scale, scale], axis=1)
        out_ref[e] = product[:, e * TOK:(e + 1) * TOK] * scale


WINDOW_ROWS = (0, 4 * LAST, 12 * LAST, 0, 8 * LAST)


def unfold(ref, out_ref, source, begin, rows):
    for part in range(rows // 16):
        line, lane = source + part // FOLD * 16, part % FOLD * LANES
        out_ref[begin + part * 16:begin + part * 16 + 16, :] = ref[line:line + 16, lane:lane + LANES]


def early_kernel(*refs):
    second, third, out_ref = refs[0:NX], refs[NX:2 * NX], refs[-1]
    for k in range(NX):
        unfold(second[k], out_ref, 2 * LAST, WINDOW_ROWS[0] + k * LAST, LAST)
        begin = WINDOW_ROWS[1] + k * 2 * LAST
        out_ref[begin:begin + 2 * LAST, :] = second[k][0:2 * LAST, FEAT:WIDE]
        begin = WINDOW_ROWS[2] + k * 2 * LAST
        out_ref[begin:begin + 2 * LAST, :] = third[k][:, FEAT:WIDE]


def late_kernel(*refs):
    last, out_ref = refs[0:NX], refs[-1]
    for k in range(NX):
        unfold(last[k], out_ref, LAST, WINDOW_ROWS[3] + k * 2 * LAST, 2 * LAST)
        begin = WINDOW_ROWS[4] + k * LAST
        out_ref[begin:begin + LAST, :] = last[k][0:LAST, FEAT:WIDE]


def shifted(size, step):
    return [(i, (i + step) % size) for i in range(size)]


def move(value, axis, size, step):
    return lax.ppermute(value, axis, shifted(size, step))


def tie(*values):
    return lax.optimization_barrier(values)


def send(packed):
    return [packed[0]] + [move(packed[k], "x", NX, k) for k in (1, 2, 3)]


def swap(kernel, rows, values):
    mine = pl.pallas_call(
        kernel,
        out_shape=jax.ShapeDtypeStruct((rows, LANES), BF16),
        in_specs=[vmem()] * len(values),
        out_specs=vmem(),
        compiler_params=params(8),
        cost_estimate=cost(0.5),
        name="window_half",
    )(*values)
    return mine, move(mine, "core", NC, 1)


def local(tokens, routing, weights, indices, codebook, hinv_panel):
    x_index, z_index = lax.axis_index("x"), lax.axis_index("z")
    core = lax.axis_index("core")
    place = jnp.stack([x_index, z_index, core]).astype(jnp.int32)
    payload = pl.pallas_call(
        payload_kernel,
        out_shape=jax.ShapeDtypeStruct((ROWS, FEAT), BF16),
        in_specs=[vmem()] * 2,
        out_specs=vmem(),
        compiler_params=params(4),
        cost_estimate=cost(0.3),
        name="payload",
    )(tokens, routing.T)
    f1, b1 = move(payload, "z", NZ, 1), move(payload, "z", NZ, -1)
    halves = pl.pallas_call(
        halves_kernel,
        grid=(1,),
        out_shape=jax.ShapeDtypeStruct((NY * NC, TOK, LANES), BF16),
        in_specs=[pl.BlockSpec((TOK, 2 * LANES), lambda i: (0, 0))],
        out_specs=pl.BlockSpec((NY * NC, TOK, LANES), lambda i: (0, 0, 0)),
        compiler_params=params(4),
        cost_estimate=cost(0.3),
        name="halves",
    )(tokens)
    edge = lax.all_to_all(halves, ("y", "core"), 0, 0, tiled=True)[0]
    counts, select0, packed = pack(
        0, place, jnp.zeros((NX * EXP_DEV, LANES), F32), [payload]
    )

    f1, b1, counts, edge, *packed = tie(f1, b1, counts, edge, *packed)
    joined_f, joined_b = pl.pallas_call(
        join_kernel,
        out_shape=[jax.ShapeDtypeStruct((ROWS, WIDE), BF16)] * 2,
        in_specs=[vmem()] * 3,
        out_specs=[vmem()] * 2,
        compiler_params=params(8),
        cost_estimate=cost(0.6),
        name="join",
    )(f1, b1, edge)
    f2, b2 = move(joined_f, "z", NZ, 1), move(joined_b, "z", NZ, -1)
    sent = [send(packed)]
    counts, select1, packed = pack(1, place, counts, [f1, b1])
    sent.append(send(packed))

    f2, b2, counts, *sent[0] = tie(f2, b2, counts, *sent[0])
    f3, b3 = move(f2, "z", NZ, 1), move(b2, "z", NZ, -1)
    counts, select2, packed = pack(2, place, counts, [f2, b2], select0, select1, edge)
    sent.append(send(packed))
    hinv_panel, counts = tie(hinv_panel, counts)
    inverse = pl.pallas_call(
        inverse_kernel,
        out_shape=jax.ShapeDtypeStruct((NY * NC, TOK, TOK), F32),
        in_specs=[vmem()],
        out_specs=vmem(),
        compiler_params=params(8),
        cost_estimate=cost(7.5),
        name="inverse",
    )(hinv_panel)

    f3, b3, counts, inverse, *sent[1] = tie(f3, b3, counts, inverse, *sent[1])
    inverses = lax.all_to_all(inverse, ("y", "core"), 0, 0, tiled=True)
    f4 = move(f3, "z", NZ, 1)
    back = move(b3[0:TOK, FEAT:WIDE], "z", NZ, -1)
    counts, select3, packed = pack(3, place, counts, [f3, b3], select2)
    sent.append(send(packed))

    f4, back, counts, *sent[2] = tie(f4, back, counts, *sent[2])
    end = move(f4[0:TOK, FEAT:WIDE], "z", NZ, 1)
    counts, _, packed = pack(4, place, counts, [f4], select3, back, end)
    weights, packed[0] = tie(weights, packed[0])
    sent.append(send(packed))
    early = swap(early_kernel, 20 * LAST, [*sent[2], *sent[3]])
    experts, rows, width = weights.shape
    pairs = indices.shape[2]
    errors = pl.pallas_call(
        errors_kernel,
        grid=(experts,),
        out_shape=jax.ShapeDtypeStruct(weights.shape, F32),
        in_specs=[
            pl.BlockSpec((1, rows, width), lambda e: (e, 0, 0)),
            pl.BlockSpec((1, rows, pairs), lambda e: (e, 0, 0)),
            pl.BlockSpec((1,) + codebook.shape[1:], lambda e: (e, 0, 0)),
            pl.BlockSpec((1, width, width), lambda e: (e, 0, 0)),
        ],
        out_specs=pl.BlockSpec((1, rows, width), lambda e: (e, 0, 0)),
        compiler_params=params(8),
        cost_estimate=cost(5),
        name="errors",
    )(weights, indices, codebook, inverses)

    errors, *rest = tie(errors, *sent[4], *sent[3])
    sent[4], sent[3] = rest[:NX], rest[NX:]
    late = swap(late_kernel, 12 * LAST, sent[4])
    operands = [sent[c][k] for k in range(NX) for c in range(len(CHUNKS))]
    operands += [*early, *late]
    hessian = pl.pallas_call(
        hessian_kernel,
        grid=(EXP_DEV // 2,),
        out_shape=jax.ShapeDtypeStruct((EXP_DEV, FEAT, TOK), F32),
        in_specs=[smem()] + [vmem()] * len(operands),
        out_specs=pl.BlockSpec((2, FEAT, TOK), lambda p: (p, 0, 0)),
        compiler_params=params(20),
        cost_estimate=cost(7.5),
        name="hessian",
    )(place, *operands)
    return hessian, errors


def solution(mesh):
    grid = Mesh(mesh.devices.reshape(NX, NZ, NY, NC), ("x", "z", "y", "core"))
    expert, row = ("x", "z"), ("y", "core")
    in_specs = (
        P(expert, row),
        P(expert, None),
        P(expert, row, None),
        P(expert, row, None),
        P(expert, None, None),
        P(expert + row, None, None),
    )
    out_specs = (P(expert, row, None), P(expert, row, None))
    return jax.shard_map(local, mesh=grid, in_specs=in_specs, out_specs=out_specs, check_vma=False)
```

time: 178 us -> 134 us (0.75)
  blocking collectives: 29.3 us -> 0 us
  between operations: 14.4 us -> 1.08 us
  local copies, waits for them, and re-layouts: 4.32 us -> 13.9 us
  waiting for transfers between devices: 34.1 us -> 28.2 us
  other arithmetic: 3.1 us -> 0.08 us
  Pallas kernels: 36.9 us -> 34.6 us
    all_gather x1 -> x0, blocking collectives: 29.3 us -> none  [local(): gathered = lax.all_gather(window_payload, 'z', axis=0, tiled=False)]
    unnamed x36 -> x92, local copies, waits for them, and re-layouts: 3.41 us -> 12.9 us
    ppermute x31 -> x26, starting transfers between devices: 55.1 us -> 46.4 us  [move(): return lax.ppermute(value, axis, shifted(size, step))]
    all_to_all x0 -> x2, starting transfers between devices: none -> 8.12 us  [the longest x1 4.47 us: local(): edge = lax.all_to_all(halves, ('y', 'core'), 0, 0, tiled=True)[0]]
    ppermute x31 -> x26, waiting for transfers between devices: 34.1 us -> 27.1 us  [move(): return lax.ppermute(value, axis, shifted(size, step))]
    select_n x3 -> x0, other arithmetic: 2.97 us -> none  [the longest x1 1.3 us: local(): jnp.where(y_index == 0, low, jnp.where(y_index == 1, up_low, jnp.where(y_...]
    pallas_call x8 -> x10, Pallas kernels: 24.1 us -> 22 us  [the longest x5 13.4 us: pack(): pl.pallas_call(functools.partial(pack_kernel, chunk), out_shape=[jax.Shap...]
  transfers between devices with their start and end apart: 32 -> 28, of which waited for: 11 -> 13; matrix products, arithmetic and copies ran while one was open for 2% -> 1% of each run, Pallas kernels for 15% -> 20%
where the time goes in v2:
time: 134 us; the launch traced here: 132 us
  starting transfers between devices  54.5 us (41%)
  Pallas kernels  34.6 us (26%)
  waiting for transfers between devices  28.2 us (21%)
  local copies, waits for them, and re-layouts  13.9 us (10%)
    ppermute x26, starting transfers between devices, move(): return lax.ppermute(value, axis, shifted(size, step))  46.4 us
    ppermute x26, waiting for transfers between devices, move(): return lax.ppermute(value, axis, shifted(size, step))  27.1 us
    pallas_call x5, Pallas kernels, pack(): pl.pallas_call(functools.partial(pack_kernel, chunk), out_shape=[jax.Shap...  13.4 us
    unnamed x92, local copies, waits for them, and re-layouts  12.9 us
    pallas_call x1, Pallas kernels, local(): pl.pallas_call(hessian_kernel, grid=(EXP_DEV // 2,), out_shape=jax.ShapeD...  7.37 us
    pallas_call x1, Pallas kernels, local(): pl.pallas_call(inverse_kernel, out_shape=jax.ShapeDtypeStruct((NY * NC, T...  6.32 us
    pallas_call x1, Pallas kernels, local(): pl.pallas_call(errors_kernel, grid=(experts,), out_shape=jax.ShapeDtypeSt...  5.25 us
    all_to_all x1, starting transfers between devices, local(): edge = lax.all_to_all(halves, ('y', 'core'), 0, 0, tiled=True)[0]  4.47 us
  transfers between devices with their start and end apart: 28, of which 13 were waited for; matrix products, arithmetic and copies ran while one was open for 1% of the time, Pallas kernels for 20%

profile of v2, /device:TPU:2, one launch (start us, length us, event | category | flops | bytes accessed | tf_op | source)
XLA Modules:
  0.0 132.4 jit_solution(14746462792543610517)
XLA Ops:
  0.6 1.0 copy-done
  1.7 0.9 halves.1
  2.5 4.5 %all-to-all-start = ((bf16[8,256,128]{2,1,0:T(8,128)(2,1)}), bf16[8,256,128]{2,1,0:T(8,128)(2,1)}, u32[]{:S(2)}, u32[]{:S(2)}) async-start(bf16[8,256,128]{2,1,0:T(8,128)(2,1)} %halves.1), calls=%async_computation | async-start | bytes 1048576 | tf_op jit(solution)/shard_map/all_to_all | solution.py:360
  7.0 0.7 copy-done.41
  7.7 5.9 %collective-permute-start.1 = (bf16[272,896]{1,0:T(8,128)(2,1)S(1)}, bf16[272,896]{1,0:T(8,128)(2,1)S(1)}, u32[]{:S(2)}, u32[]{:S(2)}) collective-permute-start(bf16[272,896]{1,0:T(8,128)(2,1)S(1)} %payload.1.refs_0_), channel_id=1, source_target_pairs={{0,56},{8,0},{16,8},{24,16},{32,24},{40,32},{48,40},{56,48},{1,57}... | collective-permute-start | bytes 1462280 | tf_op jit(solution)/shard_map/ppermute | solution.py:312
  13.8 1.2 pack_0.1
  15.0 0.7 copy-done.31
  15.7 0.7 copy-done.33
  16.4 1.1 all-to-all-done
  17.4 0.9 slice_bitcast_fusion.edge_ref.refs_4_
  18.3 6.4 %collective-permute-done.1.backward_ref.refs_1_ = bf16[272,896]{1,0:T(8,128)(2,1)S(1)} collective-permute-done((bf16[272,896]{1,0:T(8,128)(2,1)S(1)}, bf16[272,896]{1,0:T(8,128)(2,1)S(1)}, u32[]{:S(2)}, u32[]{:S(2)}) %collective-permute-start.1) | collective-permute-done | bytes 487456 | tf_op jit(solution)/shard_map/ppermute | solution.py:312
  24.7 3.4 %collective-permute-done.forward_ref.refs_0_ = bf16[272,896]{1,0:T(8,128)(2,1)S(1)} collective-permute-done((bf16[272,896]{1,0:T(8,128)(2,1)S(1)}, bf16[272,896]{1,0:T(8,128)(2,1)S(1)}, u32[]{:S(2)}, u32[]{:S(2)}) %collective-permute-start) | collective-permute-done | bytes 487456 | tf_op jit(solution)/shard_map/ppermute | solution.py:312
  28.1 0.1 join.1
  28.3 3.2 %collective-permute-start.3 = (bf16[272,1024]{1,0:T(8,128)(2,1)S(1)}, bf16[272,1024]{1,0:T(8,128)(2,1)S(1)}, u32[]{:S(2)}, u32[]{:S(2)}) collective-permute-start(bf16[272,1024]{1,0:T(8,128)(2,1)S(1)} %get-tuple-element.84), channel_id=1, source_target_pairs={{0,56},{8,0},{16,8},{24,16},{32,24},{40,32},{48,40},{56,48},{1,57}... | collective-permute-start | bytes 1671176 | tf_op jit(solution)/shard_map/ppermute | solution.py:312
  31.6 1.5 %collective-permute-start.4 = (bf16[96,896]{1,0:T(8,128)(2,1)S(1)}, bf16[96,896]{1,0:T(8,128)(2,1)S(1)}, u32[]{:S(2)}, u32[]{:S(2)}) collective-permute-start(bf16[96,896]{1,0:T(8,128)(2,1)S(1)} %get-tuple-element.88), channel_id=1, source_target_pairs={{0,64},{64,128},{128,192},{192,0},{1,65},{65,129},{129,193},{193,1... | collective-permute-start | bytes 516104 | tf_op jit(solution)/shard_map/ppermute | solution.py:312
  33.1 1.1 collective-permute-start.5
  34.2 2.2 %collective-permute-start.6 = (bf16[96,896]{1,0:T(8,128)(2,1)S(1)}, bf16[96,896]{1,0:T(8,128)(2,1)S(1)}, u32[]{:S(2)}, u32[]{:S(2)}) collective-permute-start(bf16[96,896]{1,0:T(8,128)(2,1)S(1)} %get-tuple-element.90), channel_id=1, source_target_pairs={{0,192},{64,0},{128,64},{192,128},{1,193},{65,1},{129,65},{193,129... | collective-permute-start | bytes 516104 | tf_op jit(solution)/shard_map/ppermute | solution.py:312
  36.3 3.0 %pack_1.1 = (f32[32,128]{1,0:T(8,128)S(1)}, bf16[2,768,256]{2,1,0:T(8,128)(2,1)S(1)}, bf16[192,896]{1,0:T(8,128)(2,1)S(1)}, bf16[192,896]{1,0:T(8,128)(2,1)S(1)}...) custom-call(s32[3]{0:T(128)S(1)} %pad_add_fusion.place_ref, f32[32,128]{1,0:T(8,128)S(1)} %get-tuple-element.85.before_ref, ...), custom_call_target="tpu_custom_call" | custom-call | bytes 11070000 | tf_op jit(solution)/shard_map/pack_1/pallas_call | solution.py:158
  39.3 0.8 copy-done.22
  40.1 1.3 %collective-permute-done.5.refs_10_ = bf16[96,896]{1,0:T(8,128)(2,1)S(1)} collective-permute-done((bf16[96,896]{1,0:T(8,128)(2,1)S(1)}, bf16[96,896]{1,0:T(8,128)(2,1)S(1)}, u32[]{:S(2)}, u32[]{:S(2)}) %collective-permute-start.5) | collective-permute-done | bytes 172064 | tf_op jit(solution)/shard_map/ppermute | solution.py:312
  41.4 1.0 collective-permute-done.6.refs_15_
  42.4 1.1 collective-permute-done.2.refs_0_
  43.5 3.2 %collective-permute-start.8 = (bf16[272,1024]{1,0:T(8,128)(2,1)S(1)}, bf16[272,1024]{1,0:T(8,128)(2,1)S(1)}, u32[]{:S(2)}, u32[]{:S(2)}) collective-permute-start(bf16[272,1024]{1,0:T(8,128)(2,1)S(1)} %collective-permute-done.3.refs_1_), channel_id=1, source_target_pairs={{0,56},{8,0},{16,8},{24,16},{32,24},{40,32},{48,40},{56,48},{1,57}... | collective-permute-start | bytes 1671176 | tf_op jit(solution)/shard_map/ppermute | solution.py:312
  46.7 1.5 %collective-permute-start.9 = (bf16[192,896]{1,0:T(8,128)(2,1)S(1)}, bf16[192,896]{1,0:T(8,128)(2,1)S(1)}, u32[]{:S(2)}, u32[]{:S(2)}) collective-permute-start(bf16[192,896]{1,0:T(8,128)(2,1)S(1)} %get-tuple-element.101), channel_id=1, source_target_pairs={{0,64},{64,128},{128,192},{192,0},{1,65},{65,129},{129,193},{193,1... | collective-permute-start | bytes 1032200 | tf_op jit(solution)/shard_map/ppermute | solution.py:312
  48.2 1.1 collective-permute-start.10
  49.3 2.2 %collective-permute-start.11 = (bf16[192,896]{1,0:T(8,128)(2,1)S(1)}, bf16[192,896]{1,0:T(8,128)(2,1)S(1)}, u32[]{:S(2)}, u32[]{:S(2)}) collective-permute-start(bf16[192,896]{1,0:T(8,128)(2,1)S(1)} %get-tuple-element.103), channel_id=1, source_target_pairs={{0,192},{64,0},{128,64},{192,128},{1,193},{65,1},{129,65},{193,129... | collective-permute-start | bytes 1032200 | tf_op jit(solution)/shard_map/ppermute | solution.py:312
  51.5 3.4 %pack_2.1 = (f32[32,128]{1,0:T(8,128)S(1)}, bf16[2,768,256]{2,1,0:T(8,128)(2,1)S(1)}, bf16[208,1024]{1,0:T(8,128)(2,1)S(1)}, bf16[208,1024]{1,0:T(8,128)(2,1)S(1...) custom-call(s32[3]{0:T(128)S(1)} %pad_add_fusion.place_ref, f32[32,128]{1,0:T(8,128)S(1)} %get-tuple-element.94.before_ref, ...), custom_call_target="tpu_custom_call" | custom-call | bytes 11070000 | tf_op jit(solution)/shard_map/pack_2/pallas_call | solution.py:158
  54.9 0.9 copy-done.18
  55.8 6.3 %inverse.1 = f32[8,256,256]{2,1,0:T(8,128)} custom-call(f32[1,256,256]{2,1,0:T(8,128)S(1)} %copy-done.30), custom_call_target="tpu_custom_call" | custom-call | bytes 27675000 | tf_op jit(solution)/shard_map/inverse/pallas_call | solution.py:385
  62.1 0.7 copy-done.24
  62.8 0.7 copy-done.26
  63.6 0.4 collective-permute-done.11.refs_16_
  64.0 0.8 copy-done.28
  64.8 0.8 copy-done.20
  65.6 3.6 %all-to-all-start.1 = ((f32[8,256,256]{2,1,0:T(8,128)}), f32[8,256,256]{2,1,0:T(8,128)S(1)}, u32[]{:S(2)}, u32[]{:S(2)}) async-start(f32[8,256,256]{2,1,0:T(8,128)} %inverse.1), calls=%async_computation.1 | async-start | bytes 4194304 | tf_op jit(solution)/shard_map/all_to_all | solution.py:396
  69.3 1.3 %collective-permute-start.14 = (bf16[208,1024]{1,0:T(8,128)(2,1)}, bf16[208,1024]{1,0:T(8,128)(2,1)S(1)}, u32[]{:S(2)}, u32[]{:S(2)}) collective-permute-start(bf16[208,1024]{1,0:T(8,128)(2,1)} %copy-done.45), channel_id=1, source_target_pairs={{0,64},{64,128},{128,192},{192,0},{1,65},{65,129},{129,193},{193,1... | collective-permute-start | bytes 1277960 | tf_op jit(solution)/shard_map/ppermute | solution.py:312
  70.6 2.2 %collective-permute-start.15 = (bf16[208,1024]{1,0:T(8,128)(2,1)}, bf16[208,1024]{1,0:T(8,128)(2,1)S(1)}, u32[]{:S(2)}, u32[]{:S(2)}) collective-permute-start(bf16[208,1024]{1,0:T(8,128)(2,1)} %copy-done.44), channel_id=1, source_target_pairs={{0,128},{64,192},{128,0},{192,64},{1,129},{65,193},{129,1},{193,65... | collective-permute-start | bytes 1277960 | tf_op jit(solution)/shard_map/ppermute | solution.py:312
  72.8 0.9 collective-permute-start.16
  73.7 1.1 copy-done.19
  74.9 1.1 copy-done.21
  75.9 3.4 %pack_3.1 = (f32[32,128]{1,0:T(8,128)S(1)}, bf16[2,768,256]{2,1,0:T(8,128)(2,1)S(1)}, bf16[192,1024]{1,0:T(8,128)(2,1)S(1)}, bf16[192,1024]{1,0:T(8,128)(2,1)S(1...) custom-call(s32[3]{0:T(128)S(1)} %pad_add_fusion.place_ref, ...), custom_call_target="tpu_custom_call" | custom-call | bytes 11070000 | tf_op jit(solution)/shard_map/pack_3/pallas_call | solution.py:158
  79.4 1.2 collective-permute-start.21
  80.6 1.6 %collective-permute-done.14.refs_1_.refs_7_ = bf16[208,1024]{1,0:T(8,128)(2,1)S(1)} collective-permute-done((bf16[208,1024]{1,0:T(8,128)(2,1)}, bf16[208,1024]{1,0:T(8,128)(2,1)S(1)}, u32[]{:S(2)}, u32[]{:S(2)}) %collective-permute-start.14) | collective-permute-done | bytes 426016 | tf_op jit(solution)/shard_map/ppermute | solution.py:312
  82.2 9.6 %collective-permute-start.22 = (bf16[192,1024]{1,0:T(8,128)(2,1)S(1)}, bf16[192,1024]{1,0:T(8,128)(2,1)S(1)}, u32[]{:S(2)}, u32[]{:S(2)}) collective-permute-start(bf16[192,1024]{1,0:T(8,128)(2,1)S(1)} %get-tuple-element.128), channel_id=1, source_target_pairs={{0,128},{64,192},{128,0},{192,64},{1,129},{65,193},{129,1},{193,65... | collective-permute-start | bytes 1179656 | tf_op jit(solution)/shard_map/ppermute | solution.py:312
  91.8 2.1 %collective-permute-start.23 = (bf16[192,1024]{1,0:T(8,128)(2,1)S(1)}, bf16[192,1024]{1,0:T(8,128)(2,1)S(1)}, u32[]{:S(2)}, u32[]{:S(2)}) collective-permute-start(bf16[192,1024]{1,0:T(8,128)(2,1)S(1)} %get-tuple-element.129), channel_id=1, source_target_pairs={{0,192},{64,0},{128,64},{192,128},{1,193},{65,1},{129,65},{193,129... | collective-permute-start | bytes 1179656 | tf_op jit(solution)/shard_map/ppermute | solution.py:312
  93.9 0.4 collective-permute-done.16.refs_3_.refs_17_
  94.2 1.6 %collective-permute-start.13 = (bf16[256,128]{1,0:T(8,128)(2,1)S(1)}, bf16[256,128]{1,0:T(8,128)(2,1)S(1)}, u32[]{:S(2)}, u32[]{:S(2)}) collective-permute-start(bf16[256,128]{1,0:T(8,128)(2,1)S(1)} %slice.10), channel_id=1, source_target_pairs={{0,56},{8,0},{16,8},{24,16},{32,24},{40,32},{48,40},{56,48},{1,57}... | collective-permute-start | bytes 196616 | tf_op jit(solution)/shard_map/ppermute | solution.py:312
  95.8 2.7 %collective-permute-done.13.refs_2_ = bf16[256,128]{1,0:T(8,128)(2,1)S(1)} collective-permute-done((bf16[256,128]{1,0:T(8,128)(2,1)S(1)}, bf16[256,128]{1,0:T(8,128)(2,1)S(1)}, u32[]{:S(2)}, u32[]{:S(2)}) %collective-permute-start.13) | collective-permute-done | bytes 65568 | tf_op jit(solution)/shard_map/ppermute | solution.py:312
  98.6 5.5 %collective-permute-done.17.refs_3_ = bf16[256,128]{1,0:T(8,128)(2,1)S(1)} collective-permute-done((bf16[256,128]{1,0:T(8,128)(2,1)S(1)}, bf16[256,128]{1,0:T(8,128)(2,1)S(1)}, u32[]{:S(2)}, u32[]{:S(2)}) %collective-permute-start.17) | collective-permute-done | bytes 65568 | tf_op jit(solution)/shard_map/ppermute | solution.py:312
  104.1 2.4 %pack_4.1 = (f32[32,128]{1,0:T(8,128)}, bf16[1,384,256]{2,1,0:T(8,128)(2,1)}, bf16[128,1024]{1,0:T(8,128)(2,1)S(1)}, bf16[128,1024]{1,0:T(8,128)(2,1)}, bf16[128...) custom-call(s32[3]{0:T(128)S(1)} %pad_add_fusion.place_ref, f32[32,128]{1,0:T(8,128)S(1)} %get-tuple-element.115.before_ref, ...), custom_call_target="tpu_custom_call" | custom-call | bytes 7380000 | tf_op jit(solution)/shard_map/pack_4/pallas_call | solution.py:158
  106.5 1.1 collective-permute-start.18
  107.6 1.6 %collective-permute-start.19 = (bf16[128,1024]{1,0:T(8,128)(2,1)}, bf16[128,1024]{1,0:T(8,128)(2,1)}, u32[]{:S(2)}, u32[]{:S(2)}) collective-permute-start(bf16[128,1024]{1,0:T(8,128)(2,1)} %get-tuple-element.124), channel_id=1, source_target_pairs={{0,128},{64,192},{128,0},{192,64},{1,129},{65,193},{129,1},{193,65... | collective-permute-start | bytes 786440 | tf_op jit(solution)/shard_map/ppermute | solution.py:312
  109.2 2.5 %collective-permute-start.20 = (bf16[128,1024]{1,0:T(8,128)(2,1)}, bf16[128,1024]{1,0:T(8,128)(2,1)}, u32[]{:S(2)}, u32[]{:S(2)}) collective-permute-start(bf16[128,1024]{1,0:T(8,128)(2,1)} %get-tuple-element.125), channel_id=1, source_target_pairs={{0,192},{64,0},{128,64},{192,128},{1,193},{65,1},{129,65},{193,129... | collective-permute-start | bytes 786440 | tf_op jit(solution)/shard_map/ppermute | solution.py:312
  111.7 1.8 %collective-permute-done.23.refs_7_.refs_18_ = bf16[192,1024]{1,0:T(8,128)(2,1)S(1)} collective-permute-done((bf16[192,1024]{1,0:T(8,128)(2,1)S(1)}, bf16[192,1024]{1,0:T(8,128)(2,1)S(1)}, u32[]{:S(2)}, u32[]{:S(2)}) %collective-permute-start.23) | collective-permute-done | bytes 393248 | tf_op jit(solution)/shard_map/ppermute | solution.py:312
  113.5 0.1 window_half.2.refs_20_
  113.6 0.1 collective-permute-start.24
  113.7 0.5 copy-done.12
  114.2 1.2 copy-done.16
  115.4 1.2 copy-done.17
  116.8 5.3 %errors.1 = f32[8,256,256]{2,1,0:T(8,128)} custom-call(bf16[8,256,256]{2,1,0:T(8,128)(2,1)S(1)} %copy-done.16, s32[8,256,128]{2,1,0:T(8,128)S(1)} %copy-done.17, bf16[8,2,64]{2,1,0:T(2,128)(2,1)S(1)} %copy-done.42, f32[8,256,256]{2,1,0:T(8,128)S(1)} %all-to-all-done.1.inverse_ref), custom_call_target="tpu_custom_call" | custom-call | bytes 18450000 | tf_op jit(solution)/shard_map/errors/pallas_call | solution.py:410
  122.0 1.2 window_half.3.refs_22_
  123.2 0.1 collective-permute-start.25
  123.3 1.5 %collective-permute-done.25.refs_23_ = bf16[1152,128]{1,0:T(8,128)(2,1)S(1)} collective-permute-done((bf16[1152,128]{1,0:T(8,128)(2,1)S(1)}, bf16[1152,128]{1,0:T(8,128)(2,1)S(1)}, u32[]{:S(2)}, u32[]{:S(2)}) %collective-permute-start.25) | collective-permute-done | bytes 294944 | tf_op jit(solution)/shard_map/ppermute | solution.py:312
  125.0 7.4 %hessian.1 = f32[8,896,256]{2,1,0:T(8,128)} custom-call(s32[3]{0:T(128)S(1)} %pad_add_fusion.place_ref, bf16[96,896]{1,0:T(8,128)(2,1)S(1)} %copy-done.34, bf16[192,896]{1,0:T(8,128)(2,1)S(1)} %copy-done.23, bf16[208,1024]{1,0:T(8,128)(2,1)S(1)} %get-tuple-element.114.refs_0_.refs_2_, bf16[192,1024]{1,0:T(8,128)(2,1)S(1)} %copy-done.7, ...), custom_call_target="tpu_custom_call" | custom-call | bytes 27675000 | tf_op jit(solution)/shard_map/hessian/pallas_call | solution.py:431
  (102 shorter events, 0.5 us)
Async XLA Ops:
  0.6 1.0 copy-start
  1.6 5.3 %copy-start.1 = (bf16[256,896]{1,0:T(8,128)(2,1)S(1)}, bf16[256,896]{1,0:T(8,128)(2,1)}, u32[]{:S(2)}) copy-start(bf16[256,896]{1,0:T(8,128)(2,1)} %tokens_ref.3) | copy-start | bytes 1376260
  2.5 14.9 %all-to-all-start = ((bf16[8,256,128]{2,1,0:T(8,128)(2,1)}), bf16[8,256,128]{2,1,0:T(8,128)(2,1)}, u32[]{:S(2)}, u32[]{:S(2)}) async-start(bf16[8,256,128]{2,1,0:T(8,128)(2,1)} %halves.1), calls=%async_computation | async-start | bytes 1048576 | tf_op jit(solution)/shard_map/all_to_all | solution.py:360
  7.7 17.0 %collective-permute-start.1 = (bf16[272,896]{1,0:T(8,128)(2,1)S(1)}, bf16[272,896]{1,0:T(8,128)(2,1)S(1)}, u32[]{:S(2)}, u32[]{:S(2)}) collective-permute-start(bf16[272,896]{1,0:T(8,128)(2,1)S(1)} %payload.1.refs_0_), channel_id=1, source_target_pairs={{0,56},{8,0},{16,8},{24,16},{32,24},{40,32},{48,40},{56,48},{1,57}... | collective-permute-start | bytes 1462280 | tf_op jit(solution)/shard_map/ppermute | solution.py:312
  13.7 14.5 %collective-permute-start = (bf16[272,896]{1,0:T(8,128)(2,1)S(1)}, bf16[272,896]{1,0:T(8,128)(2,1)S(1)}, u32[]{:S(2)}, u32[]{:S(2)}) collective-permute-start(bf16[272,896]{1,0:T(8,128)(2,1)S(1)} %payload.1.refs_0_), channel_id=1, source_target_pairs={{0,8},{8,16},{16,24},{24,32},{32,40},{40,48},{48,56},{56,0},{1,9},... | collective-permute-start | bytes 1462280 | tf_op jit(solution)/shard_map/ppermute | solution.py:312
  17.4 34.0 %copy-start.32 = (bf16[1,384,256]{2,1,0:T(8,128)(2,1)S(1)}, bf16[1,384,256]{2,1,0:T(8,128)(2,1)}, u32[]{:S(2)}) copy-start(bf16[1,384,256]{2,1,0:T(8,128)(2,1)} %copy-done.31) | copy-start | bytes 589828
  28.1 27.6 %copy-start.30 = (f32[1,256,256]{2,1,0:T(8,128)S(1)}, f32[1,256,256]{2,1,0:T(8,128)}, u32[]{:S(2)}) copy-start(f32[1,256,256]{2,1,0:T(8,128)} %factor_ref) | copy-start | bytes 786436
  28.3 15.2 %collective-permute-start.2 = (bf16[272,1024]{1,0:T(8,128)(2,1)S(1)}, bf16[272,1024]{1,0:T(8,128)(2,1)S(1)}, u32[]{:S(2)}, u32[]{:S(2)}) collective-permute-start(bf16[272,1024]{1,0:T(8,128)(2,1)S(1)} %get-tuple-element.83), channel_id=1, source_target_pairs={{0,8},{8,16},{16,24},{24,32},{32,40},{40,48},{48,56},{56,0},{1,9},... | collective-permute-start | bytes 1671176 | tf_op jit(solution)/shard_map/ppermute | solution.py:312
  28.3 15.1 %collective-permute-start.3 = (bf16[272,1024]{1,0:T(8,128)(2,1)S(1)}, bf16[272,1024]{1,0:T(8,128)(2,1)S(1)}, u32[]{:S(2)}, u32[]{:S(2)}) collective-permute-start(bf16[272,1024]{1,0:T(8,128)(2,1)S(1)} %get-tuple-element.84), channel_id=1, source_target_pairs={{0,56},{8,0},{16,8},{24,16},{32,24},{40,32},{48,40},{56,48},{1,57}... | collective-permute-start | bytes 1671176 | tf_op jit(solution)/shard_map/ppermute | solution.py:312
  31.6 8.5 %collective-permute-start.4 = (bf16[96,896]{1,0:T(8,128)(2,1)S(1)}, bf16[96,896]{1,0:T(8,128)(2,1)S(1)}, u32[]{:S(2)}, u32[]{:S(2)}) collective-permute-start(bf16[96,896]{1,0:T(8,128)(2,1)S(1)} %get-tuple-element.88), channel_id=1, source_target_pairs={{0,64},{64,128},{128,192},{192,0},{1,65},{65,129},{129,193},{193,1... | collective-permute-start | bytes 516104 | tf_op jit(solution)/shard_map/ppermute | solution.py:312
  33.1 8.3 %collective-permute-start.5 = (bf16[96,896]{1,0:T(8,128)(2,1)S(1)}, bf16[96,896]{1,0:T(8,128)(2,1)S(1)}, u32[]{:S(2)}, u32[]{:S(2)}) collective-permute-start(bf16[96,896]{1,0:T(8,128)(2,1)S(1)} %get-tuple-element.89), channel_id=1, source_target_pairs={{0,128},{64,192},{128,0},{192,64},{1,129},{65,193},{129,1},{193,65... | collective-permute-start | bytes 516104 | tf_op jit(solution)/shard_map/ppermute | solution.py:312
  34.2 8.2 %collective-permute-start.6 = (bf16[96,896]{1,0:T(8,128)(2,1)S(1)}, bf16[96,896]{1,0:T(8,128)(2,1)S(1)}, u32[]{:S(2)}, u32[]{:S(2)}) collective-permute-start(bf16[96,896]{1,0:T(8,128)(2,1)S(1)} %get-tuple-element.90), channel_id=1, source_target_pairs={{0,192},{64,0},{128,64},{192,128},{1,193},{65,1},{129,65},{193,129... | collective-permute-start | bytes 516104 | tf_op jit(solution)/shard_map/ppermute | solution.py:312
  40.1 22.0 %copy-start.35 = (bf16[96,896]{1,0:T(8,128)(2,1)}, bf16[96,896]{1,0:T(8,128)(2,1)S(1)}, u32[]{:S(2)}) copy-start(bf16[96,896]{1,0:T(8,128)(2,1)S(1)} %collective-permute-done.4.refs_5_) | copy-start | bytes 516100
  41.4 20.7 %copy-start.37 = (bf16[96,896]{1,0:T(8,128)(2,1)}, bf16[96,896]{1,0:T(8,128)(2,1)S(1)}, u32[]{:S(2)}) copy-start(bf16[96,896]{1,0:T(8,128)(2,1)S(1)} %collective-permute-done.5.refs_10_) | copy-start | bytes 516100
  42.4 19.7 %copy-start.39 = (bf16[96,896]{1,0:T(8,128)(2,1)}, bf16[96,896]{1,0:T(8,128)(2,1)S(1)}, u32[]{:S(2)}) copy-start(bf16[96,896]{1,0:T(8,128)(2,1)S(1)} %collective-permute-done.6.refs_15_) | copy-start | bytes 516100
  43.5 21.3 %collective-permute-start.7 = (bf16[272,1024]{1,0:T(8,128)(2,1)S(1)}, bf16[272,1024]{1,0:T(8,128)(2,1)S(1)}, u32[]{:S(2)}, u32[]{:S(2)}) collective-permute-start(bf16[272,1024]{1,0:T(8,128)(2,1)S(1)} %collective-permute-done.2.refs_0_), channel_id=1, source_target_pairs={{0,8},{8,16},{16,24},{24,32},{32,40},{40,48},{48,56},{56,0},{1,9},... | collective-permute-start | bytes 1671176 | tf_op jit(solution)/shard_map/ppermute | solution.py:312
  43.5 21.3 %collective-permute-start.8 = (bf16[272,1024]{1,0:T(8,128)(2,1)S(1)}, bf16[272,1024]{1,0:T(8,128)(2,1)S(1)}, u32[]{:S(2)}, u32[]{:S(2)}) collective-permute-start(bf16[272,1024]{1,0:T(8,128)(2,1)S(1)} %collective-permute-done.3.refs_1_), channel_id=1, source_target_pairs={{0,56},{8,0},{16,8},{24,16},{32,24},{40,32},{48,40},{56,48},{1,57}... | collective-permute-start | bytes 1671176 | tf_op jit(solution)/shard_map/ppermute | solution.py:312
  46.7 15.4 %collective-permute-start.9 = (bf16[192,896]{1,0:T(8,128)(2,1)S(1)}, bf16[192,896]{1,0:T(8,128)(2,1)S(1)}, u32[]{:S(2)}, u32[]{:S(2)}) collective-permute-start(bf16[192,896]{1,0:T(8,128)(2,1)S(1)} %get-tuple-element.101), channel_id=1, source_target_pairs={{0,64},{64,128},{128,192},{192,0},{1,65},{65,129},{129,193},{193,1... | collective-permute-start | bytes 1032200 | tf_op jit(solution)/shard_map/ppermute | solution.py:312
  48.2 14.6 %collective-permute-start.10 = (bf16[192,896]{1,0:T(8,128)(2,1)S(1)}, bf16[192,896]{1,0:T(8,128)(2,1)S(1)}, u32[]{:S(2)}, u32[]{:S(2)}) collective-permute-start(bf16[192,896]{1,0:T(8,128)(2,1)S(1)} %get-tuple-element.102), channel_id=1, source_target_pairs={{0,128},{64,192},{128,0},{192,64},{1,129},{65,193},{129,1},{193,65... | collective-permute-start | bytes 1032200 | tf_op jit(solution)/shard_map/ppermute | solution.py:312
  49.3 14.7 %collective-permute-start.11 = (bf16[192,896]{1,0:T(8,128)(2,1)S(1)}, bf16[192,896]{1,0:T(8,128)(2,1)S(1)}, u32[]{:S(2)}, u32[]{:S(2)}) collective-permute-start(bf16[192,896]{1,0:T(8,128)(2,1)S(1)} %get-tuple-element.103), channel_id=1, source_target_pairs={{0,192},{64,0},{128,64},{192,128},{1,193},{65,1},{129,65},{193,129... | collective-permute-start | bytes 1032200 | tf_op jit(solution)/shard_map/ppermute | solution.py:312
  55.8 9.0 %copy-start.43 = (bf16[208,1024]{1,0:T(8,128)(2,1)}, bf16[208,1024]{1,0:T(8,128)(2,1)S(1)}, u32[]{:S(2)}) copy-start(bf16[208,1024]{1,0:T(8,128)(2,1)S(1)} %get-tuple-element.113) | copy-start | bytes 1277956
  55.8 9.0 %copy-start.44 = (bf16[208,1024]{1,0:T(8,128)(2,1)}, bf16[208,1024]{1,0:T(8,128)(2,1)S(1)}, u32[]{:S(2)}) copy-start(bf16[208,1024]{1,0:T(8,128)(2,1)S(1)} %get-tuple-element.112) | copy-start | bytes 1277956
  55.8 9.0 %copy-start.45 = (bf16[208,1024]{1,0:T(8,128)(2,1)}, bf16[208,1024]{1,0:T(8,128)(2,1)S(1)}, u32[]{:S(2)}) copy-start(bf16[208,1024]{1,0:T(8,128)(2,1)S(1)} %get-tuple-element.111) | copy-start | bytes 1277956
  65.6 48.6 %all-to-all-start.1 = ((f32[8,256,256]{2,1,0:T(8,128)}), f32[8,256,256]{2,1,0:T(8,128)S(1)}, u32[]{:S(2)}, u32[]{:S(2)}) async-start(f32[8,256,256]{2,1,0:T(8,128)} %inverse.1), calls=%async_computation.1 | async-start | bytes 4194304 | tf_op jit(solution)/shard_map/all_to_all | solution.py:396
  69.3 12.9 %collective-permute-start.14 = (bf16[208,1024]{1,0:T(8,128)(2,1)}, bf16[208,1024]{1,0:T(8,128)(2,1)S(1)}, u32[]{:S(2)}, u32[]{:S(2)}) collective-permute-start(bf16[208,1024]{1,0:T(8,128)(2,1)} %copy-done.45), channel_id=1, source_target_pairs={{0,64},{64,128},{128,192},{192,0},{1,65},{65,129},{129,193},{193,1... | collective-permute-start | bytes 1277960 | tf_op jit(solution)/shard_map/ppermute | solution.py:312
  70.6 21.1 %collective-permute-start.15 = (bf16[208,1024]{1,0:T(8,128)(2,1)}, bf16[208,1024]{1,0:T(8,128)(2,1)S(1)}, u32[]{:S(2)}, u32[]{:S(2)}) collective-permute-start(bf16[208,1024]{1,0:T(8,128)(2,1)} %copy-done.44), channel_id=1, source_target_pairs={{0,128},{64,192},{128,0},{192,64},{1,129},{65,193},{129,1},{193,65... | collective-permute-start | bytes 1277960 | tf_op jit(solution)/shard_map/ppermute | solution.py:312
  72.8 25.7 %collective-permute-start.12 = (bf16[272,1024]{1,0:T(8,128)(2,1)S(1)}, bf16[272,1024]{1,0:T(8,128)(2,1)S(1)}, u32[]{:S(2)}, u32[]{:S(2)}) collective-permute-start(bf16[272,1024]{1,0:T(8,128)(2,1)S(1)} %collective-permute-done.7.refs_0_), channel_id=1, source_target_pairs={{0,8},{8,16},{16,24},{24,32},{32,40},{40,48},{48,56},{56,0},{1,9},... | collective-permute-start | bytes 1671176 | tf_op jit(solution)/shard_map/ppermute | solution.py:312
  72.8 21.4 %collective-permute-start.16 = (bf16[208,1024]{1,0:T(8,128)(2,1)}, bf16[208,1024]{1,0:T(8,128)(2,1)S(1)}, u32[]{:S(2)}, u32[]{:S(2)}) collective-permute-start(bf16[208,1024]{1,0:T(8,128)(2,1)} %copy-done.43), channel_id=1, source_target_pairs={{0,192},{64,0},{128,64},{192,128},{1,193},{65,1},{129,65},{193,129... | collective-permute-start | bytes 1277960 | tf_op jit(solution)/shard_map/ppermute | solution.py:312
  73.7 1.1 copy-start.19
  74.9 1.1 copy-start.21
  79.4 34.2 %copy-start.6 = (bf16[192,1024]{1,0:T(8,128)(2,1)}, bf16[192,1024]{1,0:T(8,128)(2,1)S(1)}, u32[]{:S(2)}) copy-start(bf16[192,1024]{1,0:T(8,128)(2,1)S(1)} %get-tuple-element.130.refs_4_.refs_3_) | copy-start | bytes 1179652
  79.4 29.9 %collective-permute-start.21 = (bf16[192,1024]{1,0:T(8,128)(2,1)S(1)}, bf16[192,1024]{1,0:T(8,128)(2,1)S(1)}, u32[]{:S(2)}, u32[]{:S(2)}) collective-permute-start(bf16[192,1024]{1,0:T(8,128)(2,1)S(1)} %get-tuple-element.127), channel_id=1, source_target_pairs={{0,64},{64,128},{128,192},{192,0},{1,65},{65,129},{129,193},{193,1... | collective-permute-start | bytes 1179656 | tf_op jit(solution)/shard_map/ppermute | solution.py:312
  82.2 29.5 %collective-permute-start.22 = (bf16[192,1024]{1,0:T(8,128)(2,1)S(1)}, bf16[192,1024]{1,0:T(8,128)(2,1)S(1)}, u32[]{:S(2)}, u32[]{:S(2)}) collective-permute-start(bf16[192,1024]{1,0:T(8,128)(2,1)S(1)} %get-tuple-element.128), channel_id=1, source_target_pairs={{0,128},{64,192},{128,0},{192,64},{1,129},{65,193},{129,1},{193,65... | collective-permute-start | bytes 1179656 | tf_op jit(solution)/shard_map/ppermute | solution.py:312
  91.8 21.8 %copy-start.2 = (bf16[208,1024]{1,0:T(8,128)(2,1)}, bf16[208,1024]{1,0:T(8,128)(2,1)S(1)}, u32[]{:S(2)}) copy-start(bf16[208,1024]{1,0:T(8,128)(2,1)S(1)} %collective-permute-done.15.refs_2_.refs_12_) | copy-start | bytes 1277956
  91.8 21.7 %collective-permute-start.23 = (bf16[192,1024]{1,0:T(8,128)(2,1)S(1)}, bf16[192,1024]{1,0:T(8,128)(2,1)S(1)}, u32[]{:S(2)}, u32[]{:S(2)}) collective-permute-start(bf16[192,1024]{1,0:T(8,128)(2,1)S(1)} %get-tuple-element.129), channel_id=1, source_target_pairs={{0,192},{64,0},{128,64},{192,128},{1,193},{65,1},{129,65},{193,129... | collective-permute-start | bytes 1179656 | tf_op jit(solution)/shard_map/ppermute | solution.py:312
  94.2 19.4 %copy-start.4 = (bf16[208,1024]{1,0:T(8,128)(2,1)}, bf16[208,1024]{1,0:T(8,128)(2,1)S(1)}, u32[]{:S(2)}) copy-start(bf16[208,1024]{1,0:T(8,128)(2,1)S(1)} %collective-permute-done.16.refs_3_.refs_17_) | copy-start | bytes 1277956
  94.2 4.3 %collective-permute-start.13 = (bf16[256,128]{1,0:T(8,128)(2,1)S(1)}, bf16[256,128]{1,0:T(8,128)(2,1)S(1)}, u32[]{:S(2)}, u32[]{:S(2)}) collective-permute-start(bf16[256,128]{1,0:T(8,128)(2,1)S(1)} %slice.10), channel_id=1, source_target_pairs={{0,56},{8,0},{16,8},{24,16},{32,24},{40,32},{48,40},{56,48},{1,57}... | collective-permute-start | bytes 196616 | tf_op jit(solution)/shard_map/ppermute | solution.py:312
  98.5 5.6 %collective-permute-start.17 = (bf16[256,128]{1,0:T(8,128)(2,1)S(1)}, bf16[256,128]{1,0:T(8,128)(2,1)S(1)}, u32[]{:S(2)}, u32[]{:S(2)}) collective-permute-start(bf16[256,128]{1,0:T(8,128)(2,1)S(1)} %slice.11), channel_id=1, source_target_pairs={{0,8},{8,16},{16,24},{24,32},{32,40},{40,48},{48,56},{56,0},{1,9},... | collective-permute-start | bytes 196616 | tf_op jit(solution)/shard_map/ppermute | solution.py:312
  106.5 7.2 %copy-start.14 = (bf16[128,1024]{1,0:T(8,128)(2,1)}, bf16[128,1024]{1,0:T(8,128)(2,1)S(1)}, u32[]{:S(2)}) copy-start(bf16[128,1024]{1,0:T(8,128)(2,1)S(1)} %get-tuple-element.131.refs_0_.refs_4_) | copy-start | bytes 786436
  106.5 7.7 %copy-start.42 = (bf16[8,2,64]{2,1,0:T(2,128)(2,1)S(1)}, bf16[8,2,64]{2,1,0:T(2,128)(2,1)}, u32[]{:S(2)}) copy-start(bf16[8,2,64]{2,1,0:T(2,128)(2,1)} %codebook_ref.1) | copy-start | bytes 6148
  106.5 15.5 %collective-permute-start.18 = (bf16[128,1024]{1,0:T(8,128)(2,1)}, bf16[128,1024]{1,0:T(8,128)(2,1)}, u32[]{:S(2)}, u32[]{:S(2)}) collective-permute-start(bf16[128,1024]{1,0:T(8,128)(2,1)} %get-tuple-element.123), channel_id=1, source_target_pairs={{0,64},{64,128},{128,192},{192,0},{1,65},{65,129},{129,193},{193,1... | collective-permute-start | bytes 786440 | tf_op jit(solution)/shard_map/ppermute | solution.py:312
  107.6 14.4 %collective-permute-start.19 = (bf16[128,1024]{1,0:T(8,128)(2,1)}, bf16[128,1024]{1,0:T(8,128)(2,1)}, u32[]{:S(2)}, u32[]{:S(2)}) collective-permute-start(bf16[128,1024]{1,0:T(8,128)(2,1)} %get-tuple-element.124), channel_id=1, source_target_pairs={{0,128},{64,192},{128,0},{192,64},{1,129},{65,193},{129,1},{193,65... | collective-permute-start | bytes 786440 | tf_op jit(solution)/shard_map/ppermute | solution.py:312
  109.2 4.5 %copy-start.8 = (bf16[192,1024]{1,0:T(8,128)(2,1)}, bf16[192,1024]{1,0:T(8,128)(2,1)S(1)}, u32[]{:S(2)}) copy-start(bf16[192,1024]{1,0:T(8,128)(2,1)S(1)} %collective-permute-done.21.refs_5_.refs_8_) | copy-start | bytes 1179652
  109.2 12.8 %collective-permute-start.20 = (bf16[128,1024]{1,0:T(8,128)(2,1)}, bf16[128,1024]{1,0:T(8,128)(2,1)}, u32[]{:S(2)}, u32[]{:S(2)}) collective-permute-start(bf16[128,1024]{1,0:T(8,128)(2,1)} %get-tuple-element.125), channel_id=1, source_target_pairs={{0,192},{64,0},{128,64},{192,128},{1,193},{65,1},{129,65},{193,129... | collective-permute-start | bytes 786440 | tf_op jit(solution)/shard_map/ppermute | solution.py:312
  111.7 2.0 %copy-start.10 = (bf16[192,1024]{1,0:T(8,128)(2,1)}, bf16[192,1024]{1,0:T(8,128)(2,1)S(1)}, u32[]{:S(2)}) copy-start(bf16[192,1024]{1,0:T(8,128)(2,1)S(1)} %collective-permute-done.22.refs_6_.refs_13_) | copy-start | bytes 1179652
  113.6 9.7 %collective-permute-start.24 = (bf16[1920,128]{1,0:T(8,128)(2,1)S(1)}, bf16[1920,128]{1,0:T(8,128)(2,1)}, u32[]{:S(2)}, u32[]{:S(2)}) collective-permute-start(bf16[1920,128]{1,0:T(8,128)(2,1)S(1)} %window_half.2.refs_20_), channel_id=1, source_target_pairs={{0,1},{1,0},{2,3},{3,2},{4,5},{5,4},{6,7},{7,6},{8,9},{9,8},{10,11... | collective-permute-start | bytes 1474568 | tf_op jit(solution)/shard_map/ppermute | solution.py:312
  114.2 1.2 copy-start.16
  115.4 1.2 copy-start.17
  116.7 5.4 %copy-start.15 = (bf16[128,1024]{1,0:T(8,128)(2,1)S(1)}, bf16[128,1024]{1,0:T(8,128)(2,1)}, u32[]{:S(2)}) copy-start(bf16[128,1024]{1,0:T(8,128)(2,1)} %copy-done.14) | copy-start | bytes 786436
  116.7 8.2 %copy-start.3 = (bf16[208,1024]{1,0:T(8,128)(2,1)S(1)}, bf16[208,1024]{1,0:T(8,128)(2,1)}, u32[]{:S(2)}) copy-start(bf16[208,1024]{1,0:T(8,128)(2,1)} %copy-done.2) | copy-start | bytes 1277956
  116.7 8.2 %copy-start.5 = (bf16[208,1024]{1,0:T(8,128)(2,1)S(1)}, bf16[208,1024]{1,0:T(8,128)(2,1)}, u32[]{:S(2)}) copy-start(bf16[208,1024]{1,0:T(8,128)(2,1)} %copy-done.4) | copy-start | bytes 1277956
  116.7 8.2 %copy-start.7 = (bf16[192,1024]{1,0:T(8,128)(2,1)S(1)}, bf16[192,1024]{1,0:T(8,128)(2,1)}, u32[]{:S(2)}) copy-start(bf16[192,1024]{1,0:T(8,128)(2,1)} %copy-done.6) | copy-start | bytes 1179652
  116.7 8.2 %copy-start.9 = (bf16[192,1024]{1,0:T(8,128)(2,1)S(1)}, bf16[192,1024]{1,0:T(8,128)(2,1)}, u32[]{:S(2)}) copy-start(bf16[192,1024]{1,0:T(8,128)(2,1)} %copy-done.8) | copy-start | bytes 1179652
  116.7 8.2 %copy-start.11 = (bf16[192,1024]{1,0:T(8,128)(2,1)S(1)}, bf16[192,1024]{1,0:T(8,128)(2,1)}, u32[]{:S(2)}) copy-start(bf16[192,1024]{1,0:T(8,128)(2,1)} %copy-done.10) | copy-start | bytes 1179652
  116.7 8.2 %copy-start.13 = (bf16[192,1024]{1,0:T(8,128)(2,1)S(1)}, bf16[192,1024]{1,0:T(8,128)(2,1)}, u32[]{:S(2)}) copy-start(bf16[192,1024]{1,0:T(8,128)(2,1)} %copy-done.12) | copy-start | bytes 1179652
  116.7 8.2 %copy-start.23 = (bf16[192,896]{1,0:T(8,128)(2,1)S(1)}, bf16[192,896]{1,0:T(8,128)(2,1)}, u32[]{:S(2)}) copy-start(bf16[192,896]{1,0:T(8,128)(2,1)} %copy-done.22) | copy-start | bytes 1032196
  116.7 8.2 %copy-start.25 = (bf16[192,896]{1,0:T(8,128)(2,1)S(1)}, bf16[192,896]{1,0:T(8,128)(2,1)}, u32[]{:S(2)}) copy-start(bf16[192,896]{1,0:T(8,128)(2,1)} %copy-done.24) | copy-start | bytes 1032196
  116.7 8.2 %copy-start.27 = (bf16[192,896]{1,0:T(8,128)(2,1)S(1)}, bf16[192,896]{1,0:T(8,128)(2,1)}, u32[]{:S(2)}) copy-start(bf16[192,896]{1,0:T(8,128)(2,1)} %copy-done.26) | copy-start | bytes 1032196
  116.7 8.2 %copy-start.29 = (bf16[192,896]{1,0:T(8,128)(2,1)S(1)}, bf16[192,896]{1,0:T(8,128)(2,1)}, u32[]{:S(2)}) copy-start(bf16[192,896]{1,0:T(8,128)(2,1)} %copy-done.28) | copy-start | bytes 1032196
  116.7 8.2 %copy-start.34 = (bf16[96,896]{1,0:T(8,128)(2,1)S(1)}, bf16[96,896]{1,0:T(8,128)(2,1)}, u32[]{:S(2)}) copy-start(bf16[96,896]{1,0:T(8,128)(2,1)} %copy-done.33) | copy-start | bytes 516100
  116.7 8.2 %copy-start.36 = (bf16[96,896]{1,0:T(8,128)(2,1)S(1)}, bf16[96,896]{1,0:T(8,128)(2,1)}, u32[]{:S(2)}) copy-start(bf16[96,896]{1,0:T(8,128)(2,1)} %copy-done.35) | copy-start | bytes 516100
  116.8 8.2 %copy-start.38 = (bf16[96,896]{1,0:T(8,128)(2,1)S(1)}, bf16[96,896]{1,0:T(8,128)(2,1)}, u32[]{:S(2)}) copy-start(bf16[96,896]{1,0:T(8,128)(2,1)} %copy-done.37) | copy-start | bytes 516100
  116.8 8.2 %copy-start.40 = (bf16[96,896]{1,0:T(8,128)(2,1)S(1)}, bf16[96,896]{1,0:T(8,128)(2,1)}, u32[]{:S(2)}) copy-start(bf16[96,896]{1,0:T(8,128)(2,1)} %copy-done.39) | copy-start | bytes 516100
  123.2 1.7 %collective-permute-start.25 = (bf16[1152,128]{1,0:T(8,128)(2,1)S(1)}, bf16[1152,128]{1,0:T(8,128)(2,1)S(1)}, u32[]{:S(2)}, u32[]{:S(2)}) collective-permute-start(bf16[1152,128]{1,0:T(8,128)(2,1)S(1)} %window_half.3.refs_22_), channel_id=1, source_target_pairs={{0,1},{1,0},{2,3},{3,2},{4,5},{5,4},{6,7},{7,6},{8,9},{9,8},{10,11... | collective-permute-start | bytes 884744 | tf_op jit(solution)/shard_map/ppermute | solution.py:312
  (10 other events, 7.5 us)

commit v3 on v2

--- a/solution.py
+++ b/solution.py
@@ -18,7 +18,6 @@
 CHUNKS = (1, 2, 2, 2, 1)
 PAIR = 4 * CAP
 LAST = EXP_DEV * CAP
-FOLD = 6
 F32 = jnp.float32
 BF16 = jnp.bfloat16
 
@@ -55,11 +54,33 @@
     out_ref[TOK:ROWS, 0:TOK] = routing_rows(routing_ref[...])
 
 
-def join_kernel(forward_ref, backward_ref, edge_ref, *outs):
-    for block, out in zip((forward_ref, backward_ref), outs):
+def join_kernel(*refs):
+    count = len(refs) // 3
+    for block, edge, out in zip(refs[:count], refs[count:2 * count], refs[2 * count:]):
         out[:, 0:FEAT] = block[...]
-        out[0:TOK, FEAT:WIDE] = edge_ref[...]
+        out[0:TOK, FEAT:WIDE] = edge[...]
         out[TOK:ROWS, FEAT:WIDE] = jnp.zeros((16, LANES), BF16)
+
+
+def join(blocks, edges):
+    count = len(blocks)
+    return list(pl.pallas_call(
+        join_kernel,
+        out_shape=[jax.ShapeDtypeStruct((ROWS, WIDE), BF16)] * count,
+        in_specs=[vmem()] * (2 * count),
+        out_specs=[vmem()] * count,
+        compiler_params=params(8),
+        cost_estimate=cost(0.3 * count),
+        name="join_%d" % count,
+    )(*blocks, *edges))
+
+
+def gather_kernel(*refs):
+    begin = 0
+    for ref in refs[:-1]:
+        rows = ref.shape[0] // PAIR * PAIR
+        refs[-1][begin:begin + rows, :] = ref[0:rows, FEAT:WIDE]
+        begin += rows
 
 
 def ranks(listed, x_index, z_index):
@@ -95,80 +116,42 @@
     return jnp.where(wide == want, 1.0, 0.0).astype(BF16)
 
 
-def fold(rows, out, k, begin):
-    for part in range(rows.shape[0] // 16):
-        line, lane = begin + part // FOLD * 16, part % FOLD * LANES
-        out[line:line + 16, lane:lane + LANES] = rows[part * 16:part * 16 + 16, :]
-
-
-def choose(select_ref, values, size):
+def pack_kernel(count, last, place_ref, before_ref, *refs):
+    blocks, counts_ref, outs = refs[:count], refs[count], refs[count + 1:]
+    size = count * EXP_DEV * CAP
+    counts = before_ref[...]
     total = None
-    for spot, value in enumerate(values):
-        picked = jnp.dot(select_ref[spot], value, preferred_element_type=F32)
-        total = picked if total is None else total + picked
-    total = total.astype(BF16)
-    return [total[k * size:(k + 1) * size, :] for k in range(NX)]
-
-
-def pack_kernel(chunk, place_ref, before_ref, *refs):
-    count = CHUNKS[chunk]
-    size = count * LAST
-    blocks, refs = refs[:count], refs[count:]
-    counts_ref, select_ref, outs = refs[-NX - 2], refs[-NX - 1], refs[-NX:]
-    extra = refs[:-NX - 2]
-    counts = before_ref[...]
     for spot, block in enumerate(blocks):
         listed = block[TOK:ROWS, 0:TOK].astype(F32)
         member, rank = ranks(listed, place_ref[0], place_ref[1])
         counts = counts + jnp.sum(member, axis=1, keepdims=True)
-        select_ref[spot] = selectors(rank, count, spot)
+        picked = jnp.dot(
+            selectors(rank, count, spot), block[0:TOK, :], preferred_element_type=F32
+        )
+        total = picked if total is None else total + picked
     counts_ref[...] = counts
-    features = choose(select_ref, [block[0:TOK, 0:FEAT] for block in blocks], size)
     for k, out in enumerate(outs):
-        out[0:size, 0:FEAT] = features[k]
-    if chunk == 2:
-        older_ref, old_ref, edge_ref = extra
-        near = choose(old_ref, [block[0:TOK, FEAT:WIDE] for block in blocks], 2 * LAST)
-        own = choose(older_ref, [edge_ref[...]], LAST)
-        for k, out in enumerate(outs):
-            out[0:size, FEAT:WIDE] = near[k]
-            fold(own[k], out, k, size)
-    elif chunk == 3:
-        old_ref, = extra
-        near = choose(old_ref, [block[0:TOK, FEAT:WIDE] for block in blocks], 2 * LAST)
-        for k, out in enumerate(outs):
-            out[0:size, FEAT:WIDE] = near[k]
-    elif chunk == 4:
-        old_ref, back_ref, end_ref = extra
-        near = choose(old_ref, [blocks[0][0:TOK, FEAT:WIDE], back_ref[...]], 2 * LAST)
-        end = choose(select_ref, [end_ref[...]], LAST)
-        for k, out in enumerate(outs):
-            out[0:size, FEAT:WIDE] = end[k]
-            fold(near[k], out, k, size)
-            mine = counts[k * EXP_DEV:(k + 1) * EXP_DEV, :]
-            out[size:size + 16, FOLD * LANES:FEAT] = jnp.concatenate([mine, mine], axis=0).astype(BF16)
-
-
-SHAPES = ((LAST, FEAT), (2 * LAST, FEAT), (2 * LAST + 16, WIDE), (2 * LAST, WIDE), (LAST + 32, WIDE))
-
-
-def pack(chunk, place, before, blocks, *extra):
+        out[0:size, :] = total[k * size:(k + 1) * size, :].astype(BF16)
+        if last:
+            mine = counts[k * EXP_DEV:(k + 1) * EXP_DEV, 0:1]
+            mine = jnp.broadcast_to(jnp.concatenate([mine, mine], axis=0), (16, WIDE))
+            out[size:size + 16, :] = mine.astype(BF16)
+
+
+def pack(place, before, blocks, last):
     count = len(blocks)
-    size = count * LAST
-    counts, select, *packed = pl.pallas_call(
-        functools.partial(pack_kernel, chunk),
-        out_shape=[
-            jax.ShapeDtypeStruct((NX * EXP_DEV, LANES), F32),
-            jax.ShapeDtypeStruct((count, NX * size, TOK), BF16),
-        ]
-        + [jax.ShapeDtypeStruct(SHAPES[chunk], BF16)] * NX,
-        in_specs=[smem()] + [vmem()] * (1 + count + len(extra)),
-        out_specs=[vmem()] * (2 + NX),
-        compiler_params=params(16),
+    size = count * EXP_DEV * CAP + (16 if last else 0)
+    counts, *packed = pl.pallas_call(
+        functools.partial(pack_kernel, count, last),
+        out_shape=[jax.ShapeDtypeStruct((NX * EXP_DEV, LANES), F32)]
+        + [jax.ShapeDtypeStruct((size, WIDE), BF16)] * NX,
+        in_specs=[smem()] + [vmem()] * (1 + count),
+        out_specs=[vmem()] * (1 + NX),
+        compiler_params=params(8),
         cost_estimate=cost(1 + count),
-        name="pack_%d" % chunk,
-    )(place, before, *blocks, *extra)
-    return counts, select, packed
+        name="pack_%d" % count,
+    )(place, before, *blocks)
+    return counts, packed
 
 
 def dot(left, right):
@@ -232,9 +215,11 @@
     out_ref[0] = total + jnp.dot(residual_high, inverse_high, preferred_element_type=F32)
 
 
-def hessian_kernel(place_ref, *refs):
-    pieces = NX * len(CHUNKS)
-    messages, windows_of, out_ref = refs[:pieces], refs[pieces:-1], refs[-1]
+def hessian_kernel(chunks, place_ref, *refs):
+    last = 4 in chunks
+    pieces = NX * len(chunks)
+    messages, others, out_ref = refs[:pieces], refs[pieces:2 * pieces], refs[-1]
+    counted = refs[2 * pieces:2 * pieces + NX]
     pair = pl.program_id(0)
     first = place_ref[2] == 0
     row = lax.broadcasted_iota(jnp.int32, (PAIR, TOK), 0)
@@ -242,14 +227,12 @@
     double = (row % (2 * CAP)) // CAP
     features, windows = [], []
     for k in range(NX):
-        for c, count in enumerate(CHUNKS):
-            step = pair // (3 - count)
-            where = pl.ds(pl.multiple_of(step * PAIR, 16), PAIR)
-            features.append(messages[k * len(CHUNKS) + c][where, 0:FEAT])
-            mine_ref, other_ref = windows_of[0:2] if c < 3 else windows_of[2:4]
-            begin = WINDOW_ROWS[c] + k * count * LAST
-            where = pl.ds(pl.multiple_of(begin + step * PAIR, 16), PAIR)
-            near, far = mine_ref[where, :].astype(F32), other_ref[where, :].astype(F32)
+        for c, chunk in enumerate(chunks):
+            count = CHUNKS[chunk]
+            ref = messages[k * len(chunks) + c]
+            features.append(ref[:, 0:FEAT])
+            near = ref[:, FEAT:WIDE].astype(F32)
+            far = others[k * len(chunks) + c][...].astype(F32)
             both = jnp.concatenate(
                 [jnp.where(first, near, far), jnp.where(first, far, near)], axis=1
             )
@@ -265,49 +248,57 @@
         (((0,), (0,)), ((), ())),
         preferred_element_type=F32,
     )
-    counts = jnp.zeros((16, LANES), F32)
-    for k in range(NX):
-        ref = messages[k * len(CHUNKS) + 4]
-        counts = counts + ref[LAST:LAST + 16, FOLD * LANES:FEAT].astype(F32)
+    if not last:
+        for e in range(2):
+            out_ref[e] = product[:, e * TOK:(e + 1) * TOK]
+        return
+    counts = counted[0][...].astype(F32)
+    for ref in counted[1:]:
+        counts = counts + ref[...].astype(F32)
     line = lax.broadcasted_iota(jnp.int32, counts.shape, 0)
     for e in range(2):
         count = jnp.sum(jnp.where(line == 2 * pair + e, counts, 0.0), axis=0, keepdims=True)
-        scale = 2.0 / count
-        scale = jnp.concatenate([scale, scale], axis=1)
-        out_ref[e] = product[:, e * TOK:(e + 1) * TOK] * scale
-
-
-WINDOW_ROWS = (0, 4 * LAST, 12 * LAST, 0, 8 * LAST)
-
-
-def unfold(ref, out_ref, source, begin, rows):
-    for part in range(rows // 16):
-        line, lane = source + part // FOLD * 16, part % FOLD * LANES
-        out_ref[begin + part * 16:begin + part * 16 + 16, :] = ref[line:line + 16, lane:lane + LANES]
-
-
-def early_kernel(*refs):
-    second, third, out_ref = refs[0:NX], refs[NX:2 * NX], refs[-1]
-    for k in range(NX):
-        unfold(second[k], out_ref, 2 * LAST, WINDOW_ROWS[0] + k * LAST, LAST)
-        begin = WINDOW_ROWS[1] + k * 2 * LAST
-        out_ref[begin:begin + 2 * LAST, :] = second[k][0:2 * LAST, FEAT:WIDE]
-        begin = WINDOW_ROWS[2] + k * 2 * LAST
-        out_ref[begin:begin + 2 * LAST, :] = third[k][:, FEAT:WIDE]
-
-
-def late_kernel(*refs):
-    last, out_ref = refs[0:NX], refs[-1]
-    for k in range(NX):
-        unfold(last[k], out_ref, LAST, WINDOW_ROWS[3] + k * 2 * LAST, 2 * LAST)
-        begin = WINDOW_ROWS[4] + k * LAST
-        out_ref[begin:begin + LAST, :] = last[k][0:LAST, FEAT:WIDE]
+        out_ref[e] = (product[:, e * TOK:(e + 1) * TOK] + refs[-2][e]) * (2.0 / count)
 
 
 def shifted(size, step):
     return [(i, (i + step) % size) for i in range(size)]
 
 
+def hessian_part(place, sent, group, chunks, before):
+    operands, specs, other_specs = [], [], []
+    begins, begin = {}, 0
+    for c in chunks:
+        for k in range(NX):
+            begins[k, c] = begin
+            begin += CHUNKS[c] * LAST
+    for k in range(NX):
+        for c in chunks:
+            share = 2 // CHUNKS[c]
+            operands.append(sent[c][k])
+            specs.append(pl.BlockSpec((PAIR, WIDE), lambda p, s=share: (p // s, 0)))
+            other_specs.append(
+                pl.BlockSpec((PAIR, LANES), lambda p, s=share, b=begins[k, c] // PAIR: (b + p // s, 0))
+            )
+    pieces = len(operands)
+    operands += [group] * pieces
+    specs += other_specs
+    block = pl.BlockSpec((2, FEAT, TOK), lambda p: (p, 0, 0))
+    if before is not None:
+        operands += [*sent[4], before]
+        specs += [pl.BlockSpec((16, TOK), lambda p: (LAST // 16, 0))] * NX + [block]
+    return pl.pallas_call(
+        functools.partial(hessian_kernel, chunks),
+        grid=(EXP_DEV // 2,),
+        out_shape=jax.ShapeDtypeStruct((EXP_DEV, FEAT, TOK), F32),
+        in_specs=[smem()] + specs,
+        out_specs=block,
+        compiler_params=params(24),
+        cost_estimate=cost(5),
+        name="hessian_%d" % len(chunks),
+    )(place, *operands)
+
+
 def move(value, axis, size, step):
     return lax.ppermute(value, axis, shifted(size, step))
 
@@ -320,9 +311,11 @@
     return [packed[0]] + [move(packed[k], "x", NX, k) for k in (1, 2, 3)]
 
 
-def swap(kernel, rows, values):
-    mine = pl.pallas_call(
-        kernel,
+def swap(chunks):
+    values = [value for chunk in chunks for value in chunk]
+    rows = sum(value.shape[0] // PAIR * PAIR for value in values)
+    held = pl.pallas_call(
+        gather_kernel,
         out_shape=jax.ShapeDtypeStruct((rows, LANES), BF16),
         in_specs=[vmem()] * len(values),
         out_specs=vmem(),
@@ -330,7 +323,7 @@
         cost_estimate=cost(0.5),
         name="window_half",
     )(*values)
-    return mine, move(mine, "core", NC, 1)
+    return move(held, "core", NC, 1)
 
 
 def local(tokens, routing, weights, indices, codebook, hinv_panel):
@@ -358,28 +351,21 @@
         name="halves",
     )(tokens)
     edge = lax.all_to_all(halves, ("y", "core"), 0, 0, tiled=True)[0]
-    counts, select0, packed = pack(
-        0, place, jnp.zeros((NX * EXP_DEV, LANES), F32), [payload]
+    edge_f, edge_b = move(edge, "z", NZ, 1), move(edge, "z", NZ, -1)
+    counts, packed = pack(
+        place, jnp.zeros((NX * EXP_DEV, LANES), F32), join([payload], [edge]), False
     )
 
-    f1, b1, counts, edge, *packed = tie(f1, b1, counts, edge, *packed)
-    joined_f, joined_b = pl.pallas_call(
-        join_kernel,
-        out_shape=[jax.ShapeDtypeStruct((ROWS, WIDE), BF16)] * 2,
-        in_specs=[vmem()] * 3,
-        out_specs=[vmem()] * 2,
-        compiler_params=params(8),
-        cost_estimate=cost(0.6),
-        name="join",
-    )(f1, b1, edge)
-    f2, b2 = move(joined_f, "z", NZ, 1), move(joined_b, "z", NZ, -1)
+    f1, b1, edge_f, edge_b, counts, *packed = tie(f1, b1, edge_f, edge_b, counts, *packed)
+    f1, b1 = join([f1, b1], [edge_f, edge_b])
+    f2, b2 = move(f1, "z", NZ, 1), move(b1, "z", NZ, -1)
     sent = [send(packed)]
-    counts, select1, packed = pack(1, place, counts, [f1, b1])
+    counts, packed = pack(place, counts, [f1, b1], False)
     sent.append(send(packed))
 
     f2, b2, counts, *sent[0] = tie(f2, b2, counts, *sent[0])
     f3, b3 = move(f2, "z", NZ, 1), move(b2, "z", NZ, -1)
-    counts, select2, packed = pack(2, place, counts, [f2, b2], select0, select1, edge)
+    counts, packed = pack(place, counts, [f2, b2], False)
     sent.append(send(packed))
     hinv_panel, counts = tie(hinv_panel, counts)
     inverse = pl.pallas_call(
@@ -395,16 +381,14 @@
     f3, b3, counts, inverse, *sent[1] = tie(f3, b3, counts, inverse, *sent[1])
     inverses = lax.all_to_all(inverse, ("y", "core"), 0, 0, tiled=True)
     f4 = move(f3, "z", NZ, 1)
-    back = move(b3[0:TOK, FEAT:WIDE], "z", NZ, -1)
-    counts, select3, packed = pack(3, place, counts, [f3, b3], select2)
+    early = swap(sent[0:2])
+    counts, packed = pack(place, counts, [f3, b3], False)
     sent.append(send(packed))
 
-    f4, back, counts, *sent[2] = tie(f4, back, counts, *sent[2])
-    end = move(f4[0:TOK, FEAT:WIDE], "z", NZ, 1)
-    counts, _, packed = pack(4, place, counts, [f4], select3, back, end)
+    f4, counts, early, *sent[2] = tie(f4, counts, early, *sent[2])
+    counts, packed = pack(place, counts, [f4], True)
     weights, packed[0] = tie(weights, packed[0])
     sent.append(send(packed))
-    early = swap(early_kernel, 20 * LAST, [*sent[2], *sent[3]])
     experts, rows, width = weights.shape
     pairs = indices.shape[2]
     errors = pl.pallas_call(
@@ -423,21 +407,12 @@
         name="errors",
     )(weights, indices, codebook, inverses)
 
-    errors, *rest = tie(errors, *sent[4], *sent[3])
-    sent[4], sent[3] = rest[:NX], rest[NX:]
-    late = swap(late_kernel, 12 * LAST, sent[4])
-    operands = [sent[c][k] for k in range(NX) for c in range(len(CHUNKS))]
-    operands += [*early, *late]
-    hessian = pl.pallas_call(
-        hessian_kernel,
-        grid=(EXP_DEV // 2,),
-        out_shape=jax.ShapeDtypeStruct((EXP_DEV, FEAT, TOK), F32),
-        in_specs=[smem()] + [vmem()] * len(operands),
-        out_specs=pl.BlockSpec((2, FEAT, TOK), lambda p: (p, 0, 0)),
-        compiler_params=params(20),
-        cost_estimate=cost(7.5),
-        name="hessian",
-    )(place, *operands)
+    errors, place = tie(errors, place)
+    hessian = hessian_part(place, sent, early, (0, 1), None)
+    hessian, *rest = tie(hessian, *sent[3], *sent[4])
+    sent[3], sent[4] = rest[:NX], rest[NX:]
+    late = swap(sent[2:5])
+    hessian = hessian_part(place, sent, late, (2, 3, 4), hessian)
     return hessian, errors
 
 

time: 134 us -> 135 us (level)
  local copies, waits for them, and re-layouts: 13.9 us -> 18.9 us
  starting transfers between devices: 54.5 us -> 49.9 us
  waiting for transfers between devices: 28.2 us -> 25.3 us
  Pallas kernels: 34.6 us -> 37.2 us
    unnamed x92 -> x84, local copies, waits for them, and re-layouts: 12.9 us -> 18.9 us
    ppermute x26, waiting for transfers between devices: 27.1 us -> 21.7 us  [move(): return lax.ppermute(value, axis, shifted(size, step))]
    ppermute x26, starting transfers between devices: 46.4 us -> 41.6 us  [move(): return lax.ppermute(value, axis, shifted(size, step))]
    all_to_all x1, waiting for transfers between devices: 1.07 us -> 3.67 us  [local(): edge = lax.all_to_all(halves, ('y', 'core'), 0, 0, tiled=True)[0]]
    pallas_call x9 -> x11, Pallas kernels: 22.2 us -> 24.7 us  [the longest x5 13.4 us: pack(): pl.pallas_call(functools.partial(pack_kernel, count, last), out_shape=[ja...]
  transfers between devices with their start and end apart: 28 -> 28, of which waited for: 13 -> 11; matrix products, arithmetic and copies ran while one was open for 1% -> 0% of each run, Pallas kernels for 20% -> 22%
where the time goes in v3:
time: 135 us; the launch traced here: 132 us
  starting transfers between devices  49.9 us (37%)
  Pallas kernels  37.2 us (28%)
  waiting for transfers between devices  25.3 us (19%)
  local copies, waits for them, and re-layouts  18.9 us (14%)
    ppermute x26, starting transfers between devices, move(): return lax.ppermute(value, axis, shifted(size, step))  41.6 us
    ppermute x26, waiting for transfers between devices, move(): return lax.ppermute(value, axis, shifted(size, step))  21.7 us
    unnamed x84, local copies, waits for them, and re-layouts  18.9 us
    pallas_call x5, Pallas kernels, pack(): pl.pallas_call(functools.partial(pack_kernel, count, last), out_shape=[ja...  13.4 us
    pallas_call x2, Pallas kernels, hessian_part(): pl.pallas_call(functools.partial(hessian_kernel, chunks), grid=(EXP_DEV /...  9.88 us
    pallas_call x1, Pallas kernels, local(): pl.pallas_call(inverse_kernel, out_shape=jax.ShapeDtypeStruct((NY * NC, T...  6.32 us
    pallas_call x1, Pallas kernels, local(): pl.pallas_call(errors_kernel, grid=(experts,), out_shape=jax.ShapeDtypeSt...  5.25 us
    all_to_all x1, starting transfers between devices, local(): edge = lax.all_to_all(halves, ('y', 'core'), 0, 0, tiled=True)[0]  4.47 us
  transfers between devices with their start and end apart: 28, of which 11 were waited for; matrix products, arithmetic and copies ran while one was open for 0% of the time, Pallas kernels for 22%

profile of v3, /device:TPU:2, one launch (start us, length us, event | category | flops | bytes accessed | tf_op | source)
XLA Modules:
  0.0 132.4 jit_solution(5088200601882400029)
XLA Ops:
  0.6 1.0 copy-done
  1.7 0.9 halves.1
  2.5 4.5 %all-to-all-start = ((bf16[8,256,128]{2,1,0:T(8,128)(2,1)}), bf16[8,256,128]{2,1,0:T(8,128)(2,1)S(1)}, u32[]{:S(2)}, u32[]{:S(2)}) async-start(bf16[8,256,128]{2,1,0:T(8,128)(2,1)} %halves.1), calls=%async_computation | async-start | bytes 1048576 | tf_op jit(solution)/shard_map/all_to_all | solution.py:353
  7.0 0.7 copy-done.37
  7.7 5.9 %collective-permute-start.1 = (bf16[272,896]{1,0:T(8,128)(2,1)S(1)}, bf16[272,896]{1,0:T(8,128)(2,1)S(1)}, u32[]{:S(2)}, u32[]{:S(2)}) collective-permute-start(bf16[272,896]{1,0:T(8,128)(2,1)S(1)} %payload.1.refs_0_), channel_id=1, source_target_pairs={{0,56},{8,0},{16,8},{24,16},{32,24},{40,32},{48,40},{56,48},{1,57}... | collective-permute-start | bytes 1462280 | tf_op jit(solution)/shard_map/ppermute | solution.py:303
  13.7 3.7 %all-to-all-done = bf16[8,256,128]{2,1,0:T(8,128)(2,1)S(1)} async-done(((bf16[8,256,128]{2,1,0:T(8,128)(2,1)}), bf16[8,256,128]{2,1,0:T(8,128)(2,1)S(1)}, u32[]{:S(2)}, u32[]{:S(2)}) %all-to-all-start) | async-done | bytes 524320 | tf_op jit(solution)/shard_map/all_to_all | solution.py:353
  17.3 5.9 %collective-permute-start.3 = (bf16[256,128]{1,0:T(8,128)(2,1)S(1)}, bf16[256,128]{1,0:T(8,128)(2,1)S(1)}, u32[]{:S(2)}, u32[]{:S(2)}) collective-permute-start(bf16[256,128]{1,0:T(8,128)(2,1)S(1)} %slice_bitcast_fusion.refs_1_), channel_id=1, source_target_pairs={{0,56},{8,0},{16,8},{24,16},{32,24},{40,32},{48,40},{56,48},{1,57}... | collective-permute-start | bytes 196616 | tf_op jit(solution)/shard_map/ppermute | solution.py:303
  23.4 1.2 pack_1.2
  24.6 0.5 collective-permute-done.1.refs_1_
  25.1 3.7 %collective-permute-done.refs_0_ = bf16[272,896]{1,0:T(8,128)(2,1)S(1)} collective-permute-done((bf16[272,896]{1,0:T(8,128)(2,1)S(1)}, bf16[272,896]{1,0:T(8,128)(2,1)S(1)}, u32[]{:S(2)}, u32[]{:S(2)}) %collective-permute-start) | collective-permute-done | bytes 487456 | tf_op jit(solution)/shard_map/ppermute | solution.py:303
  28.8 0.7 collective-permute-done.2.refs_2_
  29.7 3.2 %collective-permute-start.5 = (bf16[272,1024]{1,0:T(8,128)(2,1)S(1)}, bf16[272,1024]{1,0:T(8,128)(2,1)S(1)}, u32[]{:S(2)}, u32[]{:S(2)}) collective-permute-start(bf16[272,1024]{1,0:T(8,128)(2,1)S(1)} %get-tuple-element.84.refs_1_), channel_id=1, source_target_pairs={{0,56},{8,0},{16,8},{24,16},{32,24},{40,32},{48,40},{56,48},{1,57}... | collective-permute-start | bytes 1671176 | tf_op jit(solution)/shard_map/ppermute | solution.py:303
  33.0 1.5 %collective-permute-start.6 = (bf16[96,1024]{1,0:T(8,128)(2,1)S(1)}, bf16[96,1024]{1,0:T(8,128)(2,1)S(1)}, u32[]{:S(2)}, u32[]{:S(2)}) collective-permute-start(bf16[96,1024]{1,0:T(8,128)(2,1)S(1)} %get-tuple-element.88), channel_id=1, source_target_pairs={{0,64},{64,128},{128,192},{192,0},{1,65},{65,129},{129,193},{193,1... | collective-permute-start | bytes 589832 | tf_op jit(solution)/shard_map/ppermute | solution.py:303
  34.5 1.1 collective-permute-start.7
  35.6 2.2 %collective-permute-start.8 = (bf16[96,1024]{1,0:T(8,128)(2,1)S(1)}, bf16[96,1024]{1,0:T(8,128)(2,1)S(1)}, u32[]{:S(2)}, u32[]{:S(2)}) collective-permute-start(bf16[96,1024]{1,0:T(8,128)(2,1)S(1)} %get-tuple-element.90), channel_id=1, source_target_pairs={{0,192},{64,0},{128,64},{192,128},{1,193},{65,1},{129,65},{193,129... | collective-permute-start | bytes 589832 | tf_op jit(solution)/shard_map/ppermute | solution.py:303
  37.7 2.9 %pack_2.3 = (f32[32,128]{1,0:T(8,128)S(1)}, bf16[192,1024]{1,0:T(8,128)(2,1)S(1)}, bf16[192,1024]{1,0:T(8,128)(2,1)S(1)}, bf16[192,1024]{1,0:T(8,128)(2,1)S(1)}, bf16[192,1024]{1,0:T(8,128)(2,1)S(1)}) custom-call(s32[3]{0:T(128)S(1)} %pad_add_fusion.place_ref, f32[32,128]{1,0:T(8,128)S(1)} %get-tuple-element.85.before_ref, ...), custom_call_target="tpu_custom_call" | custom-call | bytes 11070000 | tf_op jit(solution)/shard_map/pack_2/pallas_call | solution.py:144
  40.7 2.8 %collective-permute-done.7.refs_2_.refs_4_ = bf16[96,1024]{1,0:T(8,128)(2,1)S(1)} collective-permute-done((bf16[96,1024]{1,0:T(8,128)(2,1)S(1)}, bf16[96,1024]{1,0:T(8,128)(2,1)S(1)}, u32[]{:S(2)}, u32[]{:S(2)}) %collective-permute-start.7) | collective-permute-done | bytes 196640 | tf_op jit(solution)/shard_map/ppermute | solution.py:303
  43.5 0.7 copy-done.28
  44.2 0.7 collective-permute-done.8.refs_3_.refs_6_
  44.9 0.7 copy-done.31
  45.6 3.2 %collective-permute-start.10 = (bf16[272,1024]{1,0:T(8,128)(2,1)S(1)}, bf16[272,1024]{1,0:T(8,128)(2,1)S(1)}, u32[]{:S(2)}, u32[]{:S(2)}) collective-permute-start(bf16[272,1024]{1,0:T(8,128)(2,1)S(1)} %collective-permute-done.5.refs_1_), channel_id=1, source_target_pairs={{0,56},{8,0},{16,8},{24,16},{32,24},{40,32},{48,40},{56,48},{1,57}... | collective-permute-start | bytes 1671176 | tf_op jit(solution)/shard_map/ppermute | solution.py:303
  48.8 1.3 collective-permute-start.11
  50.1 2.2 %collective-permute-start.12 = (bf16[192,1024]{1,0:T(8,128)(2,1)S(1)}, bf16[192,1024]{1,0:T(8,128)(2,1)S(1)}, u32[]{:S(2)}, u32[]{:S(2)}) collective-permute-start(bf16[192,1024]{1,0:T(8,128)(2,1)S(1)} %get-tuple-element.99), channel_id=1, source_target_pairs={{0,128},{64,192},{128,0},{192,64},{1,129},{65,193},{129,1},{193,65... | collective-permute-start | bytes 1179656 | tf_op jit(solution)/shard_map/ppermute | solution.py:303
  52.3 1.0 collective-permute-start.13
  53.2 2.9 %pack_2.4 = (f32[32,128]{1,0:T(8,128)S(1)}, bf16[192,1024]{1,0:T(8,128)(2,1)S(1)}, bf16[192,1024]{1,0:T(8,128)(2,1)S(1)}, bf16[192,1024]{1,0:T(8,128)(2,1)S(1)}, bf16[192,1024]{1,0:T(8,128)(2,1)S(1)}) custom-call(s32[3]{0:T(128)S(1)} %pad_add_fusion.place_ref, f32[32,128]{1,0:T(8,128)S(1)} %get-tuple-element.93.before_ref, ...), custom_call_target="tpu_custom_call" | custom-call | bytes 11070000 | tf_op jit(solution)/shard_map/pack_2/pallas_call | solution.py:144
  56.2 0.8 copy-done.12
  56.9 0.8 copy-done.39
  57.7 0.8 copy-done.40
  58.4 0.8 copy-done.41
  59.2 6.3 %inverse.1 = f32[8,256,256]{2,1,0:T(8,128)} custom-call(f32[1,256,256]{2,1,0:T(8,128)S(1)} %copy-done.36), custom_call_target="tpu_custom_call" | custom-call | bytes 27675000 | tf_op jit(solution)/shard_map/inverse/pallas_call | solution.py:371
  65.5 0.8 copy-done.6
  66.3 1.9 %collective-permute-done.13.refs_7_ = bf16[192,1024]{1,0:T(8,128)(2,1)S(1)} collective-permute-done((bf16[192,1024]{1,0:T(8,128)(2,1)S(1)}, bf16[192,1024]{1,0:T(8,128)(2,1)S(1)}, u32[]{:S(2)}, u32[]{:S(2)}) %collective-permute-start.13) | collective-permute-done | bytes 393248 | tf_op jit(solution)/shard_map/ppermute | solution.py:303
  68.2 0.8 copy-done.9
  69.0 0.8 copy-done.34
  69.8 3.8 %all-to-all-start.1 = ((f32[8,256,256]{2,1,0:T(8,128)}), f32[8,256,256]{2,1,0:T(8,128)S(1)}, u32[]{:S(2)}, u32[]{:S(2)}) async-start(f32[8,256,256]{2,1,0:T(8,128)} %inverse.1), calls=%async_computation.1 | async-start | bytes 4194304 | tf_op jit(solution)/shard_map/all_to_all | solution.py:382
  73.6 1.0 collective-permute-start.16
  74.6 2.2 %collective-permute-start.17 = (bf16[192,1024]{1,0:T(8,128)(2,1)}, bf16[192,1024]{1,0:T(8,128)(2,1)S(1)}, u32[]{:S(2)}, u32[]{:S(2)}) collective-permute-start(bf16[192,1024]{1,0:T(8,128)(2,1)} %copy-done.40), channel_id=1, source_target_pairs={{0,128},{64,192},{128,0},{192,64},{1,129},{65,193},{129,1},{193,65... | collective-permute-start | bytes 1179656 | tf_op jit(solution)/shard_map/ppermute | solution.py:303
  76.8 1.1 collective-permute-start.18
  77.9 1.1 copy-done.35
  79.0 4.3 %pack_2.5 = (f32[32,128]{1,0:T(8,128)S(1)}, bf16[192,1024]{1,0:T(8,128)(2,1)S(1)}, bf16[192,1024]{1,0:T(8,128)(2,1)S(1)}, bf16[192,1024]{1,0:T(8,128)(2,1)}, bf16[192,1024]{1,0:T(8,128)(2,1)}) custom-call(s32[3]{0:T(128)S(1)} %pad_add_fusion.place_ref, f32[32,128]{1,0:T(8,128)S(1)} %get-tuple-element.102.before_ref, ...), custom_call_target="tpu_custom_call" | custom-call | bytes 11070000 | tf_op jit(solution)/shard_map/pack_2/pallas_call | solution.py:144
  83.2 0.7 copy-done.20
  84.0 1.0 collective-permute-start.19
  85.0 1.0 copy-done.7
  86.0 1.0 copy-done.10
  87.0 0.9 copy-done.29
  87.9 0.9 copy-done.32
  89.0 0.8 copy-done.16
  89.8 2.5 %collective-permute-start.20 = (bf16[192,1024]{1,0:T(8,128)(2,1)}, bf16[192,1024]{1,0:T(8,128)(2,1)}, u32[]{:S(2)}, u32[]{:S(2)}) collective-permute-start(bf16[192,1024]{1,0:T(8,128)(2,1)} %get-tuple-element.127), channel_id=1, source_target_pairs={{0,128},{64,192},{128,0},{192,64},{1,129},{65,193},{129,1},{193,65... | collective-permute-start | bytes 1179656 | tf_op jit(solution)/shard_map/ppermute | solution.py:303
  92.3 4.4 %collective-permute-done.18.refs_3_.refs_9_ = bf16[192,1024]{1,0:T(8,128)(2,1)S(1)} collective-permute-done((bf16[192,1024]{1,0:T(8,128)(2,1)}, bf16[192,1024]{1,0:T(8,128)(2,1)S(1)}, u32[]{:S(2)}, u32[]{:S(2)}) %collective-permute-start.18) | collective-permute-done | bytes 393248 | tf_op jit(solution)/shard_map/ppermute | solution.py:303
  96.6 0.7 copy-done.18
  97.4 1.8 %collective-permute-start.21 = (bf16[192,1024]{1,0:T(8,128)(2,1)}, bf16[192,1024]{1,0:T(8,128)(2,1)}, u32[]{:S(2)}, u32[]{:S(2)}) collective-permute-start(bf16[192,1024]{1,0:T(8,128)(2,1)} %get-tuple-element.128), channel_id=1, source_target_pairs={{0,192},{64,0},{128,64},{192,128},{1,193},{65,1},{129,65},{193,129... | collective-permute-start | bytes 1179656 | tf_op jit(solution)/shard_map/ppermute | solution.py:303
  99.2 2.0 %pack_1.3 = (f32[32,128]{1,0:T(8,128)}, bf16[112,1024]{1,0:T(8,128)(2,1)S(1)}, bf16[112,1024]{1,0:T(8,128)(2,1)}, bf16[112,1024]{1,0:T(8,128)(2,1)}, bf16[112,1024]{1,0:T(8,128)(2,1)}) custom-call(s32[3]{0:T(128)S(1)} %pad_add_fusion.place_ref, f32[32,128]{1,0:T(8,128)S(1)} %get-tuple-element.117.before_ref, ...), custom_call_target="tpu_custom_call" | custom-call | bytes 7380000 | tf_op jit(solution)/shard_map/pack_1/pallas_call | solution.py:144
  101.5 3.4 %collective-permute-start.23 = (bf16[112,1024]{1,0:T(8,128)(2,1)}, bf16[112,1024]{1,0:T(8,128)(2,1)S(1)}, u32[]{:S(2)}, u32[]{:S(2)}) collective-permute-start(bf16[112,1024]{1,0:T(8,128)(2,1)} %get-tuple-element.131), channel_id=1, source_target_pairs={{0,128},{64,192},{128,0},{192,64},{1,129},{65,193},{129,1},{193,65... | collective-permute-start | bytes 688136 | tf_op jit(solution)/shard_map/ppermute | solution.py:303
  104.9 0.8 copy-done.22
  105.7 0.6 collective-permute-start.24
  106.4 1.2 copy-done.24
  107.6 1.2 copy-done.25
  108.8 5.3 %errors.1 = f32[8,256,256]{2,1,0:T(8,128)} custom-call(bf16[8,256,256]{2,1,0:T(8,128)(2,1)S(1)} %copy-done.24, s32[8,256,128]{2,1,0:T(8,128)S(1)} %copy-done.25, bf16[8,2,64]{2,1,0:T(2,128)(2,1)S(1)} %copy-done.38, f32[8,256,256]{2,1,0:T(8,128)S(1)} %all-to-all-done.1.inverse_ref), custom_call_target="tpu_custom_call" | custom-call | bytes 18450000 | tf_op jit(solution)/shard_map/errors/pallas_call | solution.py:394
  114.2 3.4 %hessian_2.1.refs_28_ = f32[8,896,256]{2,1,0:T(8,128)S(1)} custom-call(s32[3]{0:T(128)S(1)} %pad_add_fusion.place_ref, bf16[96,1024]{1,0:T(8,128)(2,1)S(1)} %get-tuple-element.105.refs_0_, bf16[192,1024]{1,0:T(8,128)(2,1)S(1)} %copy-done.3, bf16[96,1024]{1,0:T(8,128)(2,1)S(1)} %copy-done.27, bf16[192,1024]{1,0:T(8,128)(2,1)S(1)} %copy-done.5, ...), custom_call_target="tpu_custom_call" | custom-call | bytes 18450000 | tf_op jit(solution)/shard_map/hessian_2/pallas_call | solution.py:290
  117.7 0.9 collective-permute-done.23.refs_10_.refs_8_.refs_26_
  118.6 4.1 %collective-permute-done.24.refs_11_.refs_27_ = bf16[112,1024]{1,0:T(8,128)(2,1)S(1)} collective-permute-done((bf16[112,1024]{1,0:T(8,128)(2,1)}, bf16[112,1024]{1,0:T(8,128)(2,1)S(1)}, u32[]{:S(2)}, u32[]{:S(2)}) %collective-permute-start.24) | collective-permute-done | bytes 229408 | tf_op jit(solution)/shard_map/ppermute | solution.py:303
  122.8 1.2 window_half.3
  124.1 1.8 %collective-permute-done.25.refs_12_.refs_13_.refs_14_.refs_15_.refs_16_.refs_17_.refs_18_.refs_19_.refs_20_.refs_21_.refs_22_.refs_23_ = bf16[1920,128]{1,0:T(8,128)(2,1)S(1)} collective-permute-done((bf16[1920,128]{1,0:T(8,128)(2,1)S(1)}, bf16[1920,128]{1,0:T(8,128)(2,1)S(1)}, u32[]{:S(2)}, u32[]{:S(2)}) %collective-permute-start.25) | collective-permute-done | bytes 491552 | tf_op jit(solution)/shard_map/ppermute | solution.py:303
  126.0 6.5 %hessian_3.1 = f32[8,896,256]{2,1,0:T(8,128)} custom-call(s32[3]{0:T(128)S(1)} %pad_add_fusion.place_ref, bf16[192,1024]{1,0:T(8,128)(2,1)S(1)} %copy-done.13, bf16[192,1024]{1,0:T(8,128)(2,1)S(1)} %copy-done.21, bf16[112,1024]{1,0:T(8,128)(2,1)S(1)} %get-tuple-element.134.refs_8_.refs_2_.refs_24_, bf16[192,1024]{1,0:T(8,128)(2,1)S(1)} %copy-done.15, ...), custom_call_target="tpu_custom_call" | custom-call | bytes 18450000 | tf_op jit(solution)/shard_map/hessian_3/pallas_call | solution.py:290
  (94 shorter events, 1.1 us)
Async XLA Ops:
  0.6 1.0 copy-start
  1.6 5.3 %copy-start.1 = (bf16[256,896]{1,0:T(8,128)(2,1)S(1)}, bf16[256,896]{1,0:T(8,128)(2,1)}, u32[]{:S(2)}) copy-start(bf16[256,896]{1,0:T(8,128)(2,1)} %tokens_ref.3) | copy-start | bytes 1376260
  2.5 14.8 %all-to-all-start = ((bf16[8,256,128]{2,1,0:T(8,128)(2,1)}), bf16[8,256,128]{2,1,0:T(8,128)(2,1)S(1)}, u32[]{:S(2)}, u32[]{:S(2)}) async-start(bf16[8,256,128]{2,1,0:T(8,128)(2,1)} %halves.1), calls=%async_computation | async-start | bytes 1048576 | tf_op jit(solution)/shard_map/all_to_all | solution.py:353
  7.7 17.4 %collective-permute-start.1 = (bf16[272,896]{1,0:T(8,128)(2,1)S(1)}, bf16[272,896]{1,0:T(8,128)(2,1)S(1)}, u32[]{:S(2)}, u32[]{:S(2)}) collective-permute-start(bf16[272,896]{1,0:T(8,128)(2,1)S(1)} %payload.1.refs_0_), channel_id=1, source_target_pairs={{0,56},{8,0},{16,8},{24,16},{32,24},{40,32},{48,40},{56,48},{1,57}... | collective-permute-start | bytes 1462280 | tf_op jit(solution)/shard_map/ppermute | solution.py:303
  13.7 15.2 %collective-permute-start = (bf16[272,896]{1,0:T(8,128)(2,1)S(1)}, bf16[272,896]{1,0:T(8,128)(2,1)S(1)}, u32[]{:S(2)}, u32[]{:S(2)}) collective-permute-start(bf16[272,896]{1,0:T(8,128)(2,1)S(1)} %payload.1.refs_0_), channel_id=1, source_target_pairs={{0,8},{8,16},{16,24},{24,32},{32,40},{40,48},{48,56},{56,0},{1,9},... | collective-permute-start | bytes 1462280 | tf_op jit(solution)/shard_map/ppermute | solution.py:303
  17.3 11.5 %collective-permute-start.3 = (bf16[256,128]{1,0:T(8,128)(2,1)S(1)}, bf16[256,128]{1,0:T(8,128)(2,1)S(1)}, u32[]{:S(2)}, u32[]{:S(2)}) collective-permute-start(bf16[256,128]{1,0:T(8,128)(2,1)S(1)} %slice_bitcast_fusion.refs_1_), channel_id=1, source_target_pairs={{0,56},{8,0},{16,8},{24,16},{32,24},{40,32},{48,40},{56,48},{1,57}... | collective-permute-start | bytes 196616 | tf_op jit(solution)/shard_map/ppermute | solution.py:303
  23.2 6.3 %collective-permute-start.2 = (bf16[256,128]{1,0:T(8,128)(2,1)S(1)}, bf16[256,128]{1,0:T(8,128)(2,1)S(1)}, u32[]{:S(2)}, u32[]{:S(2)}) collective-permute-start(bf16[256,128]{1,0:T(8,128)(2,1)S(1)} %slice_bitcast_fusion.refs_1_), channel_id=1, source_target_pairs={{0,8},{8,16},{16,24},{24,32},{32,40},{40,48},{48,56},{56,0},{1,9},... | collective-permute-start | bytes 196616 | tf_op jit(solution)/shard_map/ppermute | solution.py:303
  23.3 35.8 %copy-start.36 = (f32[1,256,256]{2,1,0:T(8,128)S(1)}, f32[1,256,256]{2,1,0:T(8,128)}, u32[]{:S(2)}) copy-start(f32[1,256,256]{2,1,0:T(8,128)} %factor_ref) | copy-start | bytes 786436
  29.7 15.9 %collective-permute-start.4 = (bf16[272,1024]{1,0:T(8,128)(2,1)S(1)}, bf16[272,1024]{1,0:T(8,128)(2,1)S(1)}, u32[]{:S(2)}, u32[]{:S(2)}) collective-permute-start(bf16[272,1024]{1,0:T(8,128)(2,1)S(1)} %get-tuple-element.83.refs_0_), channel_id=1, source_target_pairs={{0,8},{8,16},{16,24},{24,32},{32,40},{40,48},{48,56},{56,0},{1,9},... | collective-permute-start | bytes 1671176 | tf_op jit(solution)/shard_map/ppermute | solution.py:303
  29.7 15.8 %collective-permute-start.5 = (bf16[272,1024]{1,0:T(8,128)(2,1)S(1)}, bf16[272,1024]{1,0:T(8,128)(2,1)S(1)}, u32[]{:S(2)}, u32[]{:S(2)}) collective-permute-start(bf16[272,1024]{1,0:T(8,128)(2,1)S(1)} %get-tuple-element.84.refs_1_), channel_id=1, source_target_pairs={{0,56},{8,0},{16,8},{24,16},{32,24},{40,32},{48,40},{56,48},{1,57}... | collective-permute-start | bytes 1671176 | tf_op jit(solution)/shard_map/ppermute | solution.py:303
  33.0 7.7 %collective-permute-start.6 = (bf16[96,1024]{1,0:T(8,128)(2,1)S(1)}, bf16[96,1024]{1,0:T(8,128)(2,1)S(1)}, u32[]{:S(2)}, u32[]{:S(2)}) collective-permute-start(bf16[96,1024]{1,0:T(8,128)(2,1)S(1)} %get-tuple-element.88), channel_id=1, source_target_pairs={{0,64},{64,128},{128,192},{192,0},{1,65},{65,129},{129,193},{193,1... | collective-permute-start | bytes 589832 | tf_op jit(solution)/shard_map/ppermute | solution.py:303
  34.5 9.1 %collective-permute-start.7 = (bf16[96,1024]{1,0:T(8,128)(2,1)S(1)}, bf16[96,1024]{1,0:T(8,128)(2,1)S(1)}, u32[]{:S(2)}, u32[]{:S(2)}) collective-permute-start(bf16[96,1024]{1,0:T(8,128)(2,1)S(1)} %get-tuple-element.89), channel_id=1, source_target_pairs={{0,128},{64,192},{128,0},{192,64},{1,129},{65,193},{129,1},{193,65... | collective-permute-start | bytes 589832 | tf_op jit(solution)/shard_map/ppermute | solution.py:303
  35.6 9.3 %collective-permute-start.8 = (bf16[96,1024]{1,0:T(8,128)(2,1)S(1)}, bf16[96,1024]{1,0:T(8,128)(2,1)S(1)}, u32[]{:S(2)}, u32[]{:S(2)}) collective-permute-start(bf16[96,1024]{1,0:T(8,128)(2,1)S(1)} %get-tuple-element.90), channel_id=1, source_target_pairs={{0,192},{64,0},{128,64},{192,128},{1,193},{65,1},{129,65},{193,129... | collective-permute-start | bytes 589832 | tf_op jit(solution)/shard_map/ppermute | solution.py:303
  40.6 44.3 %copy-start.2 = (bf16[192,1024]{1,0:T(8,128)(2,1)}, bf16[192,1024]{1,0:T(8,128)(2,1)S(1)}, u32[]{:S(2)}) copy-start(bf16[192,1024]{1,0:T(8,128)(2,1)S(1)} %get-tuple-element.109.refs_4_.refs_1_) | copy-start | bytes 1179652
  40.7 44.3 %copy-start.26 = (bf16[96,1024]{1,0:T(8,128)(2,1)}, bf16[96,1024]{1,0:T(8,128)(2,1)S(1)}, u32[]{:S(2)}) copy-start(bf16[96,1024]{1,0:T(8,128)(2,1)S(1)} %collective-permute-done.6.refs_1_.refs_2_) | copy-start | bytes 589828
  45.6 23.4 %collective-permute-start.9 = (bf16[272,1024]{1,0:T(8,128)(2,1)S(1)}, bf16[272,1024]{1,0:T(8,128)(2,1)}, u32[]{:S(2)}, u32[]{:S(2)}) collective-permute-start(bf16[272,1024]{1,0:T(8,128)(2,1)S(1)} %collective-permute-done.4.refs_0_), channel_id=1, source_target_pairs={{0,8},{8,16},{16,24},{24,32},{32,40},{40,48},{48,56},{56,0},{1,9},... | collective-permute-start | bytes 1671176 | tf_op jit(solution)/shard_map/ppermute | solution.py:303
  45.6 23.4 %collective-permute-start.10 = (bf16[272,1024]{1,0:T(8,128)(2,1)S(1)}, bf16[272,1024]{1,0:T(8,128)(2,1)S(1)}, u32[]{:S(2)}, u32[]{:S(2)}) collective-permute-start(bf16[272,1024]{1,0:T(8,128)(2,1)S(1)} %collective-permute-done.5.refs_1_), channel_id=1, source_target_pairs={{0,56},{8,0},{16,8},{24,16},{32,24},{40,32},{48,40},{56,48},{1,57}... | collective-permute-start | bytes 1671176 | tf_op jit(solution)/shard_map/ppermute | solution.py:303
  48.8 16.7 %collective-permute-start.11 = (bf16[192,1024]{1,0:T(8,128)(2,1)S(1)}, bf16[192,1024]{1,0:T(8,128)(2,1)S(1)}, u32[]{:S(2)}, u32[]{:S(2)}) collective-permute-start(bf16[192,1024]{1,0:T(8,128)(2,1)S(1)} %get-tuple-element.98), channel_id=1, source_target_pairs={{0,64},{64,128},{128,192},{192,0},{1,65},{65,129},{129,193},{193,1... | collective-permute-start | bytes 1179656 | tf_op jit(solution)/shard_map/ppermute | solution.py:303
  50.1 15.4 %collective-permute-start.12 = (bf16[192,1024]{1,0:T(8,128)(2,1)S(1)}, bf16[192,1024]{1,0:T(8,128)(2,1)S(1)}, u32[]{:S(2)}, u32[]{:S(2)}) collective-permute-start(bf16[192,1024]{1,0:T(8,128)(2,1)S(1)} %get-tuple-element.99), channel_id=1, source_target_pairs={{0,128},{64,192},{128,0},{192,64},{1,129},{65,193},{129,1},{193,65... | collective-permute-start | bytes 1179656 | tf_op jit(solution)/shard_map/ppermute | solution.py:303
  52.3 16.0 %collective-permute-start.13 = (bf16[192,1024]{1,0:T(8,128)(2,1)S(1)}, bf16[192,1024]{1,0:T(8,128)(2,1)S(1)}, u32[]{:S(2)}, u32[]{:S(2)}) collective-permute-start(bf16[192,1024]{1,0:T(8,128)(2,1)S(1)} %get-tuple-element.100), channel_id=1, source_target_pairs={{0,192},{64,0},{128,64},{192,128},{1,193},{65,1},{129,65},{193,129... | collective-permute-start | bytes 1179656 | tf_op jit(solution)/shard_map/ppermute | solution.py:303
  56.1 0.8 copy-start.12
  57.7 0.8 copy-start.40
  58.4 0.8 copy-start.41
  65.5 19.4 %copy-start.4 = (bf16[192,1024]{1,0:T(8,128)(2,1)}, bf16[192,1024]{1,0:T(8,128)(2,1)S(1)}, u32[]{:S(2)}) copy-start(bf16[192,1024]{1,0:T(8,128)(2,1)S(1)} %collective-permute-done.11.refs_5_.refs_3_) | copy-start | bytes 1179652
  65.5 0.8 copy-start.6
  68.2 0.8 copy-start.9
  69.0 0.8 copy-start.34
  69.8 36.6 %all-to-all-start.1 = ((f32[8,256,256]{2,1,0:T(8,128)}), f32[8,256,256]{2,1,0:T(8,128)S(1)}, u32[]{:S(2)}, u32[]{:S(2)}) async-start(f32[8,256,256]{2,1,0:T(8,128)} %inverse.1), calls=%async_computation.1 | async-start | bytes 4194304 | tf_op jit(solution)/shard_map/all_to_all | solution.py:382
  73.6 15.3 %collective-permute-start.16 = (bf16[192,1024]{1,0:T(8,128)(2,1)}, bf16[192,1024]{1,0:T(8,128)(2,1)S(1)}, u32[]{:S(2)}, u32[]{:S(2)}) collective-permute-start(bf16[192,1024]{1,0:T(8,128)(2,1)} %copy-done.41), channel_id=1, source_target_pairs={{0,64},{64,128},{128,192},{192,0},{1,65},{65,129},{129,193},{193,1... | collective-permute-start | bytes 1179656 | tf_op jit(solution)/shard_map/ppermute | solution.py:303
  74.6 24.6 %collective-permute-start.14 = (bf16[272,1024]{1,0:T(8,128)(2,1)}, bf16[272,1024]{1,0:T(8,128)(2,1)S(1)}, u32[]{:S(2)}, u32[]{:S(2)}) collective-permute-start(bf16[272,1024]{1,0:T(8,128)(2,1)} %collective-permute-done.9.refs_0_), channel_id=1, source_target_pairs={{0,8},{8,16},{16,24},{24,32},{32,40},{40,48},{48,56},{56,0},{1,9},... | collective-permute-start | bytes 1671176 | tf_op jit(solution)/shard_map/ppermute | solution.py:303
  74.6 14.4 %collective-permute-start.17 = (bf16[192,1024]{1,0:T(8,128)(2,1)}, bf16[192,1024]{1,0:T(8,128)(2,1)S(1)}, u32[]{:S(2)}, u32[]{:S(2)}) collective-permute-start(bf16[192,1024]{1,0:T(8,128)(2,1)} %copy-done.40), channel_id=1, source_target_pairs={{0,128},{64,192},{128,0},{192,64},{1,129},{65,193},{129,1},{193,65... | collective-permute-start | bytes 1179656 | tf_op jit(solution)/shard_map/ppermute | solution.py:303
  76.8 19.8 %collective-permute-start.18 = (bf16[192,1024]{1,0:T(8,128)(2,1)}, bf16[192,1024]{1,0:T(8,128)(2,1)S(1)}, u32[]{:S(2)}, u32[]{:S(2)}) collective-permute-start(bf16[192,1024]{1,0:T(8,128)(2,1)} %copy-done.39), channel_id=1, source_target_pairs={{0,192},{64,0},{128,64},{192,128},{1,193},{65,1},{129,65},{193,129... | collective-permute-start | bytes 1179656 | tf_op jit(solution)/shard_map/ppermute | solution.py:303
  77.9 1.1 copy-start.35
  78.9 27.4 %copy-start.38 = (bf16[8,2,64]{2,1,0:T(2,128)(2,1)S(1)}, bf16[8,2,64]{2,1,0:T(2,128)(2,1)}, u32[]{:S(2)}) copy-start(bf16[8,2,64]{2,1,0:T(2,128)(2,1)} %codebook_ref.1) | copy-start | bytes 6148
  84.0 20.9 %collective-permute-start.19 = (bf16[192,1024]{1,0:T(8,128)(2,1)S(1)}, bf16[192,1024]{1,0:T(8,128)(2,1)S(1)}, u32[]{:S(2)}, u32[]{:S(2)}) collective-permute-start(bf16[192,1024]{1,0:T(8,128)(2,1)S(1)} %get-tuple-element.126), channel_id=1, source_target_pairs={{0,64},{64,128},{128,192},{192,0},{1,65},{65,129},{129,193},{193,1... | collective-permute-start | bytes 1179656 | tf_op jit(solution)/shard_map/ppermute | solution.py:303
  85.0 1.0 copy-start.7
  86.0 1.0 copy-start.10
  87.0 0.9 copy-start.29
  87.9 0.9 copy-start.32
  88.9 17.4 %copy-start.14 = (bf16[192,1024]{1,0:T(8,128)(2,1)}, bf16[192,1024]{1,0:T(8,128)(2,1)S(1)}, u32[]{:S(2)}) copy-start(bf16[192,1024]{1,0:T(8,128)(2,1)S(1)} %collective-permute-done.16.refs_1_.refs_3_) | copy-start | bytes 1179652
  88.9 10.3 %collective-permute-start.15 = (bf16[1152,128]{1,0:T(8,128)(2,1)S(1)}, bf16[1152,128]{1,0:T(8,128)(2,1)S(1)}, u32[]{:S(2)}, u32[]{:S(2)}) collective-permute-start(bf16[1152,128]{1,0:T(8,128)(2,1)S(1)} %window_half.2), channel_id=1, source_target_pairs={{0,1},{1,0},{2,3},{3,2},{4,5},{5,4},{6,7},{7,6},{8,9},{9,8},{10,11... | collective-permute-start | bytes 884744 | tf_op jit(solution)/shard_map/ppermute | solution.py:303
  89.0 0.8 copy-start.16
  89.8 27.8 %collective-permute-start.20 = (bf16[192,1024]{1,0:T(8,128)(2,1)}, bf16[192,1024]{1,0:T(8,128)(2,1)}, u32[]{:S(2)}, u32[]{:S(2)}) collective-permute-start(bf16[192,1024]{1,0:T(8,128)(2,1)} %get-tuple-element.127), channel_id=1, source_target_pairs={{0,128},{64,192},{128,0},{192,64},{1,129},{65,193},{129,1},{193,65... | collective-permute-start | bytes 1179656 | tf_op jit(solution)/shard_map/ppermute | solution.py:303
  97.4 20.3 %collective-permute-start.21 = (bf16[192,1024]{1,0:T(8,128)(2,1)}, bf16[192,1024]{1,0:T(8,128)(2,1)}, u32[]{:S(2)}, u32[]{:S(2)}) collective-permute-start(bf16[192,1024]{1,0:T(8,128)(2,1)} %get-tuple-element.128), channel_id=1, source_target_pairs={{0,192},{64,0},{128,64},{192,128},{1,193},{65,1},{129,65},{193,129... | collective-permute-start | bytes 1179656 | tf_op jit(solution)/shard_map/ppermute | solution.py:303
  101.2 16.4 %collective-permute-start.22 = (bf16[112,1024]{1,0:T(8,128)(2,1)}, bf16[112,1024]{1,0:T(8,128)(2,1)S(1)}, u32[]{:S(2)}, u32[]{:S(2)}) collective-permute-start(bf16[112,1024]{1,0:T(8,128)(2,1)} %get-tuple-element.130), channel_id=1, source_target_pairs={{0,64},{64,128},{128,192},{192,0},{1,65},{65,129},{129,193},{193,1... | collective-permute-start | bytes 688136 | tf_op jit(solution)/shard_map/ppermute | solution.py:303
  101.5 17.1 %collective-permute-start.23 = (bf16[112,1024]{1,0:T(8,128)(2,1)}, bf16[112,1024]{1,0:T(8,128)(2,1)S(1)}, u32[]{:S(2)}, u32[]{:S(2)}) collective-permute-start(bf16[112,1024]{1,0:T(8,128)(2,1)} %get-tuple-element.131), channel_id=1, source_target_pairs={{0,128},{64,192},{128,0},{192,64},{1,129},{65,193},{129,1},{193,65... | collective-permute-start | bytes 688136 | tf_op jit(solution)/shard_map/ppermute | solution.py:303
  104.9 0.8 copy-start.22
  105.7 17.0 %collective-permute-start.24 = (bf16[112,1024]{1,0:T(8,128)(2,1)}, bf16[112,1024]{1,0:T(8,128)(2,1)S(1)}, u32[]{:S(2)}, u32[]{:S(2)}) collective-permute-start(bf16[112,1024]{1,0:T(8,128)(2,1)} %get-tuple-element.132), channel_id=1, source_target_pairs={{0,192},{64,0},{128,64},{192,128},{1,193},{65,1},{129,65},{193,129... | collective-permute-start | bytes 688136 | tf_op jit(solution)/shard_map/ppermute | solution.py:303
  106.3 1.2 copy-start.24
  107.6 1.2 copy-start.25
  108.8 5.3 %copy-start.3 = (bf16[192,1024]{1,0:T(8,128)(2,1)S(1)}, bf16[192,1024]{1,0:T(8,128)(2,1)}, u32[]{:S(2)}) copy-start(bf16[192,1024]{1,0:T(8,128)(2,1)} %copy-done.2) | copy-start | bytes 1179652
  108.8 5.3 %copy-start.5 = (bf16[192,1024]{1,0:T(8,128)(2,1)S(1)}, bf16[192,1024]{1,0:T(8,128)(2,1)}, u32[]{:S(2)}) copy-start(bf16[192,1024]{1,0:T(8,128)(2,1)} %copy-done.4) | copy-start | bytes 1179652
  108.8 5.3 %copy-start.8 = (bf16[192,1024]{1,0:T(8,128)(2,1)S(1)}, bf16[192,1024]{1,0:T(8,128)(2,1)}, u32[]{:S(2)}) copy-start(bf16[192,1024]{1,0:T(8,128)(2,1)} %copy-done.6) | copy-start | bytes 1179652
  108.8 5.3 %copy-start.11 = (bf16[192,1024]{1,0:T(8,128)(2,1)S(1)}, bf16[192,1024]{1,0:T(8,128)(2,1)}, u32[]{:S(2)}) copy-start(bf16[192,1024]{1,0:T(8,128)(2,1)} %copy-done.9) | copy-start | bytes 1179652
  108.8 5.3 %copy-start.27 = (bf16[96,1024]{1,0:T(8,128)(2,1)S(1)}, bf16[96,1024]{1,0:T(8,128)(2,1)}, u32[]{:S(2)}) copy-start(bf16[96,1024]{1,0:T(8,128)(2,1)} %copy-done.26) | copy-start | bytes 589828
  108.8 5.3 %copy-start.30 = (bf16[96,1024]{1,0:T(8,128)(2,1)S(1)}, bf16[96,1024]{1,0:T(8,128)(2,1)}, u32[]{:S(2)}) copy-start(bf16[96,1024]{1,0:T(8,128)(2,1)} %copy-done.28) | copy-start | bytes 589828
  108.8 5.3 %copy-start.33 = (bf16[96,1024]{1,0:T(8,128)(2,1)S(1)}, bf16[96,1024]{1,0:T(8,128)(2,1)}, u32[]{:S(2)}) copy-start(bf16[96,1024]{1,0:T(8,128)(2,1)} %copy-done.31) | copy-start | bytes 589828
  114.1 8.6 %copy-start.13 = (bf16[192,1024]{1,0:T(8,128)(2,1)S(1)}, bf16[192,1024]{1,0:T(8,128)(2,1)}, u32[]{:S(2)}) copy-start(bf16[192,1024]{1,0:T(8,128)(2,1)} %copy-done.12) | copy-start | bytes 1179652
  114.2 8.6 %copy-start.15 = (bf16[192,1024]{1,0:T(8,128)(2,1)S(1)}, bf16[192,1024]{1,0:T(8,128)(2,1)}, u32[]{:S(2)}) copy-start(bf16[192,1024]{1,0:T(8,128)(2,1)} %copy-done.14) | copy-start | bytes 1179652
  114.2 8.6 %copy-start.17 = (bf16[192,1024]{1,0:T(8,128)(2,1)S(1)}, bf16[192,1024]{1,0:T(8,128)(2,1)}, u32[]{:S(2)}) copy-start(bf16[192,1024]{1,0:T(8,128)(2,1)} %copy-done.16) | copy-start | bytes 1179652
  114.2 8.5 %copy-start.19 = (bf16[192,1024]{1,0:T(8,128)(2,1)S(1)}, bf16[192,1024]{1,0:T(8,128)(2,1)}, u32[]{:S(2)}) copy-start(bf16[192,1024]{1,0:T(8,128)(2,1)} %copy-done.18) | copy-start | bytes 1179652
  114.2 8.5 %copy-start.21 = (bf16[192,1024]{1,0:T(8,128)(2,1)S(1)}, bf16[192,1024]{1,0:T(8,128)(2,1)}, u32[]{:S(2)}) copy-start(bf16[192,1024]{1,0:T(8,128)(2,1)} %copy-done.20) | copy-start | bytes 1179652
  114.2 8.5 %copy-start.23 = (bf16[192,1024]{1,0:T(8,128)(2,1)S(1)}, bf16[192,1024]{1,0:T(8,128)(2,1)}, u32[]{:S(2)}) copy-start(bf16[192,1024]{1,0:T(8,128)(2,1)} %copy-done.22) | copy-start | bytes 1179652
  124.0 2.0 %collective-permute-start.25 = (bf16[1920,128]{1,0:T(8,128)(2,1)S(1)}, bf16[1920,128]{1,0:T(8,128)(2,1)S(1)}, u32[]{:S(2)}, u32[]{:S(2)}) collective-permute-start(bf16[1920,128]{1,0:T(8,128)(2,1)S(1)} %window_half.3), channel_id=1, source_target_pairs={{0,1},{1,0},{2,3},{3,2},{4,5},{5,4},{6,7},{7,6},{8,9},{9,8},{10,11... | collective-permute-start | bytes 1474568 | tf_op jit(solution)/shard_map/ppermute | solution.py:303
  (6 other events, 4.3 us)
